TPU v7x, 32 devices: a whole 2x2x4 slice. The times are simulated.
32 devices in a mesh: dp: 4 (over y, x), expert: 4 (over z), tensor: 2 (over core).
Axes of the slice: x: 2, y: 2, z: 4, core: 2. Of those that a mesh axis runs over, the one named last changes fastest.
Arguments:
- layer_in: bfloat16 [2048, 2048], P(('dp', 'expert')), may hold values from -6 to 6
- norm_gain: bfloat16 [2048], replicated, may hold values from 0.099609375 to 1.8984375
- query_proj: bfloat16 [2048, 3072], P('dp', 'tensor'), may hold values from -0.125 to 0.125
- latent_proj: bfloat16 [2048, 576], P('dp'), may hold values from -0.125 to 0.125
- latent_gain: bfloat16 [512], replicated, may hold values from 0.099609375 to 1.8984375
- latent_up: bfloat16 [512, 4096], P('dp', 'tensor'), may hold values from -0.25 to 0.25
- output_proj: bfloat16 [2048, 2048], P('tensor', 'dp'), may hold values from -0.75 to 0.75
- ffn_gain: bfloat16 [2048], replicated, may hold values from 0.099609375 to 1.8984375
- router: bfloat16 [2048, 16], replicated, may hold values from -0.0625 to 0.0625
- shared_gate: bfloat16 [2048, 2816], P('dp', 'tensor'), may hold values from -0.125 to 0.125
- shared_up: bfloat16 [2048, 2816], P('dp', 'tensor'), may hold values from -0.125 to 0.125
- shared_down: bfloat16 [2816, 2048], P('tensor', 'dp'), may hold values from -0.109375 to 0.109375
- expert_gate: bfloat16 [16, 2048, 1408], P('expert', None, 'tensor'), may hold values from -0.125 to 0.125
- expert_up: bfloat16 [16, 2048, 1408], P('expert', None, 'tensor'), may hold values from -0.125 to 0.125
- expert_down: bfloat16 [16, 1408, 2048], P('expert', 'tensor'), may hold values from -0.625 to 0.625
- routes: int32 [2048, 6], P(('dp', 'expert')), may hold values from 0 to 15, as said below
- leaf_parent: int32 [8], replicated, may hold values from 0 to 3, as said below
- grad_out: bfloat16 [2048, 2048], P(('dp', 'expert')), may hold values from -6 to 6
Outputs:
- layer_out: bfloat16 [2048, 2048], P(('dp', 'expert'))
- grad_in: float32 [2048, 2048], P(('dp', 'expert'))
- grad_norm_gain: float32 [2048], P(('dp', 'expert'))
- grad_query_proj: float32 [2048, 3072], P(('dp', 'expert'), 'tensor')
- grad_latent_proj: float32 [2048, 576], P(('dp', 'expert'))
- grad_latent_gain: float32 [512], P(('dp', 'expert'))
- grad_latent_up: float32 [512, 4096], P(('dp', 'expert'), 'tensor')
- grad_output_proj: float32 [2048, 2048], P('tensor', ('dp', 'expert'))
- grad_ffn_gain: float32 [2048], P(('dp', 'expert'))
- grad_router: float32 [2048, 16], P(('dp', 'expert'))
- grad_shared_gate: float32 [2048, 2816], P(('dp', 'expert'), 'tensor')
- grad_shared_up: float32 [2048, 2816], P(('dp', 'expert'), 'tensor')
- grad_shared_down: float32 [2816, 2048], P('tensor', ('dp', 'expert'))
- grad_expert_gate: float32 [16, 2048, 1408], P('expert', 'dp', 'tensor')
- grad_expert_up: float32 [16, 2048, 1408], P('expert', 'dp', 'tensor')
- grad_expert_down: float32 [16, 1408, 2048], P('expert', 'tensor', 'dp')
Inputs may be any that keep to these rules, and one draw needn't show every extreme that they name: `routes`: A row names 6 different experts. In the rows of each index of dp and expert one expert, the same one for all of them in a draw, is named exactly 96 times, and no other expert more than 96 times. `leaf_parent`: each branch is the parent of exactly 2 leaves.
All inputs are finite; a program needn't handle non-finite values.
Results may differ from a plain program's by a relative error of at most 0.02.
Values may be sent and summed in bfloat16 or wider, within the bound.
No kernel may reach another device: no remote copies, remote signals or barrier semaphores. Data moves between devices by JAX's collectives and lax.ppermute only.
A program may use at most 384 MiB of HBM per device.

v0:
```python
import jax
import jax.numpy as jnp
from jax import lax
from jax.sharding import PartitionSpec as P

D = 2048
DN = 128
DR = 64
DV = 128
R = 512
EXPERTS = 16
TOP = 6
NB = 4
NL = 2


HIGHEST = lax.Precision.HIGHEST
epsilon = 1e-06
masked_score = -1e30


def rms_stats(values):
    return lax.rsqrt(jnp.mean(values * values, axis=-1, keepdims=True) + epsilon)


def rms_back(grad_normed, unit_rows, inverse):
    return inverse * (
        grad_normed - unit_rows * jnp.mean(grad_normed * unit_rows, axis=-1, keepdims=True)
    )


def silu_parts(pre_values):
    sigmoid_value = jax.nn.sigmoid(pre_values)
    return (pre_values * sigmoid_value, sigmoid_value * (1.0 + pre_values * (1.0 - sigmoid_value)))


def rotary_tables(positions, width):
    half_width = width // 2
    freqs = 10000.0 ** (-2.0 * jnp.arange(half_width, dtype=jnp.float32) / width)
    angles = positions.astype(jnp.float32)[:, None] * freqs[None, :]
    return (jnp.cos(angles), jnp.sin(angles))


def rotate(values, cosine, sine):
    half_width = values.shape[-1] // 2
    first_half = values[..., :half_width]
    second_half = values[..., half_width:]
    return jnp.concatenate(
        [first_half * cosine - second_half * sine, second_half * cosine + first_half * sine],
        axis=-1,
    )


def rotate_back(grads_in, cosine, sine):
    half_width = grads_in.shape[-1] // 2
    first_half = grads_in[..., :half_width]
    second_half = grads_in[..., half_width:]
    return jnp.concatenate(
        [first_half * cosine + second_half * sine, second_half * cosine - first_half * sine],
        axis=-1,
    )


def tree_layout(leaf_parent, tree_len, trunk_len, seg_len):
    token_index = jnp.arange(tree_len, dtype=jnp.int32)
    beyond = token_index - trunk_len
    in_trunk = token_index < trunk_len
    in_branch = (beyond >= 0) & (beyond < NB * seg_len)
    in_leaf = beyond >= NB * seg_len
    leaf_offset = beyond - NB * seg_len
    leaf_index = jnp.clip(leaf_offset // seg_len, 0, NB * NL - 1)
    position = jnp.where(
        in_trunk,
        token_index,
        jnp.where(
            in_branch, trunk_len + beyond % seg_len, trunk_len + seg_len + leaf_offset % seg_len
        ),
    )
    segment = jnp.where(
        in_trunk, 0, jnp.where(in_branch, 1 + beyond // seg_len, 1 + NB + leaf_index)
    )
    leaf_match = (leaf_index[:, None] == jnp.arange(NB * NL, dtype=jnp.int32)[None, :]).astype(
        jnp.int32
    )
    branch_of_leaf = 1 + jnp.sum(leaf_match * leaf_parent[None, :], axis=1)
    parent = jnp.where(in_trunk, -1, jnp.where(in_branch, 0, branch_of_leaf))
    grand = jnp.where(in_leaf, 0, -1)
    return (position, segment, parent, grand.astype(jnp.int32))


def visible(query_segment, query_parent, query_grand, query_index, key_segment, key_index):
    same_segment = (query_segment[:, None] == key_segment[None, :]) & (
        key_index[None, :] <= query_index[:, None]
    )
    ancestor = (key_segment[None, :] == query_parent[:, None]) | (
        key_segment[None, :] == query_grand[:, None]
    )
    return same_segment | ancestor


def attention_probs(queries, keys, allowed, score_scale, log_total):
    raw_scores = jnp.einsum("thr,kr->htk", queries, keys, preferred_element_type=jnp.float32)
    scores = jnp.where(allowed[None], raw_scores * score_scale, masked_score)
    return jnp.exp(scores - log_total)


def per_device(
    layer_in,
    norm_gain,
    query_proj,
    latent_proj,
    latent_gain,
    latent_up,
    output_proj,
    ffn_gain,
    router,
    shared_gate,
    shared_up,
    shared_down,
    expert_gate,
    expert_up,
    expert_down,
    routes,
    leaf_parent,
    grad_out,
):
    tok_rows = layer_in.shape[0]
    group_size = lax.axis_size("expert")
    tree_len = tok_rows * group_size
    seg_len = tree_len // 16
    trunk_len = 4 * seg_len
    local_experts = expert_gate.shape[0]
    capacity = 2 * tok_rows * TOP // EXPERTS
    heads_local = output_proj.shape[0] // DV
    score_scale = (DN + DR) ** (-0.5)
    offset = lax.axis_index("expert") * tok_rows
    fetched = (
        lax.all_gather(query_proj, "dp", axis=0, tiled=True),
        lax.all_gather(latent_proj, "dp", axis=0, tiled=True),
        lax.all_gather(latent_up, "dp", axis=0, tiled=True),
        lax.all_gather(output_proj, "dp", axis=1, tiled=True),
        lax.all_gather(shared_gate, "dp", axis=0, tiled=True),
        lax.all_gather(shared_up, "dp", axis=0, tiled=True),
        lax.all_gather(shared_down, "dp", axis=1, tiled=True),
    )
    (
        query_weight,
        latent_weight,
        latent_up_weight,
        output_weight,
        shared_gate_weight,
        shared_up_weight,
        shared_down_weight,
    ) = fetched
    position, segment, parent, grand = tree_layout(leaf_parent, tree_len, trunk_len, seg_len)
    cosine, sine = rotary_tables(position, DR)
    token_index = jnp.arange(tree_len, dtype=jnp.int32)
    own_cos = lax.dynamic_slice_in_dim(cosine, offset, tok_rows, 0)
    own_sin = lax.dynamic_slice_in_dim(sine, offset, tok_rows, 0)
    allowed = visible(
        lax.dynamic_slice_in_dim(segment, offset, tok_rows, 0),
        lax.dynamic_slice_in_dim(parent, offset, tok_rows, 0),
        lax.dynamic_slice_in_dim(grand, offset, tok_rows, 0),
        lax.dynamic_slice_in_dim(token_index, offset, tok_rows, 0),
        segment,
        token_index,
    )
    input_rows = layer_in.astype(jnp.float32)
    inverse_one = rms_stats(input_rows)
    unit_one = input_rows * inverse_one
    first_norm_scale = norm_gain.astype(jnp.float32)
    normed = (unit_one * first_norm_scale).astype(jnp.bfloat16)
    query_all = jnp.dot(normed, query_weight, preferred_element_type=jnp.float32).reshape(
        tok_rows, heads_local, DN + DR
    )
    query_nope = query_all[:, :, :DN].astype(jnp.bfloat16)
    query_rope = rotate(query_all[:, :, DN:], own_cos[:, None, :], own_sin[:, None, :]).astype(
        jnp.bfloat16
    )
    latent_all = jnp.dot(normed, latent_weight, preferred_element_type=jnp.float32)
    inverse_latent = rms_stats(latent_all[:, :R])
    unit_latent = latent_all[:, :R] * inverse_latent
    latent_norm_scale = latent_gain.astype(jnp.float32)
    latent = (unit_latent * latent_norm_scale).astype(jnp.bfloat16)
    key_rope = rotate(latent_all[:, R:], own_cos, own_sin).astype(jnp.bfloat16)
    tree_latent, tree_rope = (
        lax.all_gather(latent, "expert", axis=0, tiled=True),
        lax.all_gather(key_rope, "expert", axis=0, tiled=True),
    )
    keys = jnp.concatenate([tree_latent, tree_rope], axis=1)
    up_heads = latent_up_weight.reshape(R, heads_local, DN + DV)
    up_key = up_heads[:, :, :DN]
    up_value = up_heads[:, :, DN:]
    query_latent = jnp.einsum(
        "thd,rhd->thr", query_nope, up_key, preferred_element_type=jnp.float32
    ).astype(jnp.bfloat16)
    queries = jnp.concatenate([query_latent, query_rope], axis=2)
    raw_scores = jnp.einsum("thr,kr->htk", queries, keys, preferred_element_type=jnp.float32)
    scores = jnp.where(allowed[None], raw_scores * score_scale, masked_score)
    row_top = jnp.max(scores, axis=-1, keepdims=True)
    exp_scores = jnp.exp(scores - row_top)
    row_total = jnp.sum(exp_scores, axis=-1, keepdims=True)
    log_total = row_top + jnp.log(row_total)
    forward_probs = (exp_scores / row_total).astype(jnp.bfloat16)
    mixed_latent = jnp.einsum(
        "htk,kr->thr", forward_probs, tree_latent, preferred_element_type=jnp.float32
    ).astype(jnp.bfloat16)
    heads_out = (
        jnp.einsum("thr,rhd->thd", mixed_latent, up_value, preferred_element_type=jnp.float32)
        .astype(jnp.bfloat16)
        .reshape(tok_rows, heads_local * DV)
    )
    attention = lax.psum(
        jnp.dot(heads_out, output_weight, preferred_element_type=jnp.float32), "tensor"
    )
    residual = input_rows + attention
    inverse_two = rms_stats(residual)
    unit_two = residual * inverse_two
    second_norm_scale = ffn_gain.astype(jnp.float32)
    normed_two = (unit_two * second_norm_scale).astype(jnp.bfloat16)
    router_probs = jax.nn.softmax(
        jnp.dot(normed_two, router, preferred_element_type=jnp.float32), axis=-1
    )
    choose = (routes[:, :, None] == jnp.arange(EXPERTS, dtype=jnp.int32)[None, None, :]).astype(
        jnp.float32
    )
    gates = jnp.sum(choose * router_probs[:, None, :], axis=2)
    shared_gate_pre = jnp.dot(normed_two, shared_gate_weight, preferred_element_type=jnp.float32)
    shared_up_pre = jnp.dot(normed_two, shared_up_weight, preferred_element_type=jnp.float32)
    shared_silu, shared_slope = silu_parts(shared_gate_pre)
    shared_hidden = (shared_silu * shared_up_pre).astype(jnp.bfloat16)
    shared_part = jnp.dot(shared_hidden, shared_down_weight, preferred_element_type=jnp.float32)
    flat_routes = routes.reshape(-1)
    hits = (flat_routes[:, None] == jnp.arange(EXPERTS, dtype=jnp.int32)[None, :]).astype(jnp.int32)
    earlier = jnp.cumsum(hits, axis=0) - hits
    slot = jnp.sum(earlier * hits, axis=1)
    target = flat_routes * capacity + slot
    source_row = jnp.arange(tok_rows * TOP, dtype=jnp.int32) // TOP
    slot_row = jnp.full((EXPERTS * capacity,), tok_rows, jnp.int32).at[target].set(source_row)
    padded_rows = jnp.concatenate([normed_two, jnp.zeros((1, D), jnp.bfloat16)], axis=0)
    outgoing = jnp.take(padded_rows, slot_row, axis=0).reshape(EXPERTS, capacity, D)
    arrived = lax.all_to_all(outgoing, "expert", split_axis=0, concat_axis=0, tiled=True)
    count = arrived.shape[1]
    grouped = arrived.reshape(group_size, local_experts, count, D)
    gate_pre = jnp.einsum(
        "secd,edf->secf", grouped, expert_gate, preferred_element_type=jnp.float32
    )
    up_pre = jnp.einsum("secd,edf->secf", grouped, expert_up, preferred_element_type=jnp.float32)
    hidden = (jax.nn.silu(gate_pre) * up_pre).astype(jnp.bfloat16)
    produced = jnp.einsum(
        "secf,efd->secd", hidden, expert_down, preferred_element_type=jnp.float32
    ).astype(jnp.bfloat16)
    returned = lax.all_to_all(
        produced.reshape(group_size * local_experts, count, D),
        "expert",
        split_axis=0,
        concat_axis=0,
        tiled=True,
    )
    returned, arrived_rows = (returned, arrived)
    route_values = (
        jnp.take(returned.reshape(EXPERTS * capacity, D), target, axis=0)
        .reshape(tok_rows, TOP, D)
        .astype(jnp.float32)
    )
    routed_part = jnp.sum(gates[:, :, None] * route_values, axis=1)
    ffn_total = lax.psum((shared_part + routed_part).astype(jnp.bfloat16), "tensor").astype(
        jnp.float32
    )
    layer_out = (residual + ffn_total).astype(jnp.bfloat16)
    grad_rows_out = grad_out.astype(jnp.float32)
    slot_grads = (
        (gates[:, :, None] * grad_rows_out[:, None, :])
        .astype(jnp.bfloat16)
        .reshape(tok_rows * TOP, D)
    )
    grad_outgoing = (
        jnp.zeros((EXPERTS * capacity, D), jnp.bfloat16)
        .at[target]
        .set(slot_grads)
        .reshape(EXPERTS, capacity, D)
    )
    grad_arrived = lax.all_to_all(grad_outgoing, "expert", split_axis=0, concat_axis=0, tiled=True)
    grouped = arrived_rows.reshape(group_size, local_experts, capacity, D)
    grad_grouped = grad_arrived.reshape(group_size, local_experts, capacity, D)
    gate_pre = jnp.einsum(
        "secd,edf->secf", grouped, expert_gate, preferred_element_type=jnp.float32
    )
    up_pre = jnp.einsum("secd,edf->secf", grouped, expert_up, preferred_element_type=jnp.float32)
    expert_silu, expert_slope = silu_parts(gate_pre)
    hidden = (expert_silu * up_pre).astype(jnp.bfloat16)
    grad_expert_down = jnp.einsum(
        "secf,secd->efd", hidden, grad_grouped, preferred_element_type=jnp.float32
    )
    grad_hidden = jnp.einsum(
        "secd,efd->secf", grad_grouped, expert_down, preferred_element_type=jnp.float32
    )
    grad_gate_pre = (grad_hidden * up_pre * expert_slope).astype(jnp.bfloat16)
    grad_up_pre = (grad_hidden * expert_silu).astype(jnp.bfloat16)
    grad_expert_gate = jnp.einsum(
        "secd,secf->edf", grouped, grad_gate_pre, preferred_element_type=jnp.float32
    )
    grad_expert_up = jnp.einsum(
        "secd,secf->edf", grouped, grad_up_pre, preferred_element_type=jnp.float32
    )
    grad_sent = jnp.einsum(
        "secf,edf->secd", grad_gate_pre, expert_gate, preferred_element_type=jnp.float32
    ) + jnp.einsum("secf,edf->secd", grad_up_pre, expert_up, preferred_element_type=jnp.float32)
    grad_returned = lax.all_to_all(
        grad_sent.astype(jnp.bfloat16).reshape(group_size * local_experts, capacity, D),
        "expert",
        split_axis=0,
        concat_axis=0,
        tiled=True,
    )
    route_grads = (
        jnp.take(grad_returned.reshape(EXPERTS * capacity, D), target, axis=0)
        .reshape(tok_rows, TOP, D)
        .astype(jnp.float32)
    )
    grad_shared_hidden = jnp.dot(grad_out, shared_down_weight.T, preferred_element_type=jnp.float32)
    grad_sgate_pre = (grad_shared_hidden * shared_up_pre * shared_slope).astype(jnp.bfloat16)
    grad_sup_pre = (grad_shared_hidden * shared_silu).astype(jnp.bfloat16)
    grad_shared_down = jnp.dot(shared_hidden.T, grad_out, preferred_element_type=jnp.float32)
    grad_shared_gate = jnp.dot(normed_two.T, grad_sgate_pre, preferred_element_type=jnp.float32)
    grad_shared_up = jnp.dot(normed_two.T, grad_sup_pre, preferred_element_type=jnp.float32)
    grad_normed_part = (
        jnp.sum(route_grads, axis=1)
        + jnp.dot(grad_sgate_pre, shared_gate_weight.T, preferred_element_type=jnp.float32)
        + jnp.dot(grad_sup_pre, shared_up_weight.T, preferred_element_type=jnp.float32)
    )
    gate_grad_part = jnp.sum(grad_rows_out[:, None, :] * route_values, axis=2)
    grad_normed_two, gate_grad = lax.psum((grad_normed_part, gate_grad_part), "tensor")
    prob_grad = jnp.sum(choose * gate_grad[:, :, None], axis=1)
    logit_grad = router_probs * (
        prob_grad - jnp.sum(router_probs * prob_grad, axis=-1, keepdims=True)
    )
    grad_router = jnp.dot(
        normed_two.astype(jnp.float32).T,
        logit_grad,
        precision=HIGHEST,
        preferred_element_type=jnp.float32,
    )
    grad_normed_two = grad_normed_two + jnp.dot(
        logit_grad,
        router.astype(jnp.float32).T,
        precision=HIGHEST,
        preferred_element_type=jnp.float32,
    )
    grad_ffn_gain = jnp.sum(grad_normed_two * unit_two, axis=0)
    grad_residual = grad_rows_out + rms_back(
        grad_normed_two * second_norm_scale, unit_two, inverse_two
    )
    residual_low = grad_residual.astype(jnp.bfloat16)
    grad_output_proj = jnp.dot(heads_out.T, residual_low, preferred_element_type=jnp.float32)
    grad_heads = (
        jnp.dot(residual_low, output_weight.T, preferred_element_type=jnp.float32)
        .astype(jnp.bfloat16)
        .reshape(tok_rows, heads_local, DV)
    )
    grad_value_up = jnp.einsum(
        "thr,thd->rhd", mixed_latent, grad_heads, preferred_element_type=jnp.float32
    )
    grad_mixed = jnp.einsum(
        "thd,rhd->thr", grad_heads, up_value, preferred_element_type=jnp.float32
    ).astype(jnp.bfloat16)
    probs_again = attention_probs(queries, keys, allowed, score_scale, log_total)
    grad_att = jnp.einsum(
        "thr,kr->htk", grad_mixed, tree_latent, preferred_element_type=jnp.float32
    )
    delta = jnp.sum(probs_again * grad_att, axis=-1, keepdims=True)
    score_grad = jnp.where(
        allowed[None], probs_again * (grad_att - delta) * score_scale, 0.0
    ).astype(jnp.bfloat16)
    grad_queries = jnp.einsum("htk,kr->thr", score_grad, keys, preferred_element_type=jnp.float32)
    grad_keys = jnp.einsum("htk,thr->kr", score_grad, queries, preferred_element_type=jnp.float32)
    grad_latent_keys = grad_keys[:, :R] + jnp.einsum(
        "htk,thr->kr",
        probs_again.astype(jnp.bfloat16),
        grad_mixed,
        preferred_element_type=jnp.float32,
    )
    grad_key_rope = grad_keys[:, R:]
    grad_query_latent = grad_queries[:, :, :R].astype(jnp.bfloat16)
    grad_query_nope = jnp.einsum(
        "thr,rhd->thd", grad_query_latent, up_key, preferred_element_type=jnp.float32
    )
    grad_key_up = jnp.einsum(
        "thr,thd->rhd", grad_query_latent, query_nope, preferred_element_type=jnp.float32
    )
    grad_query_rope = rotate_back(grad_queries[:, :, R:], own_cos[:, None, :], own_sin[:, None, :])
    grad_query_all = (
        jnp.concatenate([grad_query_nope, grad_query_rope], axis=2)
        .astype(jnp.bfloat16)
        .reshape(tok_rows, heads_local * (DN + DR))
    )
    grad_query_proj = jnp.dot(normed.T, grad_query_all, preferred_element_type=jnp.float32)
    grad_normed_query = jnp.dot(grad_query_all, query_weight.T, preferred_element_type=jnp.float32)
    grad_latent_up = jnp.concatenate([grad_key_up, grad_value_up], axis=2).reshape(
        R, heads_local * (DN + DV)
    )
    own_latent_grad, own_rope_grad = (
        lax.psum_scatter(
            grad_latent_keys.astype(jnp.bfloat16), "expert", scatter_dimension=0, tiled=True
        ).astype(jnp.float32),
        lax.psum_scatter(
            grad_key_rope.astype(jnp.bfloat16), "expert", scatter_dimension=0, tiled=True
        ).astype(jnp.float32),
    )
    grad_normed_query, own_latent_grad, own_rope_grad = (
        lax.psum(grad_normed_query.astype(jnp.bfloat16), "tensor").astype(jnp.float32),
        lax.psum(own_latent_grad.astype(jnp.bfloat16), "tensor").astype(jnp.float32),
        lax.psum(own_rope_grad.astype(jnp.bfloat16), "tensor").astype(jnp.float32),
    )
    grad_latent_gain = jnp.sum(own_latent_grad * unit_latent, axis=0)
    grad_latent_raw = rms_back(own_latent_grad * latent_norm_scale, unit_latent, inverse_latent)
    grad_rope_raw = rotate_back(own_rope_grad, own_cos, own_sin)
    grad_latent_all = jnp.concatenate([grad_latent_raw, grad_rope_raw], axis=1).astype(jnp.bfloat16)
    grad_latent_proj = jnp.dot(normed.T, grad_latent_all, preferred_element_type=jnp.float32)
    grad_normed_total = grad_normed_query + jnp.dot(
        grad_latent_all, latent_weight.T, preferred_element_type=jnp.float32
    )
    grad_norm_gain = jnp.sum(grad_normed_total * unit_one, axis=0)
    grad_in = grad_residual + rms_back(grad_normed_total * first_norm_scale, unit_one, inverse_one)
    grad_shared_gate, grad_shared_up, grad_shared_down = (
        lax.psum_scatter(grad_shared_gate, ("dp", "expert"), scatter_dimension=0, tiled=True),
        lax.psum_scatter(grad_shared_up, ("dp", "expert"), scatter_dimension=0, tiled=True),
        lax.psum_scatter(grad_shared_down, ("dp", "expert"), scatter_dimension=1, tiled=True),
    )
    expert_reduced = (
        lax.psum_scatter(
            grad_expert_gate.astype(jnp.bfloat16), "dp", scatter_dimension=1, tiled=True
        ).astype(jnp.float32),
        lax.psum_scatter(
            grad_expert_up.astype(jnp.bfloat16), "dp", scatter_dimension=1, tiled=True
        ).astype(jnp.float32),
        lax.psum_scatter(
            grad_expert_down.astype(jnp.bfloat16), "dp", scatter_dimension=2, tiled=True
        ).astype(jnp.float32),
    )
    reduced = (
        lax.psum_scatter(grad_query_proj, ("dp", "expert"), scatter_dimension=0, tiled=True),
        lax.psum_scatter(grad_latent_proj, ("dp", "expert"), scatter_dimension=0, tiled=True),
        lax.psum_scatter(grad_latent_up, ("dp", "expert"), scatter_dimension=0, tiled=True),
        lax.psum_scatter(grad_output_proj, ("dp", "expert"), scatter_dimension=1, tiled=True),
        lax.psum_scatter(grad_norm_gain, ("dp", "expert"), scatter_dimension=0, tiled=True),
        lax.psum_scatter(grad_latent_gain, ("dp", "expert"), scatter_dimension=0, tiled=True),
        lax.psum_scatter(grad_router, ("dp", "expert"), scatter_dimension=0, tiled=True),
        lax.psum_scatter(grad_ffn_gain, ("dp", "expert"), scatter_dimension=0, tiled=True),
    )
    return (
        layer_out,
        grad_in,
        reduced[4],
        reduced[0],
        reduced[1],
        reduced[5],
        reduced[2],
        reduced[3],
        reduced[7],
        reduced[6],
        grad_shared_gate,
        grad_shared_up,
        grad_shared_down,
        expert_reduced[0],
        expert_reduced[1],
        expert_reduced[2],
    )


def solution(mesh):
    placed = (
        P(("dp", "expert"), None),
        P(),
        P("dp", "tensor"),
        P("dp", None),
        P(),
        P("dp", "tensor"),
        P("tensor", "dp"),
        P(),
        P(),
        P("dp", "tensor"),
        P("dp", "tensor"),
        P("tensor", "dp"),
        P("expert", None, "tensor"),
        P("expert", None, "tensor"),
        P("expert", "tensor", None),
        P(("dp", "expert"), None),
        P(),
        P(("dp", "expert"), None),
    )
    return jax.shard_map(
        per_device,
        mesh=mesh,
        in_specs=placed,
        out_specs=(
            P(("dp", "expert"), None),
            P(("dp", "expert"), None),
            P(("dp", "expert")),
            P(("dp", "expert"), "tensor"),
            P(("dp", "expert"), None),
            P(("dp", "expert")),
            P(("dp", "expert"), "tensor"),
            P("tensor", ("dp", "expert")),
            P(("dp", "expert")),
            P(("dp", "expert"), None),
            P(("dp", "expert"), "tensor"),
            P(("dp", "expert"), "tensor"),
            P("tensor", ("dp", "expert")),
            P("expert", "dp", "tensor"),
            P("expert", "dp", "tensor"),
            P("expert", "tensor", "dp"),
        ),
        check_vma=False,
    )
```

profile of v0, /device:TPU:9, one launch (start us, length us, event | category | flops | bytes accessed | tf_op | source)
XLA Modules:
  0.0 2897.2 jit_solution(3357246183442260503)
XLA Ops:
  15.6 32.9 %all-gather.8.cloned.1.call-done = bf16[2048,576]{0,1:T(8,128)(2,1)} async-done(((bf16[512,576]{0,1:T(8,128)(2,1)}), bf16[2048,576]{0,1:T(8,128)(2,1)}) %all-gather.8.cloned.1.call-update) | async-done | bytes 2359312 | tf_op jit(solution)/shard_map/all_gather | solution.py:139
  61.0 12.2 all_gather.28
  73.2 47.3 %all-gather.10.cloned.1.call-done = bf16[2048,1536]{1,0:T(8,128)(2,1)} async-done(((bf16[512,1536]{1,0:T(8,128)(2,1)}), bf16[2048,1536]{1,0:T(8,128)(2,1)}) %all-gather.10.cloned.1.call-update) | async-done | bytes 6291472 | tf_op jit(solution)/shard_map/all_gather | solution.py:138
  127.3 30.8 %all-gather.12.cloned.1.call-done = bf16[512,2048]{0,1:T(8,128)(2,1)} async-done(((bf16[128,2048]{0,1:T(8,128)(2,1)}), bf16[512,2048]{0,1:T(8,128)(2,1)}) %all-gather.12.cloned.1.call-update) | async-done | bytes 2097168 | tf_op jit(solution)/shard_map/all_gather | solution.py:140
  165.1 47.3 %all-gather.14.cloned.1.call-done = bf16[1024,2048]{1,0:T(8,128)(2,1)} async-done(((bf16[1024,512]{1,0:T(8,128)(2,1)}), bf16[1024,2048]{1,0:T(8,128)(2,1)}) %all-gather.14.cloned.1.call-update) | async-done | bytes 4194320 | tf_op jit(solution)/shard_map/all_gather | solution.py:141
  220.4 16.4 all-reduce.10.cloned.1.call-done
  249.9 140.3 %all_to_all.20 = bf16[16,96,2048]{2,1,0:T(8,128)(2,1)} all-to-all(bf16[16,96,2048]{2,1,0:T(8,128)(2,1)S(1)} %broadcast_select_fusion), channel_id=1, replica_groups=mesh['dp'=4,'expert'=4,'tensor'=2] {'expert'}, dimensions={0} | all-to-all | bytes 12582912 | tf_op jit(solution)/shard_map/all_to_all | solution.py:242
  390.2 13.8 fusion.7
  404.0 14.8 fusion.21
  453.5 120.3 %all-to-all-done.1 = bf16[16,96,2048]{2,1,0:T(8,128)(2,1)} async-done(((bf16[16,96,2048]{2,1,0:T(8,128)(2,1)}), bf16[16,96,2048]{2,1,0:T(8,128)(2,1)}, u32[]{:S(2)}, u32[]{:S(2)}) %all-to-all-start.1) | async-done | bytes 6291488 | tf_op jit(solution)/shard_map/all_to_all | solution.py:253
  573.7 10.7 gather_fusion.1
  595.3 15.8 scatter_custom_fusion.1
  620.2 134.3 %all-to-all-done.2 = bf16[16,96,2048]{2,1,0:T(8,128)(2,1)} async-done(((bf16[16,96,2048]{2,1,0:T(8,128)(2,1)}), bf16[16,96,2048]{2,1,0:T(8,128)(2,1)}, u32[]{:S(2)}, u32[]{:S(2)}) %all-to-all-start.2) | async-done | bytes 6291488 | tf_op jit(solution)/shard_map/all_to_all | solution.py:283
  754.5 15.9 fusion.19
  770.5 11.4 fusion.1
  781.9 11.7 fusion.13
  813.9 61.6 %all-gather.20.cloned.1.call-done = bf16[1408,2048]{1,0:T(8,128)(2,1)} async-done(((bf16[1408,512]{1,0:T(8,128)(2,1)}), bf16[1408,2048]{1,0:T(8,128)(2,1)}) %all-gather.20.cloned.1.call-update) | async-done | bytes 5767184 | tf_op jit(solution)/shard_map/all_gather | solution.py:144
  881.2 58.6 %all-to-all-done.3 = bf16[16,96,2048]{2,1,0:T(8,128)(2,1)} async-done(((bf16[16,96,2048]{2,1,0:T(8,128)(2,1)}), bf16[16,96,2048]{2,1,0:T(8,128)(2,1)}, u32[]{:S(2)}, u32[]{:S(2)}) %all-to-all-start.3) | async-done | bytes 6291488 | tf_op jit(solution)/shard_map/all_to_all | solution.py:309
  1062.1 11.5 bitcast_convert_fusion
  1073.6 11.6 bitcast_convert_fusion.2
  1085.5 11.6 bitcast_convert_fusion.1
  1159.8 58.7 %all-reduce.4 = (f32[2048]{0:T(1024)S(1)}, f32[512]{0:T(512)S(1)}, f32[2048]{0:T(1024)S(1)}) all-reduce(f32[2048]{0:T(1024)S(1)} %get-tuple-element.19, f32[512]{0:T(512)S(1)} %get-tuple-element.21, f32[2048]{0:T(1024)S(1)} %copy-done.45), channel_id=4, replica_groups=mesh['dp'=4,'expert'=4,'tensor'=2] {'dp','expert'}, use_global_device_ids=true, to_apply=%region_33.35.clone | all-reduce | flops 4608 | bytes 36864
  1228.6 99.4 %reduce-scatter.34.cloned.1.call-done = bf16[4,512,704]{1,2,0:T(8,128)(2,1)} async-done(((bf16[4,2048,704]{1,2,0:T(8,128)(2,1)}), bf16[4,512,704]{1,2,0:T(8,128)(2,1)}) %reduce-scatter.34.cloned.1.call-update) | async-done | bytes 2883600 | tf_op jit(solution)/shard_map/reduce_scatter | solution.py:431
  1333.2 109.9 %reduce-scatter.36.cloned.1.call-done = bf16[4,512,704]{1,2,0:T(8,128)(2,1)} async-done(((bf16[4,2048,704]{1,2,0:T(8,128)(2,1)}), bf16[4,512,704]{1,2,0:T(8,128)(2,1)}) %reduce-scatter.36.cloned.1.call-update) | async-done | bytes 2883600 | tf_op jit(solution)/shard_map/reduce_scatter | solution.py:434
  1448.3 57.4 %reduce-scatter.26.cloned.1.call-done = f32[128,16]{0,1:T(8,128)} async-done(((f32[2048,16]{0,1:T(8,128)}), f32[128,16]{0,1:T(8,128)}) %reduce-scatter.26.cloned.1.call-update) | async-done | bytes 8208 | tf_op jit(solution)/shard_map/reduce_scatter | solution.py:448
  1505.7 255.9 %reduce-scatter.28.cloned.1.call-done = f32[128,1408]{1,0:T(8,128)} async-done(((f32[2048,1408]{1,0:T(8,128)}), f32[128,1408]{1,0:T(8,128)}) %reduce-scatter.28.cloned.1.call-update) | async-done | bytes 720912 | tf_op jit(solution)/shard_map/reduce_scatter | solution.py:426
  1761.6 246.4 %reduce-scatter.30.cloned.1.call-done = f32[128,1408]{1,0:T(8,128)} async-done(((f32[2048,1408]{1,0:T(8,128)}), f32[128,1408]{1,0:T(8,128)}) %reduce-scatter.30.cloned.1.call-update) | async-done | bytes 720912 | tf_op jit(solution)/shard_map/reduce_scatter | solution.py:427
  2008.0 246.5 %reduce-scatter.32.cloned.1.call-done = f32[1408,128]{1,0:T(8,128)} async-done(((f32[1408,2048]{1,0:T(8,128)}), f32[1408,128]{1,0:T(8,128)}) %reduce-scatter.32.cloned.1.call-update) | async-done | bytes 720912 | tf_op jit(solution)/shard_map/reduce_scatter | solution.py:428
  2254.5 98.5 %reduce-scatter.22.cloned.1.call-done = f32[32,2048]{1,0:T(8,128)} async-done(((f32[512,2048]{1,0:T(8,128)}), f32[32,2048]{1,0:T(8,128)}) %reduce-scatter.22.cloned.1.call-update) | async-done | bytes 262160 | tf_op jit(solution)/shard_map/reduce_scatter | solution.py:444
  2353.0 143.2 %reduce-scatter.20.cloned.1.call-done = f32[128,576]{0,1:T(8,128)} async-done(((f32[2048,576]{0,1:T(8,128)}), f32[128,576]{0,1:T(8,128)}) %reduce-scatter.20.cloned.1.call-update) | async-done | bytes 294928 | tf_op jit(solution)/shard_map/reduce_scatter | solution.py:443
  2496.2 181.9 %reduce-scatter.24.cloned.1.call-done = f32[1024,128]{1,0:T(8,128)} async-done(((f32[1024,2048]{1,0:T(8,128)}), f32[1024,128]{1,0:T(8,128)}) %reduce-scatter.24.cloned.1.call-update) | async-done | bytes 524304 | tf_op jit(solution)/shard_map/reduce_scatter | solution.py:445
  2678.1 212.2 %reduce-scatter.18.cloned.1.call-done = f32[128,1536]{1,0:T(8,128)} async-done(((f32[2048,1536]{1,0:T(8,128)}), f32[128,1536]{1,0:T(8,128)}) %reduce-scatter.18.cloned.1.call-update) | async-done | bytes 786448 | tf_op jit(solution)/shard_map/reduce_scatter | solution.py:442
  (332 shorter events, 339.7 us)
Async XLA Ops:
  7.2 446.0 %copy-start = (bf16[2048,16]{0,1:T(8,128)(2,1)S(1)}, bf16[2048,16]{0,1:T(8,128)(2,1)}, u32[]{:S(2)}) copy-start(bf16[2048,16]{0,1:T(8,128)(2,1)} %param.28) | copy-start | bytes 196612
  7.3 41.2 %all-gather.8.cloned.1.call-start = ((), (), s32[]{:S(2)}) async-start(), calls=%async_computation.17 | async-start | bytes 2949120 | tf_op jit(solution)/shard_map/all_gather | solution.py:139
  8.0 112.5 %all-gather.10.cloned.1.call-start = ((), (), s32[]{:S(2)}) async-start(), calls=%async_computation.18 | async-start | bytes 7864320 | tf_op jit(solution)/shard_map/all_gather | solution.py:138
  8.7 149.4 %all-gather.12.cloned.1.call-start = ((), (), s32[]{:S(2)}) async-start(), calls=%async_computation.19 | async-start | bytes 2621440 | tf_op jit(solution)/shard_map/all_gather | solution.py:140
  10.9 201.5 %all-gather.14.cloned.1.call-start = ((), (), s32[]{:S(2)}) async-start(), calls=%async_computation.20 | async-start | bytes 5242880 | tf_op jit(solution)/shard_map/all_gather | solution.py:141
  11.4 225.4 %all-reduce.10.cloned.1.call-start = ((), (), s32[]{:S(2)}) async-start(), calls=%async_computation.21 | async-start | bytes 2097152 | tf_op jit(solution)/shard_map/psum | solution.py:213
  11.9 114.0 %copy-start.26 = (f32[2048]{0:T(1024)}, f32[2048]{0:T(1024)S(1)}, u32[]{:S(2)}) copy-start(f32[2048]{0:T(1024)S(1)} %convert_element_type.189) | copy-start | bytes 24580
  12.4 113.5 %copy-start.43 = (f32[512]{0:T(512)}, f32[512]{0:T(512)S(1)}, u32[]{:S(2)}) copy-start(f32[512]{0:T(512)S(1)} %convert_element_type.191) | copy-start | bytes 6148
  12.4 225.9 %copy-start.36 = (f32[2048]{0:T(1024)}, f32[2048]{0:T(1024)S(1)}, u32[]{:S(2)}) copy-start(f32[2048]{0:T(1024)S(1)} %convert_element_type.200) | copy-start | bytes 24580
  14.7 111.2 %copy-start.46 = (f32[128]{0:T(128)}, f32[128]{0:T(128)S(1)}, u32[]{:S(2)}) copy-start(f32[128]{0:T(128)S(1)} %add_rsqrt_fusion.2) | copy-start | bytes 1540
  60.8 99.1 %copy-start.38 = (bf16[512,64]{0,1:T(8,128)(2,1)}, bf16[512,64]{0,1:T(8,128)(2,1)S(1)}, u32[]{:S(2)}) copy-start(bf16[512,64]{0,1:T(8,128)(2,1)S(1)} %all_gather.29) | copy-start | bytes 196612
  432.7 141.0 %all-to-all-start.1 = ((bf16[16,96,2048]{2,1,0:T(8,128)(2,1)}), bf16[16,96,2048]{2,1,0:T(8,128)(2,1)}, u32[]{:S(2)}, u32[]{:S(2)}) async-start(bf16[16,96,2048]{2,1,0:T(8,128)(2,1)} %bitcast.222), calls=%async_computation.1 | async-start | bytes 12582912 | tf_op jit(solution)/shard_map/all_to_all | solution.py:253
  440.0 366.7 %all-gather.16.cloned.1.call-start = ((), (), s32[]{:S(2)}) async-start(), calls=%async_computation.22 | async-start | bytes 7208960 | tf_op jit(solution)/shard_map/all_gather | solution.py:142
  611.1 143.5 %all-to-all-start.2 = ((bf16[16,96,2048]{2,1,0:T(8,128)(2,1)}), bf16[16,96,2048]{2,1,0:T(8,128)(2,1)}, u32[]{:S(2)}, u32[]{:S(2)}) async-start(bf16[16,96,2048]{2,1,0:T(8,128)(2,1)} %bitcast.223), calls=%async_computation.2 | async-start | bytes 12582912 | tf_op jit(solution)/shard_map/all_to_all | solution.py:283
  619.5 190.8 %all-gather.18.cloned.1.call-start = ((), (), s32[]{:S(2)}) async-start(), calls=%async_computation.23 | async-start | bytes 7208960 | tf_op jit(solution)/shard_map/all_gather | solution.py:143
  797.3 142.5 %all-to-all-start.3 = ((bf16[16,96,2048]{2,1,0:T(8,128)(2,1)}), bf16[16,96,2048]{2,1,0:T(8,128)(2,1)}, u32[]{:S(2)}, u32[]{:S(2)}) async-start(bf16[16,96,2048]{2,1,0:T(8,128)(2,1)} %bitcast.221), calls=%async_computation.3 | async-start | bytes 12582912 | tf_op jit(solution)/shard_map/all_to_all | solution.py:309
  805.6 69.9 %all-gather.20.cloned.1.call-start = ((), (), s32[]{:S(2)}) async-start(), calls=%async_computation.24 | async-start | bytes 7208960 | tf_op jit(solution)/shard_map/all_gather | solution.py:144
  806.4 200.2 %all-reduce.12.cloned.1.call-start = ((), (), s32[]{:S(2)}) async-start(), calls=%async_computation.25 | async-start | bytes 2097152 | tf_op jit(solution)/shard_map/psum | solution.py:333
  983.0 77.3 %reduce-scatter.40.cloned.1.call-start = ((), (), s32[]{:S(2)}) async-start(), calls=%async_computation.37 | async-start | bytes 655360
  1031.3 100.1 %reduce-scatter.42.cloned.1.call-start = ((), (), s32[]{:S(2)}) async-start(), calls=%async_computation.38 | async-start | bytes 163840
  1052.8 83.0 %all-reduce.14.cloned.1.call-start = ((), (), s32[]{:S(2)}) async-start(), calls=%async_computation.39 | async-start | bytes 2359296 | tf_op jit(solution)/shard_map/psum | solution.py:267
  1062.0 161.1 %reduce-scatter.38.cloned.1.call-start = ((), (), s32[]{:S(2)}) async-start(), calls=%async_computation.36 | async-start | bytes 14417920 | tf_op jit(solution)/shard_map/reduce_scatter | solution.py:437
  1073.6 254.5 %reduce-scatter.34.cloned.1.call-start = ((), (), s32[]{:S(2)}) async-start(), calls=%async_computation.34 | async-start | bytes 14417920 | tf_op jit(solution)/shard_map/reduce_scatter | solution.py:431
  1085.2 357.9 %reduce-scatter.36.cloned.1.call-start = ((), (), s32[]{:S(2)}) async-start(), calls=%async_computation.35 | async-start | bytes 14417920 | tf_op jit(solution)/shard_map/reduce_scatter | solution.py:434
  1097.1 408.6 %reduce-scatter.26.cloned.1.call-start = ((), (), s32[]{:S(2)}) async-start(), calls=%async_computation.30 | async-start | bytes 139264 | tf_op jit(solution)/shard_map/reduce_scatter | solution.py:448
  1098.7 662.9 %reduce-scatter.28.cloned.1.call-start = ((), (), s32[]{:S(2)}) async-start(), calls=%async_computation.31 | async-start | bytes 12255232 | tf_op jit(solution)/shard_map/reduce_scatter | solution.py:426
  1105.6 902.3 %reduce-scatter.30.cloned.1.call-start = ((), (), s32[]{:S(2)}) async-start(), calls=%async_computation.32 | async-start | bytes 12255232 | tf_op jit(solution)/shard_map/reduce_scatter | solution.py:427
  1112.6 1141.9 %reduce-scatter.32.cloned.1.call-start = ((), (), s32[]{:S(2)}) async-start(), calls=%async_computation.33 | async-start | bytes 12255232 | tf_op jit(solution)/shard_map/reduce_scatter | solution.py:428
  1119.6 1233.4 %reduce-scatter.22.cloned.1.call-start = ((), (), s32[]{:S(2)}) async-start(), calls=%async_computation.28 | async-start | bytes 4456448 | tf_op jit(solution)/shard_map/reduce_scatter | solution.py:444
  1131.4 1364.8 %reduce-scatter.20.cloned.1.call-start = ((), (), s32[]{:S(2)}) async-start(), calls=%async_computation.27 | async-start | bytes 5013504 | tf_op jit(solution)/shard_map/reduce_scatter | solution.py:443
  1141.2 1536.8 %reduce-scatter.24.cloned.1.call-start = ((), (), s32[]{:S(2)}) async-start(), calls=%async_computation.29 | async-start | bytes 8912896 | tf_op jit(solution)/shard_map/reduce_scatter | solution.py:445
  1146.1 1744.1 %reduce-scatter.18.cloned.1.call-start = ((), (), s32[]{:S(2)}) async-start(), calls=%async_computation.26 | async-start | bytes 13369344 | tf_op jit(solution)/shard_map/reduce_scatter | solution.py:442
  (60 other events, 943.8 us)
Sparse Core Ops, SparseCore 0:
  9.9 38.4 all-gather.7
  50.3 70.1 all-gather.9
  122.9 35.1 all-gather.11
  159.8 52.5 all-gather.13
  216.4 20.3 all-reduce.9
  442.5 67.6 all-gather.15
  622.3 66.4 all-gather.17
  808.4 67.0 all-gather.19
  983.1 23.4 all-reduce.11
  1031.4 18.2 reduce-scatter.39
  1052.9 16.4 reduce-scatter.41
  1073.1 23.3 all-reduce.13
  1099.6 112.7 reduce-scatter.37
  1215.3 112.7 reduce-scatter.33
  1331.0 112.0 reduce-scatter.35
  1445.8 59.8 reduce-scatter.25
  1508.5 253.0 reduce-scatter.27
  1764.4 243.4 reduce-scatter.29
  2011.0 243.4 reduce-scatter.31
  2257.3 95.6 reduce-scatter.21
  2359.6 136.5 reduce-scatter.19
  2499.0 178.9 reduce-scatter.23
  2684.3 205.8 reduce-scatter.17
where the time goes:
time: 2910 us; the launch traced here: 2900 us
  waiting for transfers between devices  2210 us (76%)
  matrix products  234 us (8%)
  blocking collectives  230 us (8%)
  local copies, waits for them, and re-layouts  99.1 us (3%)
  other arithmetic  80 us (3%)
    reduce_scatter x1, waiting for transfers between devices, per_device(): lax.psum_scatter(grad_shared_gate, ('dp', 'expert'), scatter_dimension=0,...  256 us
    reduce_scatter x1, waiting for transfers between devices, per_device(): lax.psum_scatter(grad_shared_down, ('dp', 'expert'), scatter_dimension=1,...  247 us
    reduce_scatter x1, waiting for transfers between devices, per_device(): lax.psum_scatter(grad_shared_up, ('dp', 'expert'), scatter_dimension=0, t...  246 us
    reduce_scatter x1, waiting for transfers between devices, per_device(): lax.psum_scatter(grad_query_proj, ('dp', 'expert'), scatter_dimension=0,...  212 us
    reduce_scatter x1, waiting for transfers between devices, per_device(): lax.psum_scatter(grad_output_proj, ('dp', 'expert'), scatter_dimension=1,...  182 us
    reduce_scatter x1, waiting for transfers between devices, per_device(): lax.psum_scatter(grad_latent_proj, ('dp', 'expert'), scatter_dimension=0,...  143 us
    all_to_all x1, blocking collectives, per_device(): lax.all_to_all(outgoing, 'expert', split_axis=0, concat_axis=0, tiled=True)  140 us
    all_to_all x1, waiting for transfers between devices, per_device(): lax.all_to_all(grad_outgoing, 'expert', split_axis=0, concat_axis=0, tile...  134 us
  transfers between devices with their start and end apart: 26, of which 20 were waited for; matrix products, arithmetic and copies ran while one was open for 10% of the time, Pallas kernels for 0%

commit v1 on v0

v1 whole, which is shorter than its diff:
```python
import functools

import jax
import jax.numpy as jnp
from jax import lax
from jax.experimental import pallas as pl
from jax.experimental.pallas import tpu as pltpu
from jax.sharding import PartitionSpec as P

D = 2048
DN = 128
DR = 64
DV = 128
R = 512
EXPERTS = 16
NB = 4
NL = 2
LANES = 128

epsilon = 1e-06
masked_score = -1e30
bf16 = jnp.bfloat16
f32 = jnp.float32


def mm(left, right):
    return jnp.dot(left, right, preferred_element_type=f32)


def mm_nt(left, right):
    return lax.dot_general(left, right, (((1,), (1,)), ((), ())), preferred_element_type=f32)


def mm_tn(left, right):
    return lax.dot_general(left, right, (((0,), (0,)), ((), ())), preferred_element_type=f32)


def rms_stats(values):
    return lax.rsqrt(jnp.mean(values * values, axis=-1, keepdims=True) + epsilon)


def rms_back(grad_normed, unit_rows, inverse):
    return inverse * (
        grad_normed - unit_rows * jnp.mean(grad_normed * unit_rows, axis=-1, keepdims=True)
    )


def rotate(values, cosine, sine):
    half_width = values.shape[-1] // 2
    first_half = values[..., :half_width]
    second_half = values[..., half_width:]
    return jnp.concatenate(
        [first_half * cosine - second_half * sine, second_half * cosine + first_half * sine],
        axis=-1,
    )


def rotate_back(grads_in, cosine, sine):
    half_width = grads_in.shape[-1] // 2
    first_half = grads_in[..., :half_width]
    second_half = grads_in[..., half_width:]
    return jnp.concatenate(
        [first_half * cosine + second_half * sine, second_half * cosine - first_half * sine],
        axis=-1,
    )


def tree_layout(leaf_parent, token_index, trunk_len, seg_len):
    beyond = token_index - trunk_len
    in_trunk = token_index < trunk_len
    in_branch = (beyond >= 0) & (beyond < NB * seg_len)
    in_leaf = beyond >= NB * seg_len
    leaf_offset = beyond - NB * seg_len
    leaf_index = jnp.clip(leaf_offset // seg_len, 0, NB * NL - 1)
    position = jnp.where(
        in_trunk,
        token_index,
        jnp.where(
            in_branch, trunk_len + beyond % seg_len, trunk_len + seg_len + leaf_offset % seg_len
        ),
    )
    segment = jnp.where(
        in_trunk, 0, jnp.where(in_branch, 1 + beyond // seg_len, 1 + NB + leaf_index)
    )
    leaf_match = (leaf_index[:, None] == jnp.arange(NB * NL, dtype=jnp.int32)[None, :]).astype(
        jnp.int32
    )
    branch_of_leaf = 1 + jnp.sum(leaf_match * leaf_parent[None, :], axis=1)
    parent = jnp.where(in_trunk, -1, jnp.where(in_branch, 0, branch_of_leaf))
    grand = jnp.where(in_leaf, 0, -1)
    return (position, segment, parent, grand.astype(jnp.int32))


def visible(query_segment, query_parent, query_grand, query_index, key_segment, key_index):
    same_segment = (query_segment[:, None] == key_segment[None, :]) & (
        key_index[None, :] <= query_index[:, None]
    )
    ancestor = (key_segment[None, :] == query_parent[:, None]) | (
        key_segment[None, :] == query_grand[:, None]
    )
    return same_segment | ancestor


def swap(values, axis, step):
    return lax.ppermute(values, axis, [(k, k ^ step) for k in range(lax.axis_size(axis))])


def gather_rel(values, axis):
    size = lax.axis_size(axis)
    if size <= 4:
        return [values] + [swap(values, axis, s) for s in range(1, size)]
    full = lax.all_gather(values, axis)
    me = lax.axis_index(axis)
    return [lax.dynamic_index_in_dim(full, me ^ s, 0, False) for s in range(size)]


def exchange_rel(pieces, axis, stride=1):
    size = lax.axis_size(axis)
    if size <= 4:
        return [pieces[0]] + [swap(p, axis, k * stride) for k, p in enumerate(pieces) if k]
    me = lax.axis_index(axis)
    zero = jnp.zeros_like(pieces[0])
    full = jnp.stack([pieces[s // stride] if s % stride == 0 else zero for s in range(size)])
    order = me ^ jnp.arange(size)
    sent = lax.all_to_all(jnp.take(full, order, axis=0), axis, 0, 0, tiled=True)
    back = jnp.take(sent, order, axis=0)
    return [back[k * stride] for k in range(len(pieces))]


def canonical(pieces, me):
    stacked = jnp.stack(pieces)
    return [lax.dynamic_index_in_dim(stacked, me ^ c, 0, False) for c in range(len(pieces))]


def permute_blocks(values, me, count):
    width = values.shape[-1] // count
    return jnp.concatenate(
        [
            lax.dynamic_slice_in_dim(values, (me ^ s) * width, width, values.ndim - 1)
            for s in range(count)
        ],
        axis=-1,
    )


def total(pieces):
    result = pieces[0].astype(f32)
    for piece in pieces[1:]:
        result = result + piece.astype(f32)
    return result


def halves(own, other, core, dim):
    return jnp.where(
        core == 0,
        jnp.concatenate([own, other], axis=dim),
        jnp.concatenate([other, own], axis=dim),
    )


def pick_half(values, which, dim):
    width = values.shape[dim] // 2
    return lax.dynamic_slice_in_dim(values, which * width, width, dim)


def gather_shared(values, axis, core, dim):
    mine = gather_rel(pick_half(values, core, dim), axis)
    return [values] + [halves(p, swap(p, "tensor", 1), core, dim) for p in mine[1:]]


def after(value, *others):
    return lax.optimization_barrier((value,) + others)[0]


def gather_dp(values):
    if lax.axis_size("dp") != 4:
        return gather_rel(values, "dp")
    cut = values.shape[0] // 2
    first, second = swap(values, "dp", 1), swap(values, "dp", 2)
    last = jnp.concatenate(
        [swap(first[:cut], "dp", 2), swap(second[cut:], "dp", 1)], axis=0
    )
    return [values, first, second, last]


def reduce_dp(pieces):
    if lax.axis_size("dp") != 4:
        return total(exchange_rel(pieces, "dp")).astype(bf16)
    cut = pieces[0].shape[0] // 2
    low, high = [p[:cut] for p in pieces], [p[cut:] for p in pieces]
    low_there, high_there = swap(low[3], "dp", 1), swap(high[3], "dp", 2)
    low_here, high_here = swap(low[1], "dp", 1), swap(high[2], "dp", 2)
    low_next = swap((low[2].astype(f32) + low_there.astype(f32)).astype(bf16), "dp", 2)
    high_next = swap((high[1].astype(f32) + high_there.astype(f32)).astype(bf16), "dp", 1)
    return jnp.concatenate(
        [
            total([low[0], low_here, low_next]).astype(bf16),
            total([high[0], high_here, high_next]).astype(bf16),
        ],
        axis=0,
    )


def gather_z(own_half):
    return jnp.concatenate(gather_rel(own_half, "expert")[1:], axis=0)


def spread_all(own_half, others):
    own_pieces = gather_dp(own_half)
    own_there = swap(jnp.concatenate(own_pieces, axis=0), "tensor", 1)
    other_pieces = gather_dp(others)
    rows, many = own_half.shape[0], others.shape[0]
    near = swap(jnp.concatenate(other_pieces[1:3], axis=0), "tensor", 1)
    other_there = [
        swap(other_pieces[0], "tensor", 1),
        near[:many],
        near[many:],
        swap(other_pieces[3], "tensor", 1),
    ]
    mine, there = [], []
    for s in range(4):
        mine += [other_pieces[s], own_pieces[s]]
        there += [other_there[s], own_there[s * rows : (s + 1) * rows]]
    return jnp.concatenate(mine, axis=0), jnp.concatenate(there, axis=0)


def along_z(others, own):
    tok = own.shape[0]
    count = others.shape[0] // tok
    pieces = [own] + [others[s * tok : (s + 1) * tok] for s in range(count)]
    return total(exchange_rel(pieces, "expert"))


def scatter_all(joined, tok):
    size_dp = lax.axis_size("dp")
    rows = joined.shape[0] // size_dp
    many = rows - tok
    others = reduce_dp([joined[s * rows : s * rows + many] for s in range(size_dp)])
    own = reduce_dp(
        after([joined[s * rows + many : (s + 1) * rows] for s in range(size_dp)], others)
    )
    return along_z(others, own), others


def feed_kernel(sh_width, width, padded, at, n_own, n_oth, g_own, g_oth, wp_own, wp_oth,
                wd_own, wd_oth, hid_out, back_out):
    half = n_own.shape[1]
    rows = n_own.shape[0]
    lane = lax.broadcasted_iota(jnp.int32, (rows, LANES), 1)
    is_router = (lane >= sh_width) & (lane < sh_width + EXPERTS)
    is_own = lane == at[0]

    pre = mm_nt(n_own[...], wp_own[...]) + mm_nt(n_oth[...], wp_oth[...])
    back = mm_nt(g_own[:, :half], wd_own[...]) + mm_nt(g_oth[:, :half], wd_oth[...])
    gate_pre, up_pre = pre[:, :padded], pre[:, padded:]
    logits = jnp.where(is_router, up_pre[:, :LANES], masked_score)
    exps = jnp.exp(logits - jnp.max(logits, axis=1, keepdims=True))
    probs = exps / jnp.sum(exps, axis=1, keepdims=True)
    prob_own = jnp.sum(jnp.where(is_own, probs, 0.0), axis=1, keepdims=True)
    mask = g_own[:, half:].astype(f32)
    routed = jnp.sum(jnp.where(is_own, mask, 0.0), axis=1, keepdims=True)
    gate = routed * prob_own

    def activate(pre, up, back):
        sigmoid = 1.0 / (1.0 + jnp.exp(-pre))
        silu = pre * sigmoid
        slope = sigmoid * (1.0 + pre * (1.0 - sigmoid))
        return silu * up, back * up * slope, back * silu

    hid_s, gg_s, gu_s = activate(gate_pre[:, :LANES], up_pre[:, :LANES], back[:, :LANES])
    hid, gg, gu = activate(gate_pre[:, LANES:], up_pre[:, LANES:], back[:, LANES:])
    prob_grad = routed * jnp.sum(hid * back[:, LANES:], axis=1, keepdims=True)
    logit_grad = probs * (jnp.where(is_own, prob_grad, 0.0) - prob_own * prob_grad)
    hid_out[:, :LANES] = hid_s.astype(bf16)
    hid_out[:, LANES:] = (hid * gate).astype(bf16)
    back_out[:, :LANES] = gg_s.astype(bf16)
    back_out[:, LANES:padded] = (gg * gate).astype(bf16)
    back_out[:, padded : padded + LANES] = jnp.where(is_router, logit_grad, gu_s).astype(bf16)
    back_out[:, padded + LANES :] = (gu * gate).astype(bf16)


def feed_call(at, sh_width, width, padded, rows_own, rows_other, grad_own, grad_other, weights):
    tokens, half = rows_own.shape
    tile = 256
    by_rows = lambda m, at: (m, 0)
    fixed = lambda m, at: (0, 0)
    acts = [rows_own, rows_other, grad_own, grad_other]
    return pl.pallas_call(
        functools.partial(feed_kernel, sh_width, width, padded),
        grid_spec=pltpu.PrefetchScalarGridSpec(
            num_scalar_prefetch=1,
            grid=(tokens // tile,),
            in_specs=[pl.BlockSpec((tile, a.shape[1]), by_rows) for a in acts]
            + [pl.BlockSpec(w.shape, fixed, pipeline_mode=pl.Buffered(1)) for w in weights],
            out_specs=[
                pl.BlockSpec((tile, padded), by_rows),
                pl.BlockSpec((tile, 2 * padded), by_rows),
            ],
        ),
        out_shape=[
            jax.ShapeDtypeStruct((tokens, padded), bf16),
            jax.ShapeDtypeStruct((tokens, 2 * padded), bf16),
        ],
        compiler_params=pltpu.CompilerParams(
            dimension_semantics=("arbitrary",), vmem_limit_bytes=52 * 1024 * 1024
        ),
        cost_estimate=pl.CostEstimate(
            flops=12 * tokens * half * padded,
            bytes_accessed=2 * tokens * (4 * half + 3 * padded) + 12 * half * padded,
            transcendentals=tokens * padded,
        ),
    )(at, *acts, *weights)


def place_kernel(at, *refs):
    pieces, outs = refs[:12], refs[12:]
    step = pl.program_id(0)
    for s in range(4):

        @pl.when(step == s)
        def _():
            for k in range(3):
                outs[k][0] = pieces[3 * s + k][...].astype(f32)


def place_call(i, pieces, width):
    cols = pieces[0].shape[1]
    tile = width // 4
    i = jnp.reshape(i, (1,)).astype(jnp.int32)

    def read(s, k):
        return lambda step, r, at: (4 * k + jnp.where(step == s, r, jnp.where(step < s, 0, 3)), 0)

    return pl.pallas_call(
        place_kernel,
        grid_spec=pltpu.PrefetchScalarGridSpec(
            num_scalar_prefetch=1,
            grid=(4, 4),
            in_specs=[
                pl.BlockSpec((tile, cols), read(s, k)) for s in range(4) for k in range(3)
            ],
            out_specs=[
                pl.BlockSpec((1, tile, cols), lambda step, r, at: (at[0] ^ step, r, 0))
                for k in range(3)
            ],
        ),
        out_shape=[jax.ShapeDtypeStruct((4, width, cols), f32) for k in range(3)],
        compiler_params=pltpu.CompilerParams(
            dimension_semantics=("arbitrary", "arbitrary"), vmem_limit_bytes=32 * 1024 * 1024
        ),
        cost_estimate=pl.CostEstimate(
            flops=0, bytes_accessed=3 * 4 * width * cols * 6, transcendentals=0
        ),
    )(i, *[p for p in pieces for k in range(3)])


def per_device(
    layer_in,
    norm_gain,
    query_proj,
    latent_proj,
    latent_gain,
    latent_up,
    output_proj,
    ffn_gain,
    router,
    shared_gate,
    shared_up,
    shared_down,
    expert_gate,
    expert_up,
    expert_down,
    routes,
    leaf_parent,
    grad_out,
):
    tok = layer_in.shape[0]
    n_dp, n_ex = lax.axis_size("dp"), lax.axis_size("expert")
    i, j, core = lax.axis_index("dp"), lax.axis_index("expert"), lax.axis_index("tensor")
    tree_len = tok * n_ex
    seg_len = tree_len // 16
    trunk_len = 4 * seg_len
    block = D // n_dp
    sub = block // n_ex
    heads_local = output_proj.shape[0] // DV
    groups = min(n_ex, heads_local)
    hp = heads_local // groups
    qg = n_ex // groups
    group = j // qg
    n_q = n_ex // qg
    rows_q = tok * n_q
    qw = DN + DR
    uw = DN + DV
    score_scale = (DN + DR) ** (-0.5)

    x_rel = permute_blocks(layer_in, i, n_dp)
    gain_one = permute_blocks(norm_gain.astype(f32), i, n_dp)
    gain_two = permute_blocks(ffn_gain.astype(f32), i, n_dp)
    gain_latent = latent_gain.astype(f32)
    x_pieces = gather_shared(x_rel, "expert", core, 1)
    wq_pieces = gather_dp(lax.dynamic_slice_in_dim(query_proj, group * hp * qw, hp * qw, 1))
    wl_half = pick_half(latent_proj.T, core, 0)
    wl_got = jnp.concatenate(gather_dp(wl_half), axis=1)
    wl = halves(wl_got, swap(wl_got, "tensor", 1), core, 0)
    wq = jnp.concatenate(wq_pieces, axis=0)
    up_rows = R // n_dp
    up_own = lax.dynamic_slice_in_dim(latent_up, group * hp * uw, hp * uw, 1)
    wo_own = lax.dynamic_slice_in_dim(output_proj, group * hp * DV, hp * DV, 0)
    if up_own.shape[1] == wo_own.shape[1]:
        both = jnp.concatenate([wo_own, up_own], axis=0)
        both_pieces = gather_dp(after(both, wq_pieces[3]))
        wo_pieces = [p[: hp * DV] for p in both_pieces]
        up_pieces = [p[hp * DV :] for p in both_pieces]
    else:
        wo_pieces = gather_rel(wo_own, "dp")
        up_pieces = gather_rel(up_own, "dp")
        both_pieces = wo_pieces
    up = jnp.concatenate(canonical(up_pieces, i), axis=0)
    wo = jnp.concatenate(wo_pieces, axis=1)

    half = D // 2
    local_experts = expert_gate.shape[0]
    parts = n_dp // local_experts
    width = expert_gate.shape[2] // parts
    sh_width = shared_gate.shape[1] // (n_dp * n_ex)
    chosen, part_at = i // parts, (i % parts) * width
    expert_id = j * local_experts + chosen
    sh_pieces = []
    for s in range(n_dp):
        at_unit = (j * n_dp + (i ^ s)) * sh_width
        sh_pieces.append(
            jnp.concatenate(
                [
                    lax.dynamic_slice_in_dim(shared_gate, at_unit, sh_width, 1).T,
                    lax.dynamic_slice_in_dim(shared_up, at_unit, sh_width, 1).T,
                    lax.dynamic_slice_in_dim(shared_down, at_unit, sh_width, 0),
                ],
                axis=0,
            )
        )
    sh_pieces = exchange_rel(after(sh_pieces, both_pieces[3]), "dp")
    sh_rows = jnp.concatenate(canonical(sh_pieces, i), axis=1)
    hidden_width = -(-(LANES + width) // LANES) * LANES

    def routed_rows(weight):
        return lax.dynamic_slice(weight, (chosen, part_at, 0), (1, width, D))[0]

    def hidden_rows(shared, routed, extra):
        room = LANES - sh_width - (0 if extra is None else EXPERTS)
        parts_in = [shared] + ([] if extra is None else [extra])
        return jnp.concatenate(
            parts_in
            + [
                jnp.zeros((room, D), bf16),
                routed,
                jnp.zeros((hidden_width - LANES - width, D), bf16),
            ],
            axis=0,
        )

    gate_w = hidden_rows(
        sh_rows[:sh_width], routed_rows(jnp.swapaxes(expert_gate, 1, 2)), None
    )
    up_w = hidden_rows(
        sh_rows[sh_width : 2 * sh_width], routed_rows(jnp.swapaxes(expert_up, 1, 2)), router.T
    )
    down_w = hidden_rows(sh_rows[2 * sh_width :], routed_rows(expert_down), None)
    pre_w = jnp.concatenate([gate_w, up_w], axis=0)
    pre_own, pre_other = pick_half(pre_w, core, 1), pick_half(pre_w, 1 - core, 1)
    down_own, down_other = pick_half(down_w, core, 1), pick_half(down_w, 1 - core, 1)

    lanes = jnp.arange(LANES, dtype=jnp.int32) - sh_width
    route_lanes = jnp.any(routes[:, :, None] == lanes[None, None, :], axis=1).astype(bf16)
    g_half = jnp.concatenate([pick_half(grad_out, core, 1), route_lanes], axis=1)
    g_others = gather_z(after(g_half, x_pieces[-1]))
    g_rows = jnp.concatenate([after(g_others, sh_pieces[-1]), g_half], axis=0)
    grad_own = jnp.concatenate(gather_dp(g_rows), axis=0)
    grad_other = swap(grad_own, "tensor", 1)

    slots = jnp.arange(tree_len, dtype=jnp.int32)
    token_index = (j ^ (slots // tok)) * tok + slots % tok

    def queries_of(values):
        if qg == 1:
            return values
        split = values.reshape((n_q, qg, tok) + values.shape[1:])[:, 0]
        return split.reshape((rows_q,) + values.shape[1:])

    position, segment, parent, grand = tree_layout(leaf_parent, token_index, trunk_len, seg_len)
    freqs = 10000.0 ** (-2.0 * jnp.arange(DR // 2, dtype=f32) / DR)
    angles = position.astype(f32)[:, None] * freqs[None, :]
    cosine, sine = jnp.cos(angles), jnp.sin(angles)
    q_cos, q_sin = queries_of(cosine), queries_of(sine)
    allowed = visible(
        queries_of(segment),
        queries_of(parent),
        queries_of(grand),
        queries_of(token_index),
        segment,
        token_index,
    )

    own_rows = x_rel.astype(f32)
    inverse_one = rms_stats(own_rows)
    unit_one = own_rows * inverse_one
    tree_rows = jnp.concatenate(x_pieces, axis=0).astype(f32)
    normed = (tree_rows * rms_stats(tree_rows) * gain_one).astype(bf16)
    normed_q = queries_of(normed)
    query_all = mm(normed_q, wq)
    latent_all = mm_nt(normed, wl)
    inverse_latent = rms_stats(latent_all[:, :R])
    unit_latent = latent_all[:, :R] * inverse_latent
    latent = (unit_latent * gain_latent).astype(bf16)
    key_rope = rotate(latent_all[:, R:], cosine, sine).astype(bf16)
    keys = jnp.concatenate([latent, key_rope], axis=1)
    up_key = [up[:, h * uw : h * uw + DN] for h in range(hp)]
    up_value = [up[:, h * uw + DN : (h + 1) * uw] for h in range(hp)]
    query_nope = [query_all[:, h * qw : h * qw + DN].astype(bf16) for h in range(hp)]
    queries = jnp.concatenate(
        [
            jnp.concatenate(
                [
                    mm_nt(query_nope[h], up_key[h]).astype(bf16),
                    rotate(query_all[:, h * qw + DN : (h + 1) * qw], q_cos, q_sin).astype(bf16),
                ],
                axis=1,
            )
            for h in range(hp)
        ],
        axis=0,
    )
    raw_scores = mm_nt(queries, keys).reshape(hp, rows_q, tree_len)
    scores = jnp.where(allowed[None], raw_scores * score_scale, masked_score)
    exp_scores = jnp.exp(scores - jnp.max(scores, axis=-1, keepdims=True))
    probs = exp_scores / jnp.sum(exp_scores, axis=-1, keepdims=True)
    probs = probs.reshape(hp * rows_q, tree_len)
    probs_low = probs.astype(bf16)
    mixed = mm(probs_low, latent).astype(bf16)
    mixed_head = [mixed[h * rows_q : (h + 1) * rows_q] for h in range(hp)]
    heads_out = jnp.concatenate(
        [mm(mixed_head[h], up_value[h]).astype(bf16) for h in range(hp)], axis=1
    )
    wo_mine, wo_other = pick_half(wo, core, 1), pick_half(wo, 1 - core, 1)

    def tree_scatter(partial_own, partial_other, count, stride):
        joined = partial_own + swap(partial_other.astype(bf16), "tensor", 1).astype(f32)
        joined = joined.astype(bf16)
        own = total(
            exchange_rel(
                [joined[s * tok : (s + 1) * tok] for s in range(count)], "expert", stride
            )
        )
        return halves(own, swap(own, "tensor", 1), core, 1)

    attention = tree_scatter(mm(heads_out, wo_mine), mm(heads_out, wo_other), n_q, qg)
    residual = own_rows + attention
    inverse_two = rms_stats(residual)
    unit_two = residual * inverse_two
    normed_two = permute_blocks((unit_two * gain_two).astype(bf16), i, n_dp)

    n_half = pick_half(normed_two, core, 1)
    rows_own, rows_other = spread_all(n_half, gather_z(n_half))
    at = jnp.reshape(sh_width + expert_id, (1,)).astype(jnp.int32)
    hidden_scaled, back_pre = feed_call(
        at, sh_width, width, hidden_width, rows_own, rows_other, grad_own, grad_other,
        [pre_own, pre_other, down_own, down_other],
    )

    def join(mine, theirs):
        return (mine.astype(f32) + swap(theirs, "tensor", 1).astype(f32)).astype(bf16)

    rows_theirs = mm(back_pre, pre_other).astype(bf16)
    back_later = after(back_pre, rows_theirs)
    grad_rows = join(mm(back_later, pre_own).astype(bf16), rows_theirs)
    gn2_half, gn2_sent = scatter_all(grad_rows, tok)
    gn2 = permute_blocks(halves(gn2_half, swap(gn2_half, "tensor", 1), core, 1), i, n_dp)

    grad_ffn_gain = jnp.sum(gn2 * unit_two, axis=0, keepdims=True)
    grad_residual = permute_blocks(grad_out, i, n_dp).astype(f32) + rms_back(
        gn2 * gain_two, unit_two, inverse_two
    )

    hidden_late, back_late, _ = lax.optimization_barrier((hidden_scaled, back_pre, grad_rows))
    out_joined = join(
        mm(hidden_late, down_own).astype(bf16), mm(hidden_late, down_other).astype(bf16)
    )
    out_joined = after(out_joined, gn2_sent)
    rows_dp = tokens_dp = out_joined.shape[0] // n_dp
    out_mine = reduce_dp([out_joined[s * rows_dp : (s + 1) * rows_dp] for s in range(n_dp)])
    ffn_half = along_z(out_mine[: rows_dp - tok], out_mine[rows_dp - tok :])
    out_half = (pick_half(permute_blocks(residual, i, n_dp), core, 1) + ffn_half).astype(bf16)
    layer_out = halves(out_half, swap(out_half, "tensor", 1), core, 1)

    def block_offset(c):
        per_half = n_dp // 2
        return ((c // per_half) ^ core) * half + (c % per_half) * block

    def both_halves(left, own, other):
        return jnp.concatenate(
            [mm_tn(left, own).astype(bf16), mm_tn(left, other).astype(bf16)], axis=1
        )

    pre_grads = both_halves(back_late, rows_own, rows_other)
    down_grads = both_halves(hidden_late, grad_own[:, :half], grad_other[:, :half])
    routed_at = slice(LANES, LANES + width)
    up_at = slice(hidden_width + LANES, hidden_width + LANES + width)
    sent_width = -(-sh_width // 16) * 16
    feed_pieces = []
    for s in range(n_dp):
        start = block_offset(i ^ s)
        pre_cut = lax.dynamic_slice_in_dim(pre_grads, start, block, 1)
        down_cut = lax.dynamic_slice_in_dim(down_grads, start, block, 1)
        feed_pieces.append(
            jnp.concatenate(
                [
                    pre_cut[routed_at],
                    pre_cut[up_at],
                    down_cut[routed_at],
                    pre_cut[:sent_width],
                    pre_cut[hidden_width : hidden_width + sent_width],
                    down_cut[:sent_width],
                ],
                axis=0,
            )
        )
    feed_pieces = exchange_rel(after(feed_pieces, out_mine), "dp")
    if parts == 1:
        placed = place_call(i, feed_pieces, width)
    else:
        stacked = jnp.stack(canonical(feed_pieces, i)).astype(f32)
        placed = [
            stacked[:, k * width : (k + 1) * width].reshape(local_experts, parts * width, block)
            for k in range(3)
        ]
    grad_expert_gate = jnp.swapaxes(placed[0], 1, 2)
    grad_expert_up = jnp.swapaxes(placed[1], 1, 2)
    grad_expert_down = placed[2]
    shared_all = jnp.stack(canonical([p[3 * width :] for p in feed_pieces], i))
    shared_all = jnp.stack(
        canonical(
            exchange_rel(
                [lax.dynamic_slice_in_dim(shared_all, (j ^ s) * sub, sub, 2) for s in range(n_ex)],
                "expert",
            ),
            j,
        )
    )

    def shared_part(k):
        rows = shared_all[:, :, k * sent_width : k * sent_width + sh_width]
        return rows.reshape(-1, sub).astype(f32)

    grad_shared_gate, grad_shared_up = shared_part(0).T, shared_part(1).T
    grad_shared_down = shared_part(2)
    router_block = pre_grads[hidden_width + sh_width : hidden_width + sh_width + EXPERTS]
    grad_router_rows = permute_blocks(
        halves(router_block[:, :half], router_block[:, half:], core, 1), i, n_dp
    )

    res_pieces = gather_shared(grad_residual.astype(bf16), "expert", core, 1)
    res_q = jnp.concatenate(res_pieces[::qg], axis=0)
    grad_heads = mm_nt(res_q, wo).astype(bf16)
    grad_head = [grad_heads[:, h * DV : (h + 1) * DV] for h in range(hp)]

    grad_wo = mm_tn(heads_out, res_q)

    grad_mixed = jnp.concatenate(
        [mm_nt(grad_head[h], up_value[h]).astype(bf16) for h in range(hp)], axis=0
    )
    grad_att = mm_nt(grad_mixed, latent)
    delta = jnp.sum(probs * grad_att, axis=-1, keepdims=True)
    score_grad = (probs * (grad_att - delta) * score_scale).astype(bf16)
    grad_queries = mm(score_grad, keys)
    grad_keys = mm_tn(score_grad, queries)
    grad_latent_keys = grad_keys[:, :R] + mm_tn(probs_low, grad_mixed)
    grad_query_latent = grad_queries[:, :R].astype(bf16)
    grad_query_parts, grad_up_parts = [], []
    for h in range(hp):
        rows = slice(h * rows_q, (h + 1) * rows_q)
        grad_query_parts.append(mm(grad_query_latent[rows], up_key[h]))
        grad_query_parts.append(rotate_back(grad_queries[rows, R:], q_cos, q_sin))
        grad_up_parts.append(mm_tn(query_nope[h], grad_query_latent[rows]))
        grad_up_parts.append(mm_tn(grad_head[h], mixed_head[h]))
    grad_query_all = jnp.concatenate(grad_query_parts, axis=1).astype(bf16)
    grad_latent_gain = jnp.sum(grad_latent_keys * unit_latent, axis=0, keepdims=True)
    grad_latent_all = jnp.concatenate(
        [
            rms_back(grad_latent_keys * gain_latent, unit_latent, inverse_latent),
            rotate_back(grad_keys[:, R:], cosine, sine),
        ],
        axis=1,
    ).astype(bf16)

    grad_query_rows = grad_query_all
    if qg > 1:
        grad_query_rows = jnp.pad(
            grad_query_all.reshape(n_q, 1, tok, -1), ((0, 0), (0, qg - 1), (0, 0), (0, 0))
        ).reshape(tree_len, -1)
    back_mine = mm_nt(grad_query_rows, pick_half(wq, core, 0)) + mm(
        grad_latent_all, pick_half(wl, core, 1)
    )
    back_other = mm_nt(grad_query_rows, pick_half(wq, 1 - core, 0)) + mm(
        grad_latent_all, pick_half(wl, 1 - core, 1)
    )
    grad_normed = tree_scatter(back_mine, back_other, n_ex, 1)
    grad_norm_gain = jnp.sum(grad_normed * unit_one, axis=0, keepdims=True)
    grad_in = permute_blocks(
        grad_residual + rms_back(grad_normed * gain_one, unit_one, inverse_one), i, n_dp
    )

    by_d = jnp.concatenate(
        [grad_wo, mm_tn(grad_query_all, normed_q), mm_tn(grad_latent_all, normed)], axis=0
    ).astype(bf16)
    by_r = jnp.concatenate(grad_up_parts, axis=0).astype(bf16)
    d_rows, r_rows = by_d.shape[0], by_r.shape[0]
    by_r = [lax.dynamic_slice_in_dim(by_r, (i ^ s) * up_rows, up_rows, 1) for s in range(n_dp)]
    split_r = block // up_rows
    cut_r = r_rows // split_r
    pieces = [
        jnp.concatenate(
            [by_d[:, s * block : (s + 1) * block]]
            + [jnp.concatenate([by_r[s][c * cut_r : (c + 1) * cut_r] for c in range(split_r)], 1)],
            axis=0,
        )
        for s in range(n_dp)
    ]
    mine = reduce_dp(pieces)
    mine_d = mine[:d_rows]
    mine_r = jnp.concatenate(
        [mine[d_rows:, c * up_rows : (c + 1) * up_rows] for c in range(split_r)], axis=0
    )
    up_sub = up_rows // n_ex
    got_d = exchange_rel(
        [lax.dynamic_slice_in_dim(mine_d, (j ^ s) * sub, sub, 1) for s in range(n_ex)], "expert"
    )
    got_r = exchange_rel(
        [lax.dynamic_slice_in_dim(mine_r, (j ^ s) * up_sub, up_sub, 1) for s in range(n_ex)],
        "expert",
    )

    def over_groups(pieces):
        ordered = canonical(pieces, j)
        return jnp.concatenate(
            [total(ordered[g * qg : (g + 1) * qg]) for g in range(groups)], axis=0
        )

    wo_rows, wq_rows = hp * DV, hp * qw
    grad_output_proj = over_groups([p[:wo_rows] for p in got_d])
    grad_query_proj = over_groups([p[wo_rows : wo_rows + wq_rows] for p in got_d]).T
    grad_latent_up = over_groups(got_r).T
    grad_wl = total([p[wo_rows + wq_rows :] for p in got_d])
    grad_latent_proj = (grad_wl + swap(grad_wl, "tensor", 1)).T

    small_d = jnp.concatenate(
        [0.5 * grad_norm_gain, 0.5 * grad_ffn_gain, grad_router_rows.astype(f32)], axis=0
    )
    small = [
        jnp.concatenate(
            [
                small_d[:, s * block : (s + 1) * block].reshape(-1, n_ex, sub),
                jnp.pad(
                    lax.dynamic_slice_in_dim(
                        grad_latent_gain, (i ^ s) * up_rows, up_rows, 1
                    ).reshape(1, n_ex, up_sub),
                    ((0, 0), (0, 0), (0, sub - up_sub)),
                ),
            ],
            axis=0,
        )
        for s in range(n_dp)
    ]
    small = total(exchange_rel(small, "dp"))
    small = total(
        exchange_rel(
            [lax.dynamic_index_in_dim(small, j ^ s, 1, False) for s in range(n_ex)], "expert"
        )
    )
    small = small + swap(small, "tensor", 1)

    return (
        layer_out,
        grad_in,
        small[0],
        grad_query_proj,
        grad_latent_proj,
        small[2 + EXPERTS, :up_sub],
        grad_latent_up,
        grad_output_proj,
        small[1],
        small[2 : 2 + EXPERTS].T,
        grad_shared_gate,
        grad_shared_up,
        grad_shared_down,
        grad_expert_gate,
        grad_expert_up,
        grad_expert_down,
    )


def solution(mesh):
    placed = (
        P(("dp", "expert"), None),
        P(),
        P("dp", "tensor"),
        P("dp", None),
        P(),
        P("dp", "tensor"),
        P("tensor", "dp"),
        P(),
        P(),
        P("dp", "tensor"),
        P("dp", "tensor"),
        P("tensor", "dp"),
        P("expert", None, "tensor"),
        P("expert", None, "tensor"),
        P("expert", "tensor", None),
        P(("dp", "expert"), None),
        P(),
        P(("dp", "expert"), None),
    )
    return jax.shard_map(
        per_device,
        mesh=mesh,
        in_specs=placed,
        out_specs=(
            P(("dp", "expert"), None),
            P(("dp", "expert"), None),
            P(("dp", "expert")),
            P(("dp", "expert"), "tensor"),
            P(("dp", "expert"), None),
            P(("dp", "expert")),
            P(("dp", "expert"), "tensor"),
            P("tensor", ("dp", "expert")),
            P(("dp", "expert")),
            P(("dp", "expert"), None),
            P(("dp", "expert"), "tensor"),
            P(("dp", "expert"), "tensor"),
            P("tensor", ("dp", "expert")),
            P("expert", "dp", "tensor"),
            P("expert", "dp", "tensor"),
            P("expert", "tensor", "dp"),
        ),
        check_vma=False,
    )
```

time: 2910 us -> 840 us (0.29)
  waiting for transfers between devices: 2210 us -> 305 us
  blocking collectives: 230 us -> 0 us
  matrix products: 234 us -> 107 us
  starting transfers between devices: 26.4 us -> 130 us
  Pallas kernels: 0 us -> 46.9 us
  other arithmetic: 80 us -> 111 us
    reduce_scatter x11 -> x0, waiting for transfers between devices: 1650 us -> none  [the longest x1 256 us: per_device(): lax.psum_scatter(grad_shared_gate, ('dp', 'expert'), scatter_dimension=0,...]
    all_to_all x3 -> x0, waiting for transfers between devices: 313 us -> none  [the longest x1 134 us: per_device(): lax.all_to_all(grad_outgoing, 'expert', split_axis=0, concat_axis=0, tile...]
    ppermute x0 -> x115, waiting for transfers between devices: none -> 305 us  [swap(): lax.ppermute(values, axis, [(k, k ^ step) for k in range(lax.axis_size(ax...]
    all_gather x7 -> x0, waiting for transfers between devices: 220 us -> none  [the longest x1 61.6 us: per_device(): lax.all_gather(shared_down, 'dp', axis=1, tiled=True)]
    all_to_all x1 -> x0, blocking collectives: 140 us -> none  [per_device(): lax.all_to_all(outgoing, 'expert', split_axis=0, concat_axis=0, tiled=True)]
    ppermute x0 -> x115, starting transfers between devices: none -> 130 us  [swap(): lax.ppermute(values, axis, [(k, k ^ step) for k in range(lax.axis_size(ax...]
    dot_general x42 -> x37, matrix products: 234 us -> 107 us  [the longest x13 48.2 us: mm_tn(): lax.dot_general(left, right, (((0,), (0,)), ((), ())), preferred_element_...]
    unnamed x1 -> x0, blocking collectives: 58.7 us -> none
  transfers between devices with their start and end apart: 26 -> 115, of which waited for: 20 -> 42; matrix products, arithmetic and copies ran while one was open for 10% -> 34% of each run, Pallas kernels for 0% -> 2%
where the time goes in v1:
time: 840 us; the launch traced here: 830 us
  waiting for transfers between devices  305 us (36%)
  starting transfers between devices  130 us (15%)
  local copies, waits for them, and re-layouts  126 us (15%)
  other arithmetic  111 us (13%)
  matrix products  107 us (13%)
  Pallas kernels  46.9 us (6%)
    ppermute x115, waiting for transfers between devices, swap(): lax.ppermute(values, axis, [(k, k ^ step) for k in range(lax.axis_size(ax...  305 us
    ppermute x115, starting transfers between devices, swap(): lax.ppermute(values, axis, [(k, k ^ step) for k in range(lax.axis_size(ax...  130 us
    unnamed x440, local copies, waits for them, and re-layouts  56.2 us
    dot_general x13, matrix products, mm_tn(): lax.dot_general(left, right, (((0,), (0,)), ((), ())), preferred_element_...  48.2 us
    dot_general x14, matrix products, mm(): return jnp.dot(left, right, preferred_element_type=f32)  47.1 us
    pallas_call x1, Pallas kernels, feed_call(): pl.pallas_call(functools.partial(feed_kernel, sh_width, width, padded), g...  33.6 us
    select_n x10, other arithmetic, halves(): jnp.where(core == 0, jnp.concatenate([own, other], axis=dim), jnp.concate...  26.9 us
  transfers between devices with their start and end apart: 115, of which 42 were waited for; matrix products, arithmetic and copies ran while one was open for 34% of the time, Pallas kernels for 2%

profile of v1, /device:TPU:9, one launch (start us, length us, event | category | flops | bytes accessed | tf_op | source)
XLA Modules:
  0.0 829.6 jit_solution(14964312219147606528)
XLA Ops:
  55.5 13.3 %collective-permute-done.4 = bf16[128,1024]{1,0:T(8,128)(2,1)S(1)} collective-permute-done((bf16[128,1024]{1,0:T(8,128)(2,1)}, bf16[128,1024]{1,0:T(8,128)(2,1)S(1)}, u32[]{:S(2)}, u32[]{:S(2)}) %collective-permute-start.4) | collective-permute-done | bytes 262176 | tf_op jit(solution)/shard_map/ppermute | solution.py:105
  103.3 8.7 %collective-permute-done.41 = bf16[128,1152]{1,0:T(8,128)(2,1)} collective-permute-done((bf16[128,1152]{1,0:T(8,128)(2,1)}, bf16[128,1152]{1,0:T(8,128)(2,1)}, u32[]{:S(2)}, u32[]{:S(2)}) %collective-permute-start.41) | collective-permute-done | bytes 294944 | tf_op jit(solution)/shard_map/ppermute | solution.py:105
  130.8 25.0 %maximum_select_fusion = bf16[576,2048]{1,0:T(8,128)(2,1)S(1)} fusion(bf16[288,2048]{1,0:T(8,128)(2,1)} %collective-permute-done.17, bf16[144,512]{1,0:T(8,128)(2,1)S(1)} %copy-done.89, bf16[144,512]{1,0:T(8,128)(2,1)S(1)} %copy-done.91, bf16[288,512]{1,0:T(8,128)(2,1)S(1)} %copy-done.43, bf16[288,512]{1,0:T(8,128)(2,1)S(1)} %copy-done.45, ...), kind=kLoop, calls=%fused_computation.41 | loop fusion | flops 29491200 | bytes 4718593 | tf_op jit(solution)/shard_map/jit(_where)/select_n | solution.py:154
  193.5 9.5 %collective-permute-done.22 = bf16[128,1024]{1,0:T(8,128)(2,1)S(1)} collective-permute-done((bf16[128,1024]{1,0:T(8,128)(2,1)S(1)}, bf16[128,1024]{1,0:T(8,128)(2,1)S(1)}, u32[]{:S(2)}, u32[]{:S(2)}) %collective-permute-start.22) | collective-permute-done | bytes 262176 | tf_op jit(solution)/shard_map/ppermute | solution.py:105
  217.7 8.5 %collective-permute-done.24 = bf16[128,1024]{1,0:T(8,128)(2,1)S(1)} collective-permute-done((bf16[128,1024]{1,0:T(8,128)(2,1)S(1)}, bf16[128,1024]{1,0:T(8,128)(2,1)S(1)}, u32[]{:S(2)}, u32[]{:S(2)}) %collective-permute-start.24) | collective-permute-done | bytes 262176 | tf_op jit(solution)/shard_map/ppermute | solution.py:105
  226.2 6.9 collective-permute-done.25
  233.2 7.2 collective-permute-done.26
  248.5 15.9 %collective-permute-done.28 = bf16[128,1024]{1,0:T(8,128)(2,1)S(1)} collective-permute-done((bf16[128,1024]{1,0:T(8,128)(2,1)S(1)}, bf16[128,1024]{1,0:T(8,128)(2,1)S(1)}, u32[]{:S(2)}, u32[]{:S(2)}) %collective-permute-start.28) | collective-permute-done | bytes 262176 | tf_op jit(solution)/shard_map/ppermute | solution.py:105
  270.8 7.6 collective-permute-done.31
  290.5 6.9 constant_dynamic-slice_fusion.46
  302.0 33.6 %shard_map.297 = (bf16[2048,896]{1,0:T(8,128)(2,1)}, bf16[2048,1792]{1,0:T(8,128)(2,1)}) custom-call(s32[1]{0:T(128)} %bitcast.10.at, bf16[2048,1024]{1,0:T(8,128)(2,1)} %copy-done.149, bf16[2048,1024]{1,0:T(8,128)(2,1)} %copy-done.128, bf16[2048,1152]{1,0:T(8,128)(2,1)} %copy-done.127, bf16[2048,1152]{1,0:T(8,128)(2,1)} %collective-permute-done.47.g_oth, ...), custom_call_target="tpu_custom_call" | custom-call | flops 22548578304 | bytes 38797312 | tf_op jit(solution)/shard_map/pallas_call | solution.py:288
  335.6 11.5 %convolution_convert_fusion = bf16[2048,1024]{1,0:T(8,128)(2,1)} fusion(bf16[2048,1792]{1,0:T(8,128)(2,1)} %get-tuple-element.54, bf16[1792,1024]{1,0:T(8,128)(2,1)S(1)} %copy-done.23), kind=kOutput, calls=%fused_computation.30 | convolution fusion | flops 7518289920 | bytes 15204352 | tf_op jit(solution)/shard_map/dot_general | solution.py:27
  351.3 10.0 %fusion.216 = bf16[2048,1024]{1,0:T(8,128)(2,1)S(1)} fusion(bf16[2048,1792]{1,0:T(8,128)(2,1)} %get-tuple-element.54, bf16[1792,1024]{1,0:T(8,128)(2,1)S(1)} %copy-done.22), kind=kOutput, calls=%fused_computation.626 | convolution fusion | flops 7516192768 | bytes 15204352 | tf_op jit(solution)/shard_map/dot_general | solution.py:27
  368.2 10.8 %convolution_convert_fusion.2 = bf16[1792,1024]{1,0:T(8,128)(2,1)S(1)} fusion(bf16[2048,1792]{1,0:T(8,128)(2,1)} %get-tuple-element.54, bf16[2048,1024]{1,0:T(8,128)(2,1)S(1)} %copy-done.129), kind=kOutput, calls=%fused_computation.32 | convolution fusion | flops 7518027776 | bytes 15204352 | tf_op jit(solution)/shard_map/dot_general | solution.py:35
  379.0 11.5 %convolution_convert_fusion.3 = bf16[1792,1024]{1,0:T(8,128)(2,1)S(1)} fusion(bf16[2048,1792]{1,0:T(8,128)(2,1)} %get-tuple-element.54, bf16[2048,1024]{1,0:T(8,128)(2,1)} %copy-done.149), kind=kOutput, calls=%fused_computation.33 | convolution fusion | flops 7518027776 | bytes 15204352 | tf_op jit(solution)/shard_map/dot_general | solution.py:35
  390.5 6.1 convolution_convert_fusion.1
  408.3 7.5 fusion.16
  422.3 7.4 collective-permute-done.54
  432.6 6.7 collective-permute-done.57
  474.0 17.9 %collective-permute-done.82 = bf16[128,1024]{1,0:T(8,128)(2,1)S(1)} collective-permute-done((bf16[128,1024]{1,0:T(8,128)(2,1)S(1)}, bf16[128,1024]{1,0:T(8,128)(2,1)S(1)}, u32[]{:S(2)}, u32[]{:S(2)}) %collective-permute-start.82) | collective-permute-done | bytes 262176 | tf_op jit(solution)/shard_map/ppermute | solution.py:105
  496.3 5.9 collective-permute-done.78
  502.6 20.4 %collective-permute-done.111.refs_9_.refs_10_.refs_11_ = bf16[2400,512]{1,0:T(8,128)(2,1)S(1)} collective-permute-done((bf16[2400,512]{1,0:T(8,128)(2,1)S(1)}, bf16[2400,512]{1,0:T(8,128)(2,1)S(1)}, u32[]{:S(2)}, u32[]{:S(2)}) %collective-permute-start.111) | collective-permute-done | bytes 2457632 | tf_op jit(solution)/shard_map/ppermute | solution.py:105
  524.3 51.7 %collective-permute-done.110.refs_6_.refs_7_.refs_8_ = bf16[2400,512]{1,0:T(8,128)(2,1)S(1)} collective-permute-done((bf16[2400,512]{1,0:T(8,128)(2,1)S(1)}, bf16[2400,512]{1,0:T(8,128)(2,1)S(1)}, u32[]{:S(2)}, u32[]{:S(2)}) %collective-permute-start.110) | collective-permute-done | bytes 2457632 | tf_op jit(solution)/shard_map/ppermute | solution.py:105
  579.2 9.0 %shard_map.298 = (f32[4,704,512]{2,1,0:T(8,128)}, f32[4,704,512]{2,1,0:T(8,128)}, f32[4,704,512]{2,1,0:T(8,128)}) custom-call(s32[1]{0:T(128)} %bitcast.79.at, bf16[2400,512]{1,0:T(8,128)(2,1)S(1)} %constant_dynamic-update-slice_fusion.44.refs_0_.refs_1_.refs_2_, bf16[2400,512]{1,0:T(8,128)(2,1)S(1)} %constant_dynamic-update-slice_fusion.44.refs_0_.refs_1_.refs_2_, ...), custom_call_target="tpu_custom_call" | custom-call | bytes 25952256 | tf_op jit(solution)/shard_map/pallas_call | solution.py:334
  661.5 5.0 collective-permute-done.100
  674.7 14.3 %collective-permute-done.87 = bf16[128,1024]{1,0:T(8,128)(2,1)S(1)} collective-permute-done((bf16[128,1024]{1,0:T(8,128)(2,1)S(1)}, bf16[128,1024]{1,0:T(8,128)(2,1)S(1)}, u32[]{:S(2)}, u32[]{:S(2)}) %collective-permute-start.87) | collective-permute-done | bytes 262176 | tf_op jit(solution)/shard_map/ppermute | solution.py:105
  699.4 8.8 %collective-permute-done.96 = bf16[672,512]{1,0:T(8,128)(2,1)S(1)} collective-permute-done((bf16[672,512]{1,0:T(8,128)(2,1)S(1)}, bf16[672,512]{1,0:T(8,128)(2,1)S(1)}, u32[]{:S(2)}, u32[]{:S(2)}) %collective-permute-start.96) | collective-permute-done | bytes 688160 | tf_op jit(solution)/shard_map/ppermute | solution.py:105
  718.5 18.5 %collective-permute-done.104 = bf16[1216,128]{1,0:T(8,128)(2,1)S(1)} collective-permute-done((bf16[1216,128]{1,0:T(8,128)(2,1)S(1)}, bf16[1216,128]{1,0:T(8,128)(2,1)S(1)}, u32[]{:S(2)}, u32[]{:S(2)}) %collective-permute-start.104) | collective-permute-done | bytes 311328 | tf_op jit(solution)/shard_map/ppermute | solution.py:105
  749.2 7.6 add_convert_fusion
  772.3 9.9 %collective-permute-done.91 = f32[19,4,128]{2,1,0:T(4,128)S(1)} collective-permute-done((f32[19,4,128]{2,1,0:T(4,128)S(1)}, f32[19,4,128]{2,1,0:T(4,128)S(1)}, u32[]{:S(2)}, u32[]{:S(2)}) %collective-permute-start.91) | collective-permute-done | bytes 38944 | tf_op jit(solution)/shard_map/ppermute | solution.py:105
  807.2 6.5 collective-permute-done.65
  814.7 11.3 %collective-permute-done.66 = bf16[128,1024]{1,0:T(8,128)(2,1)S(1)} collective-permute-done((bf16[128,1024]{1,0:T(8,128)(2,1)S(1)}, bf16[128,1024]{1,0:T(8,128)(2,1)S(1)}, u32[]{:S(2)}, u32[]{:S(2)}) %collective-permute-start.66) | collective-permute-done | bytes 262176 | tf_op jit(solution)/shard_map/ppermute | solution.py:105
  (919 shorter events, 423.7 us)
Async XLA Ops:
  2.8 50.6 %collective-permute-start.10 = (bf16[384,512]{1,0:T(8,128)(2,1)}, bf16[384,512]{1,0:T(8,128)(2,1)}, u32[]{:S(2)}, u32[]{:S(2)}) collective-permute-start(bf16[384,512]{1,0:T(8,128)(2,1)} %pad_maximum_fusion.41), channel_id=1, source_target_pairs={{0,8},{8,0},{16,24},{24,16},{1,9},{9,1},{17,25},{25,17},{2,10},{10... | collective-permute-start | bytes 1179656 | tf_op jit(solution)/shard_map/ppermute | solution.py:105
  4.0 47.4 %collective-permute-start.11 = (bf16[384,512]{1,0:T(8,128)(2,1)}, bf16[384,512]{1,0:T(8,128)(2,1)}, u32[]{:S(2)}, u32[]{:S(2)}) collective-permute-start(bf16[384,512]{1,0:T(8,128)(2,1)} %pad_maximum_fusion.41), channel_id=1, source_target_pairs={{0,16},{8,24},{16,0},{24,8},{1,17},{9,25},{17,1},{25,9},{2,18},{10... | collective-permute-start | bytes 1179656 | tf_op jit(solution)/shard_map/ppermute | solution.py:105
  6.2 42.5 %collective-permute-start.14 = (bf16[288,512]{1,0:T(8,128)(2,1)S(1)}, bf16[288,512]{1,0:T(8,128)(2,1)S(1)}, u32[]{:S(2)}, u32[]{:S(2)}) collective-permute-start(bf16[288,512]{1,0:T(8,128)(2,1)S(1)} %dynamic-slice_bitcast_fusion.2), channel_id=1, source_target_pairs={{0,16},{8,24},{16,0},{24,8},{1,17},{9,25},{17,1},{25,9},{2,18},{10... | collective-permute-start | bytes 884744 | tf_op jit(solution)/shard_map/ppermute | solution.py:105
  6.5 43.5 %collective-permute-start.13 = (bf16[288,512]{1,0:T(8,128)(2,1)S(1)}, bf16[288,512]{1,0:T(8,128)(2,1)S(1)}, u32[]{:S(2)}, u32[]{:S(2)}) collective-permute-start(bf16[288,512]{1,0:T(8,128)(2,1)S(1)} %dynamic-slice_bitcast_fusion.2), channel_id=1, source_target_pairs={{0,8},{8,0},{16,24},{24,16},{1,9},{9,1},{17,25},{25,17},{2,10},{10... | collective-permute-start | bytes 884744 | tf_op jit(solution)/shard_map/ppermute | solution.py:105
  8.5 60.5 %collective-permute-start.6 = (bf16[512,384]{1,0:T(8,128)(2,1)}, bf16[512,384]{1,0:T(8,128)(2,1)}, u32[]{:S(2)}, u32[]{:S(2)}) collective-permute-start(bf16[512,384]{1,0:T(8,128)(2,1)} %get-tuple-element.157), channel_id=1, source_target_pairs={{0,8},{8,0},{16,24},{24,16},{1,9},{9,1},{17,25},{25,17},{2,10},{10... | collective-permute-start | bytes 1179656 | tf_op jit(solution)/shard_map/ppermute | solution.py:105
  48.7 26.3 %collective-permute-start.7 = (bf16[512,384]{1,0:T(8,128)(2,1)}, bf16[512,384]{1,0:T(8,128)(2,1)S(1)}, u32[]{:S(2)}, u32[]{:S(2)}) collective-permute-start(bf16[512,384]{1,0:T(8,128)(2,1)} %get-tuple-element.157), channel_id=1, source_target_pairs={{0,16},{8,24},{16,0},{24,8},{1,17},{9,25},{17,1},{25,9},{2,18},{10... | collective-permute-start | bytes 1179656 | tf_op jit(solution)/shard_map/ppermute | solution.py:105
  85.2 45.6 %collective-permute-start.17 = (bf16[288,2048]{1,0:T(8,128)(2,1)}, bf16[288,2048]{1,0:T(8,128)(2,1)}, u32[]{:S(2)}, u32[]{:S(2)}) collective-permute-start(bf16[288,2048]{1,0:T(8,128)(2,1)} %maximum_maximum_fusion.1), channel_id=1, source_target_pairs={{0,1},{1,0},{2,3},{3,2},{4,5},{5,4},{6,7},{7,6},{8,9},{9,8},{10,11... | collective-permute-start | bytes 3538952 | tf_op jit(solution)/shard_map/ppermute | solution.py:105
  120.4 68.7 %collective-permute-start.43 = (bf16[512,1152]{1,0:T(8,128)(2,1)}, bf16[512,1152]{1,0:T(8,128)(2,1)}, u32[]{:S(2)}, u32[]{:S(2)}) collective-permute-start(bf16[512,1152]{1,0:T(8,128)(2,1)} %maximum_maximum_fusion.2), channel_id=1, source_target_pairs={{0,8},{8,0},{16,24},{24,16},{1,9},{9,1},{17,25},{25,17},{2,10},{10... | collective-permute-start | bytes 3538952 | tf_op jit(solution)/shard_map/ppermute | solution.py:105
  120.7 70.4 %collective-permute-start.44 = (bf16[512,1152]{1,0:T(8,128)(2,1)}, bf16[512,1152]{1,0:T(8,128)(2,1)}, u32[]{:S(2)}, u32[]{:S(2)}) collective-permute-start(bf16[512,1152]{1,0:T(8,128)(2,1)} %maximum_maximum_fusion.2), channel_id=1, source_target_pairs={{0,16},{8,24},{16,0},{24,8},{1,17},{9,25},{17,1},{25,9},{2,18},{10... | collective-permute-start | bytes 3538952 | tf_op jit(solution)/shard_map/ppermute | solution.py:105
  217.1 82.9 %collective-permute-start.47 = (bf16[2048,1152]{1,0:T(8,128)(2,1)S(1)}, bf16[2048,1152]{1,0:T(8,128)(2,1)}, u32[]{:S(2)}, u32[]{:S(2)}) collective-permute-start(bf16[2048,1152]{1,0:T(8,128)(2,1)S(1)} %constant_dynamic-update-slice_fusion.29.g_own), channel_id=1, source_target_pairs={{0,1},{1,0},{2,3},{3,2},{4,5},{5,4},{6,7},{7,6},{8,9},{9,8},{10,11... | collective-permute-start | bytes 14155784 | tf_op jit(solution)/shard_map/ppermute | solution.py:105
  240.4 27.0 %collective-permute-start.27 = (bf16[384,1024]{1,0:T(8,128)(2,1)S(1)}, bf16[384,1024]{1,0:T(8,128)(2,1)S(1)}, u32[]{:S(2)}, u32[]{:S(2)}) collective-permute-start(bf16[384,1024]{1,0:T(8,128)(2,1)S(1)} %get-tuple-element.328), channel_id=1, source_target_pairs={{0,8},{8,0},{16,24},{24,16},{1,9},{9,1},{17,25},{25,17},{2,10},{10... | collective-permute-start | bytes 2359304 | tf_op jit(solution)/shard_map/ppermute | solution.py:105
  264.3 33.1 %collective-permute-start.35 = (bf16[384,1024]{1,0:T(8,128)(2,1)S(1)}, bf16[384,1024]{1,0:T(8,128)(2,1)S(1)}, u32[]{:S(2)}, u32[]{:S(2)}) collective-permute-start(bf16[384,1024]{1,0:T(8,128)(2,1)S(1)} %get-tuple-element.328), channel_id=1, source_target_pairs={{0,1},{1,0},{2,3},{3,2},{4,5},{5,4},{6,7},{7,6},{8,9},{9,8},{10,11... | collective-permute-start | bytes 2359304 | tf_op jit(solution)/shard_map/ppermute | solution.py:105
  403.5 29.0 %collective-permute-start.55 = (bf16[192,1024]{1,0:T(8,128)(2,1)S(1)}, bf16[192,1024]{1,0:T(8,128)(2,1)}, u32[]{:S(2)}, u32[]{:S(2)}) collective-permute-start(bf16[192,1024]{1,0:T(8,128)(2,1)S(1)} %get-tuple-element.188), channel_id=1, source_target_pairs={{0,16},{8,24},{16,0},{24,8},{1,17},{9,25},{17,1},{25,9},{2,18},{10... | collective-permute-start | bytes 1179656 | tf_op jit(solution)/shard_map/ppermute | solution.py:105
  467.1 56.0 %collective-permute-start.111 = (bf16[2400,512]{1,0:T(8,128)(2,1)S(1)}, bf16[2400,512]{1,0:T(8,128)(2,1)S(1)}, u32[]{:S(2)}, u32[]{:S(2)}) collective-permute-start(bf16[2400,512]{1,0:T(8,128)(2,1)S(1)} %constant_dynamic-update-slice_fusion.53), channel_id=1, source_target_pairs={{0,24},{8,16},{16,8},{24,0},{1,25},{9,17},{17,9},{25,1},{2,26},{10... | collective-permute-start | bytes 7372808 | tf_op jit(solution)/shard_map/ppermute | solution.py:105
  469.5 106.6 %collective-permute-start.110 = (bf16[2400,512]{1,0:T(8,128)(2,1)S(1)}, bf16[2400,512]{1,0:T(8,128)(2,1)S(1)}, u32[]{:S(2)}, u32[]{:S(2)}) collective-permute-start(bf16[2400,512]{1,0:T(8,128)(2,1)S(1)} %constant_dynamic-update-slice_fusion.50), channel_id=1, source_target_pairs={{0,16},{8,24},{16,0},{24,8},{1,17},{9,25},{17,1},{25,9},{2,18},{10... | collective-permute-start | bytes 7372808 | tf_op jit(solution)/shard_map/ppermute | solution.py:105
  469.5 106.8 %collective-permute-start.109 = (bf16[2400,512]{1,0:T(8,128)(2,1)S(1)}, bf16[2400,512]{1,0:T(8,128)(2,1)S(1)}, u32[]{:S(2)}, u32[]{:S(2)}) collective-permute-start(bf16[2400,512]{1,0:T(8,128)(2,1)S(1)} %constant_dynamic-update-slice_fusion.47), channel_id=1, source_target_pairs={{0,8},{8,0},{16,24},{24,16},{1,9},{9,1},{17,25},{25,17},{2,10},{10... | collective-permute-start | bytes 7372808 | tf_op jit(solution)/shard_map/ppermute | solution.py:105
  495.8 92.4 %collective-permute-start.83 = (bf16[128,1024]{1,0:T(8,128)(2,1)S(1)}, bf16[128,1024]{1,0:T(8,128)(2,1)S(1)}, u32[]{:S(2)}, u32[]{:S(2)}) collective-permute-start(bf16[128,1024]{1,0:T(8,128)(2,1)S(1)} %collective-permute-done.82), channel_id=1, source_target_pairs={{0,1},{1,0},{2,3},{3,2},{4,5},{5,4},{6,7},{7,6},{8,9},{9,8},{10,11... | collective-permute-start | bytes 786440 | tf_op jit(solution)/shard_map/ppermute | solution.py:105
  502.2 87.6 %collective-permute-start.81 = (bf16[128,1024]{1,0:T(8,128)(2,1)S(1)}, bf16[128,1024]{1,0:T(8,128)(2,1)S(1)}, u32[]{:S(2)}, u32[]{:S(2)}) collective-permute-start(bf16[128,1024]{1,0:T(8,128)(2,1)S(1)} %collective-permute-done.80), channel_id=1, source_target_pairs={{0,1},{1,0},{2,3},{3,2},{4,5},{5,4},{6,7},{7,6},{8,9},{9,8},{10,11... | collective-permute-start | bytes 786440 | tf_op jit(solution)/shard_map/ppermute | solution.py:105
  523.1 66.9 %collective-permute-start.79 = (bf16[128,1024]{1,0:T(8,128)(2,1)S(1)}, bf16[128,1024]{1,0:T(8,128)(2,1)S(1)}, u32[]{:S(2)}, u32[]{:S(2)}) collective-permute-start(bf16[128,1024]{1,0:T(8,128)(2,1)S(1)} %collective-permute-done.78), channel_id=1, source_target_pairs={{0,1},{1,0},{2,3},{3,2},{4,5},{5,4},{6,7},{7,6},{8,9},{9,8},{10,11... | collective-permute-start | bytes 786440 | tf_op jit(solution)/shard_map/ppermute | solution.py:105
  577.9 71.5 %collective-permute-start.114 = (bf16[4,288,128]{2,1,0:T(8,128)(2,1)}, bf16[4,288,128]{2,1,0:T(8,128)(2,1)}, u32[]{:S(2)}, u32[]{:S(2)}) collective-permute-start(bf16[4,288,128]{2,1,0:T(8,128)(2,1)} %get-tuple-element.228), channel_id=1, source_target_pairs={{0,6},{2,4},{4,2},{6,0},{1,7},{3,5},{5,3},{7,1},{8,14},{10,12},{12... | collective-permute-start | bytes 884744 | tf_op jit(solution)/shard_map/ppermute | solution.py:105
  578.2 71.9 %collective-permute-start.113 = (bf16[4,288,128]{2,1,0:T(8,128)(2,1)}, bf16[4,288,128]{2,1,0:T(8,128)(2,1)}, u32[]{:S(2)}, u32[]{:S(2)}) collective-permute-start(bf16[4,288,128]{2,1,0:T(8,128)(2,1)} %get-tuple-element.229), channel_id=1, source_target_pairs={{0,4},{2,6},{4,0},{6,2},{1,5},{3,7},{5,1},{7,3},{8,12},{10,14},{12... | collective-permute-start | bytes 884744 | tf_op jit(solution)/shard_map/ppermute | solution.py:105
  588.3 62.7 %collective-permute-start.112 = (bf16[4,288,128]{2,1,0:T(8,128)(2,1)}, bf16[4,288,128]{2,1,0:T(8,128)(2,1)}, u32[]{:S(2)}, u32[]{:S(2)}) collective-permute-start(bf16[4,288,128]{2,1,0:T(8,128)(2,1)} %get-tuple-element.230), channel_id=1, source_target_pairs={{0,2},{2,0},{4,6},{6,4},{1,3},{3,1},{5,7},{7,5},{8,10},{10,8},{12,... | collective-permute-start | bytes 884744 | tf_op jit(solution)/shard_map/ppermute | solution.py:105
  639.9 28.7 %collective-permute-start.84 = (bf16[512,1024]{1,0:T(8,128)(2,1)}, bf16[512,1024]{1,0:T(8,128)(2,1)}, u32[]{:S(2)}, u32[]{:S(2)}) collective-permute-start(bf16[512,1024]{1,0:T(8,128)(2,1)} %add_convert_fusion.3), channel_id=1, source_target_pairs={{0,1},{1,0},{2,3},{3,2},{4,5},{5,4},{6,7},{7,6},{8,9},{9,8},{10,11... | collective-permute-start | bytes 3145736 | tf_op jit(solution)/shard_map/ppermute | solution.py:105
  644.2 28.7 %collective-permute-start.97 = (bf16[672,512]{1,0:T(8,128)(2,1)}, bf16[672,512]{1,0:T(8,128)(2,1)}, u32[]{:S(2)}, u32[]{:S(2)}) collective-permute-start(bf16[672,512]{1,0:T(8,128)(2,1)} %get-tuple-element.173), channel_id=1, source_target_pairs={{0,8},{8,0},{16,24},{24,16},{1,9},{9,1},{17,25},{25,17},{2,10},{10... | collective-permute-start | bytes 2064392 | tf_op jit(solution)/shard_map/ppermute | solution.py:105
  650.1 44.2 %collective-permute-start.99 = (bf16[672,512]{1,0:T(8,128)(2,1)}, bf16[672,512]{1,0:T(8,128)(2,1)}, u32[]{:S(2)}, u32[]{:S(2)}) collective-permute-start(bf16[672,512]{1,0:T(8,128)(2,1)} %pad_maximum_fusion.25), channel_id=1, source_target_pairs={{0,16},{8,24},{16,0},{24,8},{1,17},{9,25},{17,1},{25,9},{2,18},{10... | collective-permute-start | bytes 2064392 | tf_op jit(solution)/shard_map/ppermute | solution.py:105
  667.8 28.6 %collective-permute-start.101 = (bf16[672,512]{1,0:T(8,128)(2,1)S(1)}, bf16[672,512]{1,0:T(8,128)(2,1)S(1)}, u32[]{:S(2)}, u32[]{:S(2)}) collective-permute-start(bf16[672,512]{1,0:T(8,128)(2,1)S(1)} %add_convert_fusion.6), channel_id=1, source_target_pairs={{0,8},{8,0},{16,24},{24,16},{1,9},{9,1},{17,25},{25,17},{2,10},{10... | collective-permute-start | bytes 2064392 | tf_op jit(solution)/shard_map/ppermute | solution.py:105
  689.0 60.2 %collective-permute-start.51 = (bf16[2048,1024]{1,0:T(8,128)(2,1)}, bf16[2048,1024]{1,0:T(8,128)(2,1)}, u32[]{:S(2)}, u32[]{:S(2)}) collective-permute-start(bf16[2048,1024]{1,0:T(8,128)(2,1)} %convolution_convert_fusion.1), channel_id=1, source_target_pairs={{0,1},{1,0},{2,3},{3,2},{4,5},{5,4},{6,7},{7,6},{8,9},{9,8},{10,11... | collective-permute-start | bytes 12582920 | tf_op jit(solution)/shard_map/ppermute | solution.py:105
  694.3 66.0 %collective-permute-start.88 = (f32[128,1024]{1,0:T(8,128)S(1)}, f32[128,1024]{1,0:T(8,128)}, u32[]{:S(2)}, u32[]{:S(2)}) collective-permute-start(f32[128,1024]{1,0:T(8,128)S(1)} %convert_add_fusion.1), channel_id=1, source_target_pairs={{0,1},{1,0},{2,3},{3,2},{4,5},{5,4},{6,7},{7,6},{8,9},{9,8},{10,11... | collective-permute-start | bytes 1572872 | tf_op jit(solution)/shard_map/ppermute | solution.py:105
  714.5 28.1 %collective-permute-start.103 = (bf16[1216,128]{1,0:T(8,128)(2,1)S(1)}, bf16[1216,128]{1,0:T(8,128)(2,1)S(1)}, u32[]{:S(2)}, u32[]{:S(2)}) collective-permute-start(bf16[1216,128]{1,0:T(8,128)(2,1)S(1)} %get-tuple-element.214), channel_id=1, source_target_pairs={{0,4},{2,6},{4,0},{6,2},{1,5},{3,7},{5,1},{7,3},{8,12},{10,14},{12... | collective-permute-start | bytes 933896 | tf_op jit(solution)/shard_map/ppermute | solution.py:105
  758.9 28.5 %collective-permute-start.61 = (bf16[256,1024]{1,0:T(8,128)(2,1)}, bf16[256,1024]{1,0:T(8,128)(2,1)S(1)}, u32[]{:S(2)}, u32[]{:S(2)}) collective-permute-start(bf16[256,1024]{1,0:T(8,128)(2,1)} %get-tuple-element.180), channel_id=1, source_target_pairs={{0,8},{8,0},{16,24},{24,16},{1,9},{9,1},{17,25},{25,17},{2,10},{10... | collective-permute-start | bytes 1572872 | tf_op jit(solution)/shard_map/ppermute | solution.py:105
  759.7 28.1 %collective-permute-start.59 = (bf16[256,1024]{1,0:T(8,128)(2,1)}, bf16[256,1024]{1,0:T(8,128)(2,1)}, u32[]{:S(2)}, u32[]{:S(2)}) collective-permute-start(bf16[256,1024]{1,0:T(8,128)(2,1)} %get-tuple-element.182), channel_id=1, source_target_pairs={{0,16},{8,24},{16,0},{24,8},{1,17},{9,25},{17,1},{25,9},{2,18},{10... | collective-permute-start | bytes 1572872 | tf_op jit(solution)/shard_map/ppermute | solution.py:105
  783.0 44.6 %collective-permute-start.105 = (f32[576,128]{1,0:T(8,128)S(1)}, f32[576,128]{1,0:T(8,128)S(1)}, u32[]{:S(2)}, u32[]{:S(2)}) collective-permute-start(f32[576,128]{1,0:T(8,128)S(1)} %convert_add_fusion.4), channel_id=1, source_target_pairs={{0,1},{1,0},{2,3},{3,2},{4,5},{5,4},{6,7},{7,6},{8,9},{9,8},{10,11... | collective-permute-start | bytes 884744 | tf_op jit(solution)/shard_map/ppermute | solution.py:105
  (265 other events, 3025.4 us)

commit v2 on v1

v2 whole, which is shorter than its diff:
```python
import functools

import jax
import jax.numpy as jnp
from jax import lax
from jax.experimental import pallas as pl
from jax.experimental.pallas import tpu as pltpu
from jax.sharding import PartitionSpec as P

D = 2048
DN = 128
DR = 64
DV = 128
R = 512
EXPERTS = 16
NB = 4
NL = 2
LANES = 128

epsilon = 1e-06
masked_score = -1e30
bf16 = jnp.bfloat16
f32 = jnp.float32


def mm(left, right):
    return jnp.dot(left, right, preferred_element_type=f32)


def mm_nt(left, right):
    return lax.dot_general(left, right, (((1,), (1,)), ((), ())), preferred_element_type=f32)


def mm_tn(left, right):
    return lax.dot_general(left, right, (((0,), (0,)), ((), ())), preferred_element_type=f32)


def rms_stats(values):
    return lax.rsqrt(jnp.mean(values * values, axis=-1, keepdims=True) + epsilon)


def rms_back(grad_normed, unit_rows, inverse):
    return inverse * (
        grad_normed - unit_rows * jnp.mean(grad_normed * unit_rows, axis=-1, keepdims=True)
    )


def rotate(values, cosine, sine):
    half_width = values.shape[-1] // 2
    first_half = values[..., :half_width]
    second_half = values[..., half_width:]
    return jnp.concatenate(
        [first_half * cosine - second_half * sine, second_half * cosine + first_half * sine],
        axis=-1,
    )


def rotate_back(grads_in, cosine, sine):
    half_width = grads_in.shape[-1] // 2
    first_half = grads_in[..., :half_width]
    second_half = grads_in[..., half_width:]
    return jnp.concatenate(
        [first_half * cosine + second_half * sine, second_half * cosine - first_half * sine],
        axis=-1,
    )


def tree_layout(leaf_parent, token_index, trunk_len, seg_len):
    beyond = token_index - trunk_len
    in_trunk = token_index < trunk_len
    in_branch = (beyond >= 0) & (beyond < NB * seg_len)
    in_leaf = beyond >= NB * seg_len
    leaf_offset = beyond - NB * seg_len
    leaf_index = jnp.clip(leaf_offset // seg_len, 0, NB * NL - 1)
    position = jnp.where(
        in_trunk,
        token_index,
        jnp.where(
            in_branch, trunk_len + beyond % seg_len, trunk_len + seg_len + leaf_offset % seg_len
        ),
    )
    segment = jnp.where(
        in_trunk, 0, jnp.where(in_branch, 1 + beyond // seg_len, 1 + NB + leaf_index)
    )
    leaf_match = (leaf_index[:, None] == jnp.arange(NB * NL, dtype=jnp.int32)[None, :]).astype(
        jnp.int32
    )
    branch_of_leaf = 1 + jnp.sum(leaf_match * leaf_parent[None, :], axis=1)
    parent = jnp.where(in_trunk, -1, jnp.where(in_branch, 0, branch_of_leaf))
    grand = jnp.where(in_leaf, 0, -1)
    return (position, segment, parent, grand.astype(jnp.int32))


def visible(query_segment, query_parent, query_grand, query_index, key_segment, key_index):
    same_segment = (query_segment[:, None] == key_segment[None, :]) & (
        key_index[None, :] <= query_index[:, None]
    )
    ancestor = (key_segment[None, :] == query_parent[:, None]) | (
        key_segment[None, :] == query_grand[:, None]
    )
    return same_segment | ancestor


def swap(values, axis, step):
    return lax.ppermute(values, axis, [(k, k ^ step) for k in range(lax.axis_size(axis))])


def gather_rel(values, axis):
    size = lax.axis_size(axis)
    if size <= 4:
        return [values] + [swap(values, axis, s) for s in range(1, size)]
    full = lax.all_gather(values, axis)
    me = lax.axis_index(axis)
    return [lax.dynamic_index_in_dim(full, me ^ s, 0, False) for s in range(size)]


def exchange_rel(pieces, axis, stride=1):
    size = lax.axis_size(axis)
    if size <= 4:
        return [pieces[0]] + [swap(p, axis, k * stride) for k, p in enumerate(pieces) if k]
    me = lax.axis_index(axis)
    zero = jnp.zeros_like(pieces[0])
    full = jnp.stack([pieces[s // stride] if s % stride == 0 else zero for s in range(size)])
    order = me ^ jnp.arange(size)
    sent = lax.all_to_all(jnp.take(full, order, axis=0), axis, 0, 0, tiled=True)
    back = jnp.take(sent, order, axis=0)
    return [back[k * stride] for k in range(len(pieces))]


def canonical(pieces, me):
    stacked = jnp.stack(pieces)
    return [lax.dynamic_index_in_dim(stacked, me ^ c, 0, False) for c in range(len(pieces))]


def permute_blocks(values, me, count):
    width = values.shape[-1] // count
    return jnp.concatenate(
        [
            lax.dynamic_slice_in_dim(values, (me ^ s) * width, width, values.ndim - 1)
            for s in range(count)
        ],
        axis=-1,
    )


def total(pieces):
    result = pieces[0].astype(f32)
    for piece in pieces[1:]:
        result = result + piece.astype(f32)
    return result


def halves(own, other, core, dim):
    return jnp.where(
        core == 0,
        jnp.concatenate([own, other], axis=dim),
        jnp.concatenate([other, own], axis=dim),
    )


def pick_half(values, which, dim):
    width = values.shape[dim] // 2
    return lax.dynamic_slice_in_dim(values, which * width, width, dim)


def gather_shared(values, axis, core, dim):
    mine = gather_rel(pick_half(values, core, dim), axis)
    return [values] + [halves(p, swap(p, "tensor", 1), core, dim) for p in mine[1:]]


def keep_kernel(*refs):
    pass


def order(values, others):
    count, total_count = len(values), len(values) + len(others)
    anywhere = pl.BlockSpec(memory_space=pl.ANY)
    return pl.pallas_call(
        keep_kernel,
        in_specs=[anywhere] * total_count,
        out_specs=[anywhere] * count,
        out_shape=[jax.ShapeDtypeStruct(v.shape, v.dtype) for v in values],
        input_output_aliases={k: k for k in range(count)},
        cost_estimate=pl.CostEstimate(flops=0, bytes_accessed=0, transcendentals=0),
    )(*values, *others)


def place_rows(parts, rows, others=()):
    spans = [p[5] if len(p) > 5 else (0, p[0].shape[1]) for p in parts]
    columns = max(part[4] + span[1] for part, span in zip(parts, spans))

    def body(*refs):
        out, sems = refs[-2], refs[-1]
        copies = []
        for k, part in enumerate(parts):
            source = refs[k].at[pl.ds(part[1], part[2]), pl.ds(*spans[k])]
            target = out.at[pl.ds(part[3], part[2]), pl.ds(part[4], spans[k][1])]
            copies.append(pltpu.make_async_copy(source, target, sems.at[k]))
        for copy in copies:
            copy.start()
        for copy in copies:
            copy.wait()

    anywhere = pl.BlockSpec(memory_space=pl.ANY)
    return pl.pallas_call(
        body,
        in_specs=[anywhere] * (len(parts) + len(others)),
        out_specs=pl.BlockSpec(memory_space=pltpu.VMEM),
        out_shape=jax.ShapeDtypeStruct((rows, columns), parts[0][0].dtype),
        scratch_shapes=[pltpu.SemaphoreType.DMA((len(parts),))],
        compiler_params=pltpu.CompilerParams(vmem_limit_bytes=48 * 1024 * 1024),
        cost_estimate=pl.CostEstimate(flops=0, bytes_accessed=0, transcendentals=0),
    )(*[part[0] for part in parts], *others)


def pack_kernel(at, query, latent, up, out_w, packed):
    turned = query[...].T
    rows = DN + DR
    packed[0:DN] = turned[:DN]
    packed[DN : 2 * DN] = turned[rows : rows + DN]
    packed[2 * DN : 2 * DN + DR] = turned[DN:rows]
    packed[2 * DN + DR : 2 * rows] = turned[rows + DN :]
    first = 2 * rows
    for ref in (latent, up, out_w):
        packed[first : first + ref.shape[0]] = ref[...]
        first += ref.shape[0]


def pack_call(at, query_proj, latent_t, latent_up, output_proj, wide):
    block = query_proj.shape[0]
    qw, uw = 2 * (DN + DR), 2 * (DN + DV)
    sizes = [qw, latent_t.shape[0] // 2, latent_up.shape[0], 2 * DV]
    return pl.pallas_call(
        pack_kernel,
        grid_spec=pltpu.PrefetchScalarGridSpec(
            num_scalar_prefetch=1,
            grid=(1,),
            in_specs=[
                pl.BlockSpec((block, qw), lambda m, at: (0, at[0])),
                pl.BlockSpec((sizes[1], block), lambda m, at: (at[1], 0)),
                pl.BlockSpec((sizes[2], uw), lambda m, at: (0, at[0])),
                pl.BlockSpec((sizes[3], block), lambda m, at: (at[0], 0)),
            ],
            out_specs=pl.BlockSpec((sum(sizes), block), lambda m, at: (0, 0)),
        ),
        out_shape=jax.ShapeDtypeStruct((sum(sizes), block), bf16),
        compiler_params=pltpu.CompilerParams(vmem_limit_bytes=24 * 1024 * 1024),
        cost_estimate=pl.CostEstimate(flops=0, bytes_accessed=0, transcendentals=0),
    )(at, query_proj, latent_t, latent_up, output_proj)


def join_rows(arrays, others=()):
    parts, at = [], 0
    for array in arrays:
        parts.append((array, 0, array.shape[0], at, 0))
        at += array.shape[0]
    return place_rows(parts, at, others)


def gather_parts(values, between=None):
    if lax.axis_size("dp") != 4:
        return [[p] for p in gather_rel(values, "dp")]
    cut = values.shape[0] // 2
    first, second = swap(values, "dp", 1), swap(values, "dp", 2)
    low, high = first[:cut], second[cut:]
    if between is not None:
        low, high = order([low, high], between)
    return [[values], [first], [second], [swap(low, "dp", 2), swap(high, "dp", 1)]]


def gather_dp(values, between=None):
    return [p[0] if len(p) == 1 else join_rows(p) for p in gather_parts(values, between)]


def stack_kernel(*refs):
    at = 0
    for ref in refs[:-1]:
        refs[-1][at : at + ref.shape[0]] = ref[...].astype(bf16)
        at += ref.shape[0]


def stack_rows(parts, block):
    rows, columns = sum(p.shape[0] for p in parts), parts[0].shape[1]
    made = pl.pallas_call(
        stack_kernel,
        grid=(columns // block,),
        in_specs=[pl.BlockSpec((p.shape[0], block), lambda c: (0, c)) for p in parts],
        out_specs=pl.BlockSpec((rows, block), lambda c: (c, 0)),
        out_shape=jax.ShapeDtypeStruct((rows * (columns // block), block), bf16),
        compiler_params=pltpu.CompilerParams(vmem_limit_bytes=32 * 1024 * 1024),
        cost_estimate=pl.CostEstimate(flops=0, bytes_accessed=8 * rows * columns, transcendentals=0),
    )(*parts)
    return [made[c * rows : (c + 1) * rows] for c in range(columns // block)]


def reduce_first(pieces):
    cut = pieces[0].shape[0] // 2
    low, high = [p[:cut] for p in pieces], [p[cut:] for p in pieces]
    low_got = swap(jnp.concatenate([low[1], low[3]], axis=0), "dp", 1)
    high_got = swap(jnp.concatenate([high[2], high[3]], axis=0), "dp", 2)
    return low, high, low_got, high_got


def reduce_second(state, between=None):
    low, high, low_got, high_got = state
    cut = low[0].shape[0]
    low_sum = (low[2].astype(f32) + low_got[cut:].astype(f32)).astype(bf16)
    high_sum = (high[1].astype(f32) + high_got[cut:].astype(f32)).astype(bf16)
    if between is not None:
        low_sum, high_sum = order([low_sum, high_sum], between)
    low_next, high_next = swap(low_sum, "dp", 2), swap(high_sum, "dp", 1)
    return jnp.concatenate(
        [
            total([low[0], low_got[:cut], low_next]).astype(bf16),
            total([high[0], high_got[:cut], high_next]).astype(bf16),
        ],
        axis=0,
    )


def gather_z(own_half):
    return jnp.concatenate(gather_rel(own_half, "expert")[1:], axis=0)


def along_z(others, own):
    tok = own.shape[0]
    count = others.shape[0] // tok
    pieces = [own] + [others[s * tok : (s + 1) * tok] for s in range(count)]
    return total(exchange_rel(pieces, "expert"))


def rows_join(own, other, core):
    rows = own.shape[0]
    result = jnp.zeros((2 * rows,) + own.shape[1:], own.dtype)
    result = lax.dynamic_update_slice_in_dim(result, own, core * rows, 0)
    return lax.dynamic_update_slice_in_dim(result, other, (1 - core) * rows, 0)


def feed_kernel(sh_width, width, padded, sub, at, n_own, n_oth, g_own, g_oth, gate_hbm, up_hbm, down_hbm,
                shared_hbm, *refs):
    hid_out, back_out, rows_own, rows_oth, out_own, out_oth, pre_w, down_w, sems = refs[-9:]
    half = n_own.shape[1]

    @pl.when(pl.program_id(0) == 0)
    def _():
        pick, core = at[0], at[1]
        copies = []
        for k in range(2):
            here = pl.multiple_of((core if k == 0 else 1 - core) * half, LANES)
            cols, to = pl.ds(here, half), pl.ds(k * half, half)
            moves = [
                (gate_hbm.at[pick, :, cols], pre_w.at[pl.ds(LANES, width), to]),
                (up_hbm.at[pick, :, cols], pre_w.at[pl.ds(padded + LANES, width), to]),
                (down_hbm.at[pick, :, cols], down_w.at[pl.ds(LANES, width), to]),
                (shared_hbm.at[pl.ds(0, LANES), cols], pre_w.at[pl.ds(0, LANES), to]),
                (shared_hbm.at[pl.ds(LANES, LANES), cols], pre_w.at[pl.ds(padded, LANES), to]),
                (shared_hbm.at[pl.ds(2 * LANES, LANES), cols], down_w.at[pl.ds(0, LANES), to]),
            ]
            for m, (source, target) in enumerate(moves):
                copies.append(pltpu.make_async_copy(source, target, sems.at[6 * k + m]))
        for copy in copies:
            copy.start()
        room = padded - LANES - width
        if room:
            zeros = jnp.zeros((room, 2 * half), bf16)
            pre_w[pl.ds(LANES + width, room), :] = zeros
            pre_w[pl.ds(padded + LANES + width, room), :] = zeros
            down_w[pl.ds(LANES + width, room), :] = zeros
        for copy in copies:
            copy.wait()

    lane = lax.broadcasted_iota(jnp.int32, (sub, LANES), 1)
    is_router = (lane >= sh_width) & (lane < sh_width + EXPERTS)
    is_own = lane == at[2]

    def activate(pre, up, back):
        sigmoid = 1.0 / (1.0 + jnp.exp(-pre))
        silu = pre * sigmoid
        slope = sigmoid + silu * (1.0 - sigmoid)
        return silu * up, back * up * slope, back * silu

    for start in range(0, n_own.shape[0], sub):
        rows = slice(start, start + sub)
        pre = mm_nt(n_own[rows], pre_w[:, :half]) + mm_nt(n_oth[rows], pre_w[:, half:])
        back = mm_nt(g_own[rows, :half], down_w[:, :half])
        back = back + mm_nt(g_oth[rows, :half], down_w[:, half:])
        gate_pre, up_pre = pre[:, :padded], pre[:, padded:]
        logits = jnp.where(is_router, up_pre[:, :LANES], masked_score)
        exps = jnp.exp(logits - jnp.max(logits, axis=1, keepdims=True))
        probs = exps / jnp.sum(exps, axis=1, keepdims=True)
        prob_own = jnp.sum(jnp.where(is_own, probs, 0.0), axis=1, keepdims=True)
        mask = g_own[rows, half:].astype(f32)
        routed = jnp.sum(jnp.where(is_own, mask, 0.0), axis=1, keepdims=True)
        gate = routed * prob_own
        hid_s, gg_s, gu_s = activate(gate_pre[:, :LANES], up_pre[:, :LANES], back[:, :LANES])
        hid, gg, gu = activate(gate_pre[:, LANES:], up_pre[:, LANES:], back[:, LANES:])
        prob_grad = routed * jnp.sum(hid * back[:, LANES:], axis=1, keepdims=True)
        logit_grad = probs * (jnp.where(is_own, prob_grad, 0.0) - prob_own * prob_grad)
        hid_out[rows, :LANES] = hid_s.astype(bf16)
        hid_out[rows, LANES:] = (hid * gate).astype(bf16)
        back_out[rows, :LANES] = gg_s.astype(bf16)
        back_out[rows, LANES:padded] = (gg * gate).astype(bf16)
        back_out[rows, padded : padded + LANES] = jnp.where(is_router, logit_grad, gu_s).astype(bf16)
        back_out[rows, padded + LANES :] = (gu * gate).astype(bf16)
        rows_oth[rows] = mm(back_out[rows], pre_w[:, half:]).astype(bf16)
        rows_own[rows] = mm(back_out[rows], pre_w[:, :half]).astype(bf16)
        out_oth[rows] = mm(hid_out[rows], down_w[:, half:]).astype(bf16)
        out_own[rows] = mm(hid_out[rows], down_w[:, :half]).astype(bf16)


def feed_call(at, sh_width, width, padded, rows_own, rows_other, grad_own, grad_other, weights, place, kept, others):
    tokens, half = rows_own.shape
    tile, sub = 256, 256
    by_rows = lambda m, at: (m, 0)
    first, every = place[0] // tile, place[1]
    placed_rows = lambda m, at: (m + first, 0)
    acts = [rows_own, rows_other, grad_own, grad_other]
    widths = [padded, 2 * padded, half, half, half, half]
    return pl.pallas_call(
        functools.partial(feed_kernel, sh_width, width, padded, sub),
        grid_spec=pltpu.PrefetchScalarGridSpec(
            num_scalar_prefetch=1,
            grid=(tokens // tile,),
            in_specs=[pl.BlockSpec((tile, a.shape[1]), by_rows) for a in acts]
            + [pl.BlockSpec(memory_space=pl.ANY) for w in weights + kept + others],
            out_specs=[
                pl.BlockSpec((tile, w), placed_rows if k < 2 else by_rows)
                for k, w in enumerate(widths)
            ],
            scratch_shapes=[
                pltpu.VMEM((2 * padded, 2 * half), bf16),
                pltpu.VMEM((padded, 2 * half), bf16),
                pltpu.SemaphoreType.DMA((12,)),
            ],
        ),
        out_shape=[
            jax.ShapeDtypeStruct((every if k < 2 else tokens, w), bf16)
            for k, w in enumerate(widths)
        ],
        input_output_aliases={9 + k: k for k in range(len(kept))},
        compiler_params=pltpu.CompilerParams(
            dimension_semantics=("arbitrary",), vmem_limit_bytes=58 * 1024 * 1024
        ),
        cost_estimate=pl.CostEstimate(
            flops=24 * tokens * half * padded,
            bytes_accessed=2 * tokens * (8 * half + 3 * padded) + 12 * half * padded,
            transcendentals=tokens * padded,
        ),
    )(at, *acts, *weights, *kept, *others)


def swap_quarters(values):
    lane = lax.broadcasted_iota(jnp.int32, values.shape, 1)
    return jnp.where(lane % 64 < 32, pltpu.roll(values, 96, 1), pltpu.roll(values, 32, 1))


def assemble(at, sources, x, wq, wl, up, wo, sems):
    x_rel, x_got, x_there, wl_there = sources[0], sources[1:4], sources[4:7], sources[7]
    pieces = [[sources[8]], [sources[9]], [sources[10]], list(sources[11:])]
    core, index = at[0], at[1]
    block = sources[8].shape[1]
    half, own, wl_rows = D // 2, x_rel.shape[0], wl_there.shape[0]
    up_rows = R // 4
    copies = []

    def copy(source, target):
        copies.append(pltpu.make_async_copy(source, target, sems.at[len(copies)]))

    def columns(which):
        return pl.ds(pl.multiple_of(which * half, LANES), half)

    def rows(first, unit, count):
        return pl.ds(pl.multiple_of(first * unit, 16), count)

    copy(x_rel, x.at[pl.ds(0, own)])
    for k in range(3):
        to = pl.ds((k + 1) * own, own)
        copy(x_got[k].at[:, pl.ds(0, half)], x.at[to, columns(core)])
        copy(x_there[k].at[:, pl.ds(0, half)], x.at[to, columns(1 - core)])
    copy(wl_there, wl.at[rows(1 - core, wl_rows, wl_rows)])
    fields = [wq.shape[0], wl_rows, up_rows, 0 if wo is None else wo.shape[0]]
    for s, parts in enumerate(pieces):
        base = 0
        for part in parts:
            start = 0
            for f, size in enumerate(fields):
                first, last = max(start, base), min(start + size, base + part.shape[0])
                if first < last:
                    source = part.at[pl.ds(first - base, last - first)]
                    off, count = first - start, last - first
                    to = pl.ds(s * block, block)
                    if f == 0:
                        copy(source, wq.at[pl.ds(off, count), to])
                    elif f == 1:
                        here = pl.multiple_of(core * wl_rows + off, 16)
                        copy(source, wl.at[pl.ds(here, count), to])
                    elif f == 2:
                        here = pl.multiple_of((index ^ s) * up_rows + off, 16)
                        copy(source, up.at[pl.ds(here, count)])
                    else:
                        copy(source, wo.at[pl.ds(off, count), to])
                start += size
            base += part.shape[0]
    for one in copies:
        one.start()
    for one in copies:
        one.wait()


def attend_kernel(at, *refs):
    sources, refs = refs[:13], refs[13:]
    (gain, cos, sin, mask, latent_gain, part_own, part_oth, normed_out, keys_out, queries_out, nope_out,
     probs_out, mixed_out, heads_out, unit_out, inverse_out, x, wq, wl, up, wo, sems) = refs
    assemble(at, sources, x, wq, wl, up, wo, sems)
    rows = x[...].astype(f32)
    normed = (rows * rms_stats(rows) * gain[...]).astype(bf16)
    normed_out[...] = normed
    query = mm_nt(normed, wq[...])
    latent_all = mm_nt(normed, wl[:R])
    inverse = rms_stats(latent_all)
    unit = latent_all * inverse
    unit_out[...] = unit
    inverse_out[...] = jnp.broadcast_to(inverse, inverse_out.shape)
    latent = (unit * latent_gain[...]).astype(bf16)
    key_rope = mm_nt(normed, jnp.concatenate([wl[R:], wl[R:]], axis=0))
    keys_out[:, :R] = latent
    keys_out[:, R:] = (key_rope * cos[...] + swap_quarters(key_rope) * sin[...]).astype(bf16)
    ropes = query[:, 2 * DN :]
    ropes = (ropes * cos[...] + swap_quarters(ropes) * sin[...]).astype(bf16)
    lane = lax.broadcasted_iota(jnp.int32, ropes.shape, 1)
    keys = keys_out[...]
    allowed = mask[...] > 0
    for h in range(2):
        nope = query[:, h * DN : (h + 1) * DN].astype(bf16)
        nope_out[:, h * DN : (h + 1) * DN] = nope
        queries_out[h, :, :R] = mm_nt(nope, up[:, h * (DN + DV) : h * (DN + DV) + DN]).astype(bf16)
        queries_out[h, :, R:] = jnp.where(lane // 64 == h, ropes, jnp.zeros_like(ropes))
        scores = mm_nt(queries_out[h], keys) * (DN + DR) ** (-0.5)
        scores = jnp.where(allowed, scores, masked_score)
        exps = jnp.exp(scores - jnp.max(scores, axis=1, keepdims=True))
        probs = exps / jnp.sum(exps, axis=1, keepdims=True)
        probs_out[h] = probs
        mixed = mm(probs.astype(bf16), latent).astype(bf16)
        mixed_out[h] = mixed
        heads_out[:, h * DV : (h + 1) * DV] = mm(
            mixed, up[:, h * (DN + DV) + DN : (h + 1) * (DN + DV)]
        ).astype(bf16)
    half = part_own.shape[1]
    part = mm(heads_out[...], wo[...]).astype(bf16)
    first = at[0] == 0
    part_own[...] = jnp.where(first, part[:, :half], part[:, half:])
    part_oth[...] = jnp.where(first, part[:, half:], part[:, :half])


def attend_back_kernel(at, *refs):
    sources, refs = refs[:13], refs[13:]
    (res, normed, cos, sin, latent_gain, keys, queries, nope, probs, mixed, heads, unit, inverse,
     back_own, back_oth, grad_wo, grad_wq, grad_wl, grad_wl_oth, grad_up, grad_gain, grad_latent_gain,
     gl_ref, gq_ref, gk_ref, x, wq, wl, up, wo, sems) = refs
    assemble(at, sources, x, wq, wl, up, wo, sems)
    res_rows = res[...]
    grad_wo[...] = mm_tn(heads[...], res_rows).astype(bf16)
    grad_heads = mm_nt(res_rows, wo[...]).astype(bf16)
    latent = keys[:, :R]
    lane = lax.broadcasted_iota(jnp.int32, cos.shape, 1)
    grad_ropes = jnp.zeros(cos.shape, f32)
    uw = DN + DV
    for h in range(2):
        grad_head = grad_heads[:, h * DV : (h + 1) * DV]
        up_key = up[:, h * uw : h * uw + DN]
        grad_mixed = mm_nt(grad_head, up[:, h * uw + DN : (h + 1) * uw]).astype(bf16)
        prob = probs[h]
        grad_att = mm_nt(grad_mixed, latent)
        delta = jnp.sum(prob * grad_att, axis=1, keepdims=True)
        score_grad = (prob * (grad_att - delta) * (DN + DR) ** (-0.5)).astype(bf16)
        grad_query = mm(score_grad, keys[...])
        grad_keys = mm_tn(score_grad, queries[h])
        grad_latent = grad_keys[:, :R] + mm_tn(prob.astype(bf16), grad_mixed)
        if h == 0:
            gk_ref[:, :R] = grad_latent
            gk_ref[:, R:] = grad_keys[:, R:]
        else:
            gk_ref[:, :R] += grad_latent
            gk_ref[:, R:] += grad_keys[:, R:]
        grad_ropes = grad_ropes + jnp.where(lane // 64 == h, grad_query[:, R:], 0.0)
        grad_ql = grad_query[:, :R].astype(bf16)
        gq_ref[:, h * DN : (h + 1) * DN] = mm(grad_ql, up_key).astype(bf16)
        grad_up[h * uw : h * uw + DN] = mm_tn(nope[:, h * DN : (h + 1) * DN], grad_ql).astype(bf16)
        grad_up[h * uw + DN : (h + 1) * uw] = mm_tn(grad_head, mixed[h]).astype(bf16)
    gq_ref[:, 2 * DN :] = (grad_ropes * cos[...] - swap_quarters(grad_ropes) * sin[...]).astype(bf16)
    grad_latent = gk_ref[:, :R]
    grad_latent_gain[...] = jnp.sum(grad_latent * unit[...], axis=0, keepdims=True)
    gl_ref[:, :R] = rms_back(grad_latent * latent_gain[...], unit[...], inverse[:, :1]).astype(bf16)
    key_ropes = gk_ref[:, R:]
    key_ropes = key_ropes + pltpu.roll(key_ropes, 64, 1)
    key_ropes = key_ropes * cos[...] - swap_quarters(key_ropes) * sin[...]
    gl_ref[:, R:] = key_ropes.astype(bf16)
    back = mm(gq_ref[...], wq[...]) + mm(gl_ref[:, :R], wl[:R]) + mm(gl_ref[:, R : R + DR], wl[R:])
    tree_rows = x[...].astype(f32)
    unit_rows = tree_rows * rms_stats(tree_rows)
    grad_gain[...] = jnp.sum(back * unit_rows, axis=0, keepdims=True)
    half = back_own.shape[1]
    back = back.astype(bf16)
    first = at[0] == 0
    back_own[...] = jnp.where(first, back[:, :half], back[:, half:])
    back_oth[...] = jnp.where(first, back[:, half:], back[:, :half])
    rows = normed[...]
    grad_wq[...] = mm_tn(gq_ref[...], rows).astype(bf16)
    cut = grad_wl.shape[0]
    low = mm_tn(gl_ref[:, : 3 * LANES], rows).astype(bf16)
    high = mm_tn(gl_ref[:, 2 * LANES :], rows).astype(bf16)
    low, high = low[:cut], high[cut - 2 * LANES : 2 * cut - 2 * LANES]
    grad_wl[...] = jnp.where(first, low, high)
    grad_wl_oth[...] = jnp.where(first, high, low)


def whole_call(kernel, sources, operands, outs, scratch, at, tree_len, wq_rows, wo_rows):
    scratch = scratch + [
        pltpu.VMEM((tree_len, D), bf16),
        pltpu.VMEM((wq_rows, D), bf16),
        pltpu.VMEM((R + DR, D), bf16),
        pltpu.VMEM((R, R), bf16),
        pltpu.VMEM((wo_rows, D), bf16),
        pltpu.SemaphoreType.DMA((32,)),
    ]
    return pl.pallas_call(
        kernel,
        in_specs=[pl.BlockSpec(memory_space=pltpu.SMEM)]
        + [pl.BlockSpec(memory_space=pl.ANY)] * len(sources)
        + [pl.BlockSpec(memory_space=pltpu.VMEM)] * len(operands),
        out_specs=[pl.BlockSpec(memory_space=pltpu.VMEM)] * len(outs),
        out_shape=[jax.ShapeDtypeStruct(shape, kind) for shape, kind in outs],
        scratch_shapes=scratch,
        compiler_params=pltpu.CompilerParams(vmem_limit_bytes=58 * 1024 * 1024),
        cost_estimate=pl.CostEstimate(flops=0, bytes_accessed=0, transcendentals=0),
    )(at, *sources, *operands)


def weight_kernel(segments, at, lefts, owns, others, out):
    c = pl.program_id(0)
    mine = (c // (pl.num_programs(0) // 2)) == at[0]

    def run(rights):
        to = 0
        for start, rows in segments:
            result = jnp.zeros((rows, out.shape[1]), f32)
            first = 0
            for right in rights:
                deep = right.shape[0]
                result = result + mm_tn(lefts[first : first + deep, start : start + rows], right[...])
                first += deep
            out[to : to + rows] = result.astype(bf16)
            to += rows

    @pl.when(mine)
    def _():
        run(owns)

    @pl.when(jnp.logical_not(mine))
    def _():
        run(others)


def weight_call(core, left, owns, others, segments, count):
    block = D // count
    rows = sum(size for first, size in segments)
    per_half = count // 2

    def body(at, *refs):
        parts = len(owns)
        weight_kernel(segments, at, refs[0], refs[1 : 1 + parts], refs[1 + parts : -1], refs[-1])

    columns = lambda c, at: (0, c % per_half)
    return pl.pallas_call(
        body,
        grid_spec=pltpu.PrefetchScalarGridSpec(
            num_scalar_prefetch=1,
            grid=(count,),
            in_specs=[pl.BlockSpec(left.shape, lambda c, at: (0, 0), pipeline_mode=pl.Buffered(1))]
            + [pl.BlockSpec((r.shape[0], block), columns) for r in owns + others],
            out_specs=pl.BlockSpec((rows, block), lambda c, at: (c, 0)),
        ),
        out_shape=jax.ShapeDtypeStruct((count * rows, block), bf16),
        compiler_params=pltpu.CompilerParams(
            dimension_semantics=("arbitrary",), vmem_limit_bytes=58 * 1024 * 1024
        ),
        cost_estimate=pl.CostEstimate(flops=0, bytes_accessed=0, transcendentals=0),
    )(jnp.reshape(core, (1,)).astype(jnp.int32), left, *owns, *others)


def per_device(
    layer_in,
    norm_gain,
    query_proj,
    latent_proj,
    latent_gain,
    latent_up,
    output_proj,
    ffn_gain,
    router,
    shared_gate,
    shared_up,
    shared_down,
    expert_gate,
    expert_up,
    expert_down,
    routes,
    leaf_parent,
    grad_out,
):
    tok = layer_in.shape[0]
    n_dp, n_ex = lax.axis_size("dp"), lax.axis_size("expert")
    i, j, core = lax.axis_index("dp"), lax.axis_index("expert"), lax.axis_index("tensor")
    tree_len = tok * n_ex
    seg_len = tree_len // 16
    trunk_len = 4 * seg_len
    block = D // n_dp
    sub = block // n_ex
    heads_local = output_proj.shape[0] // DV
    groups = min(n_ex, heads_local)
    hp = heads_local // groups
    qg = n_ex // groups
    group = j // qg
    n_q = n_ex // qg
    rows_q = tok * n_q
    qw = DN + DR
    uw = DN + DV
    score_scale = (DN + DR) ** (-0.5)

    x_rel = permute_blocks(layer_in, i, n_dp)
    gain_one = permute_blocks(norm_gain.astype(f32), i, n_dp)
    gain_two = permute_blocks(ffn_gain.astype(f32), i, n_dp)
    gain_latent = latent_gain.astype(f32)
    half = D // 2
    up_rows = R // n_dp
    by_kernel = qg == 1 and hp == 2 and tree_len <= 512 and n_ex == 4
    sh_width = shared_gate.shape[1] // (n_dp * n_ex)
    lanes = jnp.arange(LANES, dtype=jnp.int32) - sh_width
    route_lanes = jnp.any(routes[:, :, None] == lanes[None, None, :], axis=1).astype(bf16)

    def with_grad(which):
        return jnp.concatenate(
            [pick_half(x_rel, which, 1), pick_half(grad_out, which, 1), route_lanes], axis=1
        )

    xg_own, xg_other = with_grad(core), with_grad(1 - core)
    xg_got = gather_rel(xg_own, "expert")[1:]
    xg_there = [swap(p, "tensor", 1) for p in xg_got]
    grad_wide = half + LANES

    def grad_rows_of(got, own):
        return place_rows(
            [(p, 0, tok, k * tok, 0, (half, grad_wide)) for k, p in enumerate(got + [own])], tree_len
        )

    g_rows = grad_rows_of(xg_got, xg_own)
    wq_rows, wl_rows = hp * qw, (R + DR) // 2
    if by_kernel:
        at_pack = jnp.stack([group, core]).astype(jnp.int32)
        packed = pack_call(at_pack, query_proj, latent_proj.T, latent_up, output_proj, block)
        first = gather_parts(packed, xg_got)
        wl_parts = []
        for s, piece in enumerate(first):
            base = 0
            for part in piece:
                low = max(wq_rows, base)
                high = min(wq_rows + wl_rows, base + part.shape[0])
                if low < high:
                    wl_parts.append((part, low - base, high - low, low - wq_rows, s * block))
                base += part.shape[0]
        wl_there = swap(place_rows(wl_parts, wl_rows), "tensor", 1)
        gathered = [x_rel] + xg_got + xg_there + [wl_there] + [p for piece in first for p in piece]
        ready = first[3]
    else:
        wq_own = lax.dynamic_slice_in_dim(query_proj, group * hp * qw, hp * qw, 1).T
        wl_own = pick_half(latent_proj.T, core, 0)
        up_own = lax.dynamic_slice_in_dim(latent_up, group * hp * uw, hp * uw, 1)
        wo_own = lax.dynamic_slice_in_dim(output_proj, group * hp * DV, hp * DV, 0)
        x_got = jnp.concatenate([p[:, :half] for p in xg_got], axis=0)
        x_there = jnp.concatenate([p[:, :half] for p in xg_there], axis=0)
        wq = jnp.concatenate(gather_dp(wq_own), axis=1)
        wl_got = jnp.concatenate(gather_dp(wl_own), axis=1)
        wl = rows_join(wl_got, swap(wl_got, "tensor", 1), core)
        up = jnp.concatenate(canonical(gather_rel(up_own, "dp"), i), axis=0)
        wo = jnp.concatenate(gather_rel(wo_own, "dp"), axis=1)
        x_tree = jnp.concatenate([x_rel, halves(x_got, x_there, core, 1)], axis=0)
        ready = [wq, wo]

    local_experts = expert_gate.shape[0]
    parts = n_dp // local_experts
    width = expert_gate.shape[2] // parts
    chosen, part_at = i // parts, (i % parts) * width
    expert_id = j * local_experts + chosen
    sh_sent = []
    for c in range(n_dp):
        at_unit = (j * n_dp + c) * sh_width
        sh_sent += [
            lax.dynamic_slice_in_dim(shared_gate, at_unit, sh_width, 1).T,
            lax.dynamic_slice_in_dim(shared_up, at_unit, sh_width, 1).T,
            lax.dynamic_slice_in_dim(shared_down, at_unit, sh_width, 0),
        ]
    sh_sent = order([jnp.concatenate(sh_sent, axis=0)], ready)[0]
    sh_got = lax.all_to_all(sh_sent, "dp", 0, 0, tiled=True)
    sh_rows = jnp.concatenate(
        [sh_got[c * 3 * sh_width : (c + 1) * 3 * sh_width] for c in range(n_dp)], axis=1
    )
    hidden_width = -(-(LANES + width) // LANES) * LANES

    room = LANES - sh_width
    shared_w = jnp.concatenate(
        [
            jnp.pad(sh_rows[:sh_width], ((0, room), (0, 0))),
            sh_rows[sh_width : 2 * sh_width],
            router.T,
            jnp.zeros((room - EXPERTS, D), bf16),
            jnp.pad(sh_rows[2 * sh_width :], ((0, room), (0, 0))),
        ],
        axis=0,
    )
    feed_weights = [jnp.swapaxes(expert_gate, 1, 2), jnp.swapaxes(expert_up, 1, 2), expert_down]
    pick = chosen
    if parts > 1:
        feed_weights = [lax.dynamic_slice(w, (chosen, part_at, 0), (1, width, D)) for w in feed_weights]
        pick = chosen * 0
    feed_weights = feed_weights + [shared_w]

    slots = jnp.arange(tree_len, dtype=jnp.int32)
    token_index = (j ^ (slots // tok)) * tok + slots % tok

    def queries_of(values):
        if qg == 1:
            return values
        split = values.reshape((n_q, qg, tok) + values.shape[1:])[:, 0]
        return split.reshape((rows_q,) + values.shape[1:])

    position, segment, parent, grand = tree_layout(leaf_parent, token_index, trunk_len, seg_len)
    freqs = 10000.0 ** (-2.0 * jnp.arange(DR // 2, dtype=f32) / DR)
    angles = position.astype(f32)[:, None] * freqs[None, :]
    cosine, sine = jnp.cos(angles), jnp.sin(angles)
    q_cos, q_sin = queries_of(cosine), queries_of(sine)
    allowed = visible(
        queries_of(segment),
        queries_of(parent),
        queries_of(grand),
        queries_of(token_index),
        segment,
        token_index,
    )

    own_rows = x_rel.astype(f32)
    inverse_one = rms_stats(own_rows)
    unit_one = own_rows * inverse_one
    at_all = jnp.stack([core, i]).astype(jnp.int32)
    if by_kernel:
        cos_lanes = jnp.concatenate([cosine] * 4, axis=1)
        sin_lanes = jnp.concatenate([-sine, sine] * 2, axis=1)
        rows, wide = tree_len, (tree_len, LANES)
        (
            part_own, part_other, normed, keys, queries, nope, probs, mixed, heads_out, unit_latent,
            inverse_latent,
        ) = whole_call(
            attend_kernel,
            gathered,
            [
                gain_one[None], cos_lanes, sin_lanes, allowed.astype(bf16),
                gain_latent[None],
            ],
            [
                ((rows, half), bf16), ((rows, half), bf16),
                ((rows, D), bf16), ((rows, R + LANES), bf16), ((2, rows, R + LANES), bf16),
                ((rows, 2 * DN), bf16), ((2, rows, rows), f32), ((2, rows, R), bf16),
                ((rows, 2 * DV), bf16), ((rows, R), f32), (wide, f32),
            ],
            [],
            at_all, tree_len, wq_rows, hp * DV,
        )
        part_other = order([part_other], [sh_got])[0]
    else:
        tree_unit = x_tree.astype(f32)
        tree_unit = tree_unit * rms_stats(tree_unit)
        normed = (tree_unit * gain_one).astype(bf16)
        normed_q = queries_of(normed)
        query_all = mm_nt(normed_q, wq)
        latent_all = mm_nt(normed, wl)
        inverse_latent = rms_stats(latent_all[:, :R])
        unit_latent = latent_all[:, :R] * inverse_latent
        latent = (unit_latent * gain_latent).astype(bf16)
        key_rope = rotate(latent_all[:, R:], cosine, sine).astype(bf16)
        keys = jnp.concatenate([latent, key_rope], axis=1)
        up_key = [up[:, h * uw : h * uw + DN] for h in range(hp)]
        up_value = [up[:, h * uw + DN : (h + 1) * uw] for h in range(hp)]
        query_nope = [query_all[:, h * qw : h * qw + DN].astype(bf16) for h in range(hp)]
        queries = jnp.concatenate(
            [
                jnp.concatenate(
                    [
                        mm_nt(query_nope[h], up_key[h]).astype(bf16),
                        rotate(query_all[:, h * qw + DN : (h + 1) * qw], q_cos, q_sin).astype(bf16),
                    ],
                    axis=1,
                )
                for h in range(hp)
            ],
            axis=0,
        )
        raw_scores = mm_nt(queries, keys).reshape(hp, rows_q, tree_len)
        scores = jnp.where(allowed[None], raw_scores * score_scale, masked_score)
        exp_scores = jnp.exp(scores - jnp.max(scores, axis=-1, keepdims=True))
        probs = exp_scores / jnp.sum(exp_scores, axis=-1, keepdims=True)
        probs = probs.reshape(hp * rows_q, tree_len)
        probs_low = probs.astype(bf16)
        mixed = mm(probs_low, latent).astype(bf16)
        mixed_head = [mixed[h * rows_q : (h + 1) * rows_q] for h in range(hp)]
        heads_out = jnp.concatenate(
            [mm(mixed_head[h], up_value[h]).astype(bf16) for h in range(hp)], axis=1
        )
        part_own, part_other = mm(heads_out, pick_half(wo, core, 1)), mm(
            heads_out, pick_half(wo, 1 - core, 1)
        )

    g_parts = gather_parts(g_rows)

    def tree_scatter(partial_own, partial_other, count, stride, before=None):
        there = swap(partial_other.astype(bf16), "tensor", 1)
        joined = (partial_own.astype(f32) + there.astype(f32)).astype(bf16)
        own = total(
            exchange_rel(
                [joined[s * tok : (s + 1) * tok] for s in range(count)], "expert", stride
            )
        )
        if before is not None:
            own = order([own], before)[0]
        return halves(own, swap(own, "tensor", 1), core, 1)

    attention = tree_scatter(part_own, part_other, n_q, qg, g_parts[1] + g_parts[2])
    residual = own_rows + attention
    inverse_two = rms_stats(residual)
    unit_two = residual * inverse_two
    normed_two = permute_blocks((unit_two * gain_two).astype(bf16), i, n_dp)

    n_half = pick_half(normed_two, core, 1)
    n_other = pick_half(normed_two, 1 - core, 1)
    n_others = join_rows(gather_rel(n_half, "expert")[1:])
    own_parts = gather_parts(n_half)
    n_others = order([n_others], g_parts[3] + own_parts[1] + own_parts[2])[0]
    n_there = swap(n_others, "tensor", 1)
    g_rest = join_rows(g_parts[1] + g_parts[2] + g_parts[3])
    grad_own = [g_rows, g_rest]
    grad_other = [grad_rows_of(xg_there, xg_other), swap(g_rest, "tensor", 1)]
    at = jnp.stack([pick, core, sh_width + expert_id]).astype(jnp.int32)
    tree_rows = n_others.shape[0] + tok
    tokens = tree_rows * n_dp

    def feed(k, own, other, kept, others):
        return feed_call(
            at, sh_width, width, hidden_width, own, other, grad_own[k], grad_other[k],
            feed_weights, (k * tree_rows, tokens), kept, others,
        )

    rows_own = [join_rows([n_others, n_half])]
    rows_other = [join_rows([n_there, n_other])]
    made = feed(0, rows_own[0], rows_other[0], [], [])
    other_parts = gather_parts(n_others, [made[0]])
    near = join_rows(
        other_parts[1] + own_parts[1] + other_parts[2] + own_parts[2], [made[0]]
    )
    far = join_rows(other_parts[3] + own_parts[3])
    rows_own.append(join_rows([near, far]))
    rows_other.append(join_rows([swap(near, "tensor", 1), swap(far, "tensor", 1)]))
    grad_parts, out_parts = [made[2:4]], [made[4:6]]
    theirs = [swap(made[3], "tensor", 1)]
    out_there = [swap(made[5], "tensor", 1)]
    made = feed(1, rows_own[1], rows_other[1], list(made[:2]), theirs + out_there)
    grad_parts.append(made[2:4])
    out_parts.append(made[4:6])
    hidden_scaled, back_pre = made[:2]

    def join(mine, theirs):
        return (mine.astype(f32) + swap(theirs, "tensor", 1).astype(f32)).astype(bf16)

    routed_at, up_at = (LANES, width), (hidden_width + LANES, width)
    sent_width = -(-sh_width // 16) * 16
    sent_router = -(-(sh_width + EXPERTS) // 16) * 16

    theirs.append(swap(grad_parts[1][1], "tensor", 1))
    many = tree_rows - tok

    def joined(mine, there, low, high):
        return (mine[low:high].astype(f32) + there[low:high].astype(f32)).astype(bf16)

    def cut_of(parts, there, low, high):
        return [joined(parts[0], there[0], low, high)] + [
            joined(parts[1], there[1], s * tree_rows + low, s * tree_rows + high)
            for s in range(n_dp - 1)
        ]

    grad_mine = [p[0] for p in grad_parts]
    hidden_late = order([hidden_scaled], [theirs[1]])[0]
    down_sent = weight_call(
        core, hidden_late, grad_own, grad_other, [routed_at, (0, sent_width)], n_dp
    )
    others_state = reduce_first(cut_of(grad_mine, theirs, 0, many))
    others_first = list(others_state[2:])
    back_late = order([back_pre], others_first)[0]
    gate_sent = weight_call(
        core, back_late, rows_own, rows_other,
        [routed_at, (0, sent_width), (hidden_width, sent_router)], n_dp,
    )
    own_state = reduce_first(order(cut_of(grad_mine, theirs, many, tree_rows), others_first))
    gn2_others = reduce_second(others_state, [down_sent])
    gn2_own = order([reduce_second(own_state)], [gate_sent])[0]

    out_there.append(swap(order([out_parts[1][1]], [theirs[1]])[0], "tensor", 1))
    out_state = reduce_first(
        order(
            cut_of(
                [p[0] for p in out_parts],
                out_there,
                0,
                tree_rows,
            ),
            [gn2_own],
        )
    )
    out_first = list(out_state[2:])
    z_sent = gn2_others
    z_got = exchange_rel(
        [gn2_own] + [z_sent[s * tok : (s + 1) * tok] for s in range(n_ex - 1)], "expert"
    )
    back_last = order([back_late], [gn2_others])[0]
    up_sent = weight_call(core, back_last, rows_own, rows_other, [up_at], n_dp)
    gn2_half = order([total(z_got)], [up_sent])[0]
    gn2 = permute_blocks(halves(gn2_half, swap(gn2_half, "tensor", 1), core, 1), i, n_dp)

    grad_ffn_gain = jnp.sum(gn2 * unit_two, axis=0, keepdims=True)
    grad_residual = permute_blocks(grad_out, i, n_dp).astype(f32) + rms_back(
        gn2 * gain_two, unit_two, inverse_two
    )
    res_half = pick_half(grad_residual.astype(bf16), core, 1)

    out_mine = reduce_second(out_state)

    def to_owners(sent, others):
        sent = order([sent], others)[0]
        return lax.all_to_all(sent, "dp", 0, 0, tiled=True).reshape(n_dp, -1, block)

    down_got = to_owners(down_sent, [gn2_own])
    gate_got = to_owners(gate_sent, [gn2_half])
    up_got = to_owners(up_sent, [gn2_half])
    router_at = width + sent_width + sh_width
    router_block = gate_sent.reshape(n_dp, -1, block)[:, router_at : router_at + EXPERTS]
    grad_router_rows = jnp.concatenate(
        [lax.dynamic_index_in_dim(router_block, i ^ s, 0, False) for s in range(n_dp)], axis=1
    )

    res_others = gather_z(res_half)
    res_others = halves(res_others, swap(res_others, "tensor", 1), core, 1)
    res_tree = jnp.concatenate([grad_residual.astype(bf16), res_others], axis=0)
    res_tree = order([res_tree], out_first)[0]
    if by_kernel:
        (
            back_mine, back_other, grad_wo, wq_grad, wl_grad, wl_sent, by_r, grad_norm_gain,
            grad_latent_gain,
        ) = (
            whole_call(
                attend_back_kernel,
                gathered,
                [
                    res_tree, normed, cos_lanes, sin_lanes, gain_latent[None], keys, queries, nope,
                    probs, mixed, heads_out, unit_latent, inverse_latent,
                ],
                [
                    ((rows, half), bf16), ((rows, half), bf16), ((2 * DV, D), bf16),
                    ((2 * qw, D), bf16), ((wl_rows, D), bf16), ((wl_rows, D), bf16),
                    ((2 * uw, R), bf16), ((1, D), f32),
                    ((1, R), f32),
                ],
                [
                    pltpu.VMEM((rows, R + LANES), bf16),
                    pltpu.VMEM((rows, 2 * qw), bf16),
                    pltpu.VMEM((rows, R + LANES), f32),
                ],
                at_all, tree_len, wq_rows, hp * DV,
            )
        )
    else:
        res_q = res_tree
        res_q = queries_of(res_q)
        grad_heads = mm_nt(res_q, wo).astype(bf16)
        grad_head = [grad_heads[:, h * DV : (h + 1) * DV] for h in range(hp)]

        grad_wo = mm_tn(heads_out, res_q)

        grad_mixed = jnp.concatenate(
            [mm_nt(grad_head[h], up_value[h]).astype(bf16) for h in range(hp)], axis=0
        )
        grad_att = mm_nt(grad_mixed, latent)
        delta = jnp.sum(probs * grad_att, axis=-1, keepdims=True)
        score_grad = (probs * (grad_att - delta) * score_scale).astype(bf16)
        grad_queries = mm(score_grad, keys)
        grad_keys = mm_tn(score_grad, queries)
        grad_latent_keys = grad_keys[:, :R] + mm_tn(probs_low, grad_mixed)
        grad_query_latent = grad_queries[:, :R].astype(bf16)
        grad_query_parts, grad_up_parts = [], []
        for h in range(hp):
            rows = slice(h * rows_q, (h + 1) * rows_q)
            grad_query_parts.append(mm(grad_query_latent[rows], up_key[h]))
            grad_query_parts.append(rotate_back(grad_queries[rows, R:], q_cos, q_sin))
            grad_up_parts.append(mm_tn(query_nope[h], grad_query_latent[rows]))
            grad_up_parts.append(mm_tn(grad_head[h], mixed_head[h]))
        grad_query_all = jnp.concatenate(grad_query_parts, axis=1).astype(bf16)
        grad_latent_gain = jnp.sum(grad_latent_keys * unit_latent, axis=0, keepdims=True)
        grad_latent_all = jnp.concatenate(
            [
                rms_back(grad_latent_keys * gain_latent, unit_latent, inverse_latent),
                rotate_back(grad_keys[:, R:], cosine, sine),
            ],
            axis=1,
        ).astype(bf16)

        grad_query_rows = grad_query_all
        if qg > 1:
            grad_query_rows = jnp.pad(
                grad_query_all.reshape(n_q, 1, tok, -1), ((0, 0), (0, qg - 1), (0, 0), (0, 0))
            ).reshape(tree_len, -1)
        def back_half(which):
            return mm(grad_query_rows, pick_half(wq, which, 1)) + mm(
                grad_latent_all, pick_half(wl, which, 1)
            )

        back_mine, back_other = back_half(core), back_half(1 - core)
        norm_mine = jnp.sum(back_mine * pick_half(tree_unit, core, 1), axis=0, keepdims=True)
        norm_other = jnp.sum(back_other * pick_half(tree_unit, 1 - core, 1), axis=0, keepdims=True)
        grad_norm_gain = halves(norm_mine, norm_other, core, 1)
        wq_grad, wl_grad = mm_tn(grad_query_all, normed_q), mm_tn(grad_latent_all, normed)
        by_r = jnp.concatenate(grad_up_parts, axis=0)


    up_sub = up_rows // n_ex
    gain_row = jnp.concatenate(
        [
            lax.dynamic_slice_in_dim(grad_latent_gain, (i ^ s) * up_rows, up_rows, 1)
            for s in range(n_dp)
        ],
        axis=1,
    ).reshape(n_dp * n_ex, up_sub)
    gain_row = jnp.pad(gain_row, ((0, 0), (0, sub - up_sub))).reshape(1, D)
    if not by_kernel:
        wl_grad = wl_grad.astype(bf16)
        wl_grad, wl_sent = pick_half(wl_grad, core, 0), pick_half(wl_grad, 1 - core, 0)
    wl_there = swap(wl_sent, "tensor", 1)
    wl_grad = wl_grad.astype(f32) + wl_there.astype(f32)
    small_rows = jnp.concatenate(
        [
            grad_norm_gain,
            0.5 * grad_ffn_gain,
            grad_router_rows.astype(f32),
            gain_row,
            jnp.zeros((13, D), f32),
        ],
        axis=0,
    )
    by_d = [grad_wo, wq_grad, wl_grad, small_rows]
    by_r = by_r.astype(bf16)
    d_rows, r_rows = sum(p.shape[0] for p in by_d), by_r.shape[0]
    by_r = [lax.dynamic_slice_in_dim(by_r, (i ^ s) * up_rows, up_rows, 1) for s in range(n_dp)]
    split_r = block // up_rows
    cut_r = r_rows // split_r
    by_r = jnp.concatenate(
        [
            jnp.concatenate([by_r[s][c * cut_r : (c + 1) * cut_r] for c in range(split_r)], 1)
            for s in range(n_dp)
        ],
        axis=1,
    )
    by_d[0] = order([by_d[0]], [down_got])[0]
    tail_state = reduce_first(stack_rows(by_d + [by_r], block))
    grad_normed = tree_scatter(back_mine, back_other, n_ex, 1, list(tail_state[2:]))
    grad_in = permute_blocks(
        grad_residual + rms_back(grad_normed * gain_one, unit_one, inverse_one), i, n_dp
    )

    mine = reduce_second(tail_state, [gate_got])
    out_mine = order([out_mine], [back_mine])[0]
    ffn_half = along_z(out_mine[:many], out_mine[many:])
    out_half = (pick_half(permute_blocks(residual, i, n_dp), core, 1) + ffn_half).astype(bf16)
    layer_out = halves(out_half, swap(out_half, "tensor", 1), core, 1)

    mine_r = jnp.concatenate(
        [mine[d_rows:, c * up_rows : (c + 1) * up_rows] for c in range(split_r)], axis=0
    )

    def z_piece(s):
        to = j ^ s
        rows_r = lax.dynamic_slice_in_dim(mine_r, to * up_sub, up_sub, 1)
        cut = r_rows * up_sub // sub
        return jnp.concatenate(
            [lax.dynamic_slice_in_dim(mine[:d_rows], to * sub, sub, 1)]
            + [
                jnp.concatenate(
                    [rows_r[c * cut : (c + 1) * cut] for c in range(sub // up_sub)], axis=1
                )
            ],
            axis=0,
        )

    got = exchange_rel([z_piece(s) for s in range(n_ex)], "expert")

    def over_groups(pieces):
        ordered = canonical(pieces, j)
        return jnp.concatenate(
            [total(ordered[g * qg : (g + 1) * qg]) for g in range(groups)], axis=0
        )

    ends = [hp * DV, hp * DV + wq_rows, hp * DV + wq_rows + wl_rows]
    grad_output_proj = over_groups([p[: ends[0]] for p in got])
    grad_query_rows = [p[ends[0] : ends[1]] for p in got]
    if by_kernel:
        grad_query_rows = [
            jnp.concatenate(
                [p[:DN], p[2 * DN : 2 * DN + DR], p[DN : 2 * DN], p[2 * DN + DR :]], axis=0
            )
            for p in grad_query_rows
        ]
    grad_query_proj = over_groups(grad_query_rows).T
    grad_latent_up = over_groups(
        [
            jnp.concatenate(
                [p[d_rows:, c * up_sub : (c + 1) * up_sub] for c in range(sub // up_sub)], axis=0
            )
            for p in got
        ]
    ).T
    rest = total([p[ends[1] : d_rows] for p in got])
    rest_there = swap(rest, "tensor", 1)
    grad_latent_proj = rows_join(rest[:wl_rows], rest_there[:wl_rows], core).T
    small = rest[wl_rows:] + rest_there[wl_rows:]

    down_got, gate_got = order([down_got, gate_got], list(tail_state[2:]))
    up_got = order([up_got], [mine])[0]
    shared_all = jnp.concatenate(
        [gate_got[:, width : width + 2 * sent_width], down_got[:, width:]], axis=1
    )
    shared_all = jnp.stack(
        canonical(
            exchange_rel(
                [lax.dynamic_slice_in_dim(shared_all, (j ^ s) * sub, sub, 2) for s in range(n_ex)],
                "expert",
            ),
            j,
        )
    )

    def shared_part(k):
        rows = shared_all[:, :, k * sent_width : k * sent_width + sh_width]
        return rows.reshape(-1, sub).astype(f32)

    def expert_part(got):
        return got[:, :width].reshape(local_experts, parts * width, block).astype(f32)

    grad_shared_gate, grad_shared_up = shared_part(0).T, shared_part(1).T
    grad_shared_down = shared_part(2)
    grad_expert_gate = jnp.swapaxes(expert_part(gate_got), 1, 2)
    grad_expert_up = jnp.swapaxes(expert_part(up_got), 1, 2)
    grad_expert_down = expert_part(down_got)

    return (
        layer_out,
        grad_in,
        small[0],
        grad_query_proj,
        grad_latent_proj,
        small[2 + EXPERTS, :up_sub],
        grad_latent_up,
        grad_output_proj,
        small[1],
        small[2 : 2 + EXPERTS].T,
        grad_shared_gate,
        grad_shared_up,
        grad_shared_down,
        grad_expert_gate,
        grad_expert_up,
        grad_expert_down,
    )


def solution(mesh):
    placed = (
        P(("dp", "expert"), None),
        P(),
        P("dp", "tensor"),
        P("dp", None),
        P(),
        P("dp", "tensor"),
        P("tensor", "dp"),
        P(),
        P(),
        P("dp", "tensor"),
        P("dp", "tensor"),
        P("tensor", "dp"),
        P("expert", None, "tensor"),
        P("expert", None, "tensor"),
        P("expert", "tensor", None),
        P(("dp", "expert"), None),
        P(),
        P(("dp", "expert"), None),
    )
    return jax.shard_map(
        per_device,
        mesh=mesh,
        in_specs=placed,
        out_specs=(
            P(("dp", "expert"), None),
            P(("dp", "expert"), None),
            P(("dp", "expert")),
            P(("dp", "expert"), "tensor"),
            P(("dp", "expert"), None),
            P(("dp", "expert")),
            P(("dp", "expert"), "tensor"),
            P("tensor", ("dp", "expert")),
            P(("dp", "expert")),
            P(("dp", "expert"), None),
            P(("dp", "expert"), "tensor"),
            P(("dp", "expert"), "tensor"),
            P("tensor", ("dp", "expert")),
            P("expert", "dp", "tensor"),
            P("expert", "dp", "tensor"),
            P("expert", "tensor", "dp"),
        ),
        check_vma=False,
    )
```

time: 840 us -> 688 us (0.82)
  Pallas kernels: 46.9 us -> 164 us
  matrix products: 107 us -> 0 us
  waiting for transfers between devices: 305 us -> 224 us
  local copies, waits for them, and re-layouts: 126 us -> 93 us
  starting transfers between devices: 130 us -> 103 us
  other arithmetic: 111 us -> 94.7 us
    pallas_call x2 -> x45, Pallas kernels: 42.6 us -> 164 us  [the longest x2 69.3 us: feed_call(): pl.pallas_call(functools.partial(feed_kernel, sh_width, width, padded, su...]
    dot_general x37 -> x0, matrix products: 107 us -> none  [the longest x13 48.2 us: mm_tn(): lax.dot_general(left, right, (((0,), (0,)), ((), ())), preferred_element_...]
    ppermute x115 -> x80, waiting for transfers between devices: 305 us -> 224 us  [swap(): lax.ppermute(values, axis, [(k, k ^ step) for k in range(lax.axis_size(ax...]
    ppermute x115 -> x80, starting transfers between devices: 130 us -> 86.2 us  [swap(): lax.ppermute(values, axis, [(k, k ^ step) for k in range(lax.axis_size(ax...]
    select_n x10 -> x3, other arithmetic: 26.9 us -> 4.67 us  [halves(): jnp.where(core == 0, jnp.concatenate([own, other], axis=dim), jnp.concate...]
    all_to_all x0 -> x4, starting transfers between devices: none -> 17.1 us  [the longest x3 13.4 us: to_owners(): return lax.all_to_all(sent, 'dp', 0, 0, tiled=True).reshape(n_dp, -1, block)]
    dynamic_slice x6 -> x3, local copies, waits for them, and re-layouts: 11.3 us -> 0.14 us  [pick_half(): return lax.dynamic_slice_in_dim(values, which * width, width, dim)]
    transpose x3 -> x4, other arithmetic: 1.52 us -> 11.1 us  [the longest x1 5.2 us: per_device(): grad_expert_up = jnp.swapaxes(expert_part(up_got), 1, 2)]
  transfers between devices with their start and end apart: 115 -> 84, of which waited for: 42 -> 36; matrix products, arithmetic and copies ran while one was open for 34% -> 21% of each run, Pallas kernels for 2% -> 17%
where the time goes in v2:
time: 688 us; the launch traced here: 682 us
  waiting for transfers between devices  224 us (33%)
  Pallas kernels  164 us (24%)
  starting transfers between devices  103 us (15%)
  other arithmetic  94.7 us (14%)
  local copies, waits for them, and re-layouts  93 us (14%)
    ppermute x80, waiting for transfers between devices, swap(): lax.ppermute(values, axis, [(k, k ^ step) for k in range(lax.axis_size(ax...  224 us
    ppermute x80, starting transfers between devices, swap(): lax.ppermute(values, axis, [(k, k ^ step) for k in range(lax.axis_size(ax...  86.2 us
    pallas_call x2, Pallas kernels, feed_call(): pl.pallas_call(functools.partial(feed_kernel, sh_width, width, padded, su...  69.3 us
    unnamed x259, local copies, waits for them, and re-layouts  56.6 us
    pallas_call x3, Pallas kernels, weight_call(): pl.pallas_call(body, grid_spec=pltpu.PrefetchScalarGridSpec(num_scalar_pr...  42.5 us
    pallas_call x2, Pallas kernels, whole_call(): pl.pallas_call(kernel, in_specs=[pl.BlockSpec(memory_space=pltpu.SMEM)] +...  36.9 us
  transfers between devices with their start and end apart: 84, of which 36 were waited for; matrix products, arithmetic and copies ran while one was open for 21% of the time, Pallas kernels for 17%

profile of v2, /device:TPU:9, one launch (start us, length us, event | category | flops | bytes accessed | tf_op | source)
XLA Modules:
  0.0 682.1 jit_solution(13522581414918046374)
XLA Ops:
  44.7 11.4 %collective-permute-done.2.refs_4_.refs_3_.refs_2_ = bf16[128,2176]{1,0:T(8,128)(2,1)} collective-permute-done((bf16[128,2176]{1,0:T(8,128)(2,1)}, bf16[128,2176]{1,0:T(8,128)(2,1)}, u32[]{:S(2)}, u32[]{:S(2)}) %collective-permute-start.2) | collective-permute-done | bytes 557088 | tf_op jit(solution)/shard_map/ppermute | solution.py:105
  61.0 7.3 %collective-permute-done.8.refs_3_.refs_11_.refs_1_ = bf16[528,512]{1,0:T(8,128)(2,1)S(1)} collective-permute-done((bf16[528,512]{1,0:T(8,128)(2,1)}, bf16[528,512]{1,0:T(8,128)(2,1)S(1)}, u32[]{:S(2)}, u32[]{:S(2)}) %collective-permute-start.8) | collective-permute-done | bytes 540704 | tf_op jit(solution)/shard_map/ppermute | solution.py:105
  90.9 15.2 %shard_map.300 = (bf16[512,1024]{1,0:T(8,128)(2,1)}, bf16[512,1024]{1,0:T(8,128)(2,1)}, bf16[512,2048]{1,0:T(8,128)(2,1)}, bf16[512,640]{1,0:T(8,128)(2,1)}, bf1...) custom-call(s32[2]{0:T(128)} %pad_add_fusion.at, ...), custom_call_target="tpu_custom_call" | custom-call | tf_op jit(solution)/shard_map/pallas_call | solution.py:626
  107.8 12.0 %collective-permute-done.15.refs_1_.refs_0_ = bf16[512,1152]{1,0:T(8,128)(2,1)S(1)} collective-permute-done((bf16[512,1152]{1,0:T(8,128)(2,1)}, bf16[512,1152]{1,0:T(8,128)(2,1)S(1)}, u32[]{:S(2)}, u32[]{:S(2)}) %collective-permute-start.15) | collective-permute-done | bytes 1179680 | tf_op jit(solution)/shard_map/ppermute | solution.py:105
  140.6 10.7 %collective-permute-done.14 = bf16[128,1024]{1,0:T(8,128)(2,1)} collective-permute-done((bf16[128,1024]{1,0:T(8,128)(2,1)}, bf16[128,1024]{1,0:T(8,128)(2,1)}, u32[]{:S(2)}, u32[]{:S(2)}) %collective-permute-start.14) | collective-permute-done | bytes 262176 | tf_op jit(solution)/shard_map/ppermute | solution.py:105
  163.2 6.5 collective-permute-done.18.refs_0_
  173.2 11.2 %collective-permute-done.20.refs_2_ = bf16[128,1024]{1,0:T(8,128)(2,1)S(1)} collective-permute-done((bf16[128,1024]{1,0:T(8,128)(2,1)S(1)}, bf16[128,1024]{1,0:T(8,128)(2,1)S(1)}, u32[]{:S(2)}, u32[]{:S(2)}) %collective-permute-start.20) | collective-permute-done | bytes 262176 | tf_op jit(solution)/shard_map/ppermute | solution.py:105
  192.1 21.0 %shard_map.310 = (bf16[2048,896]{1,0:T(8,128)(2,1)}, bf16[2048,1792]{1,0:T(8,128)(2,1)}, bf16[512,1024]{1,0:T(8,128)(2,1)}, bf16[512,1024]{1,0:T(8,128)(2,1)}, b...) custom-call(s32[3]{0:T(128)} %pad_add_fusion.2.at, bf16[512,1024]{1,0:T(8,128)(2,1)} %copy-done.4, ...), custom_call_target="tpu_custom_call" | custom-call | flops 11274289152 | bytes 22151168 | tf_op jit(solution)/shard_map/pallas_call | solution.py:419
  218.3 12.0 %collective-permute-done.31.refs_2_ = bf16[64,1024]{1,0:T(8,128)(2,1)S(1)} collective-permute-done((bf16[64,1024]{1,0:T(8,128)(2,1)S(1)}, bf16[64,1024]{1,0:T(8,128)(2,1)S(1)}, u32[]{:S(2)}, u32[]{:S(2)}) %collective-permute-start.31) | collective-permute-done | bytes 131104 | tf_op jit(solution)/shard_map/ppermute | solution.py:105
  244.1 48.3 %shard_map.317 = (bf16[2048,896]{1,0:T(8,128)(2,1)}, bf16[2048,1792]{1,0:T(8,128)(2,1)}, bf16[1536,1024]{1,0:T(8,128)(2,1)}, bf16[1536,1024]{1,0:T(8,128)(2,1)},...) custom-call(s32[3]{0:T(128)} %pad_add_fusion.2.at, ...), custom_call_target="tpu_custom_call", output_to_operand_aliasing={{0}: (9, {}), {1}: (10, {})} | custom-call | flops 33822867456 | bytes 44433408 | tf_op jit(solution)/shard_map/pallas_call | solution.py:419
  292.7 5.6 collective-permute-done.37.refs_1_
  307.5 13.0 %shard_map.325.refs_2_.refs_0_ = bf16[3200,512]{1,0:T(8,128)(2,1)} custom-call(s32[1]{0:T(128)} %bitcast.at, bf16[2048,896]{1,0:T(8,128)(2,1)} %shard_map.324.refs_0_, bf16[512,1152]{1,0:T(8,128)(2,1)} %shard_map.303.g_own.refs_1_, bf16[1536,1152]{1,0:T(8,128)(2,1)} %shard_map.316.g_own.refs_2_, bf16[512,1152]{1,0:T(8,128)(2,1)} %copy-done.18, ...), custom_call_target="tpu_custom_call" | custom-call | tf_op jit(solution)/shard_map/pallas_call | solution.py:674
  332.8 15.8 %shard_map.321.refs_1_.refs_0_ = bf16[3648,512]{1,0:T(8,128)(2,1)} custom-call(s32[1]{0:T(128)} %bitcast.at, bf16[2048,1792]{1,0:T(8,128)(2,1)} %shard_map.320.refs_0_, bf16[512,1024]{1,0:T(8,128)(2,1)} %copy-done.4, bf16[1536,1024]{1,0:T(8,128)(2,1)} %shard_map.314.n_own.refs_2_, bf16[512,1024]{1,0:T(8,128)(2,1)} %copy-done.5, ...), custom_call_target="tpu_custom_call" | custom-call | tf_op jit(solution)/shard_map/pallas_call | solution.py:674
  354.9 13.7 %shard_map.328.refs_1_.refs_0_ = bf16[2816,512]{1,0:T(8,128)(2,1)} custom-call(s32[1]{0:T(128)} %bitcast.at, bf16[2048,1792]{1,0:T(8,128)(2,1)} %shard_map.327.refs_0_, bf16[512,1024]{1,0:T(8,128)(2,1)} %copy-done.4, bf16[1536,1024]{1,0:T(8,128)(2,1)} %shard_map.314.n_own.refs_2_, bf16[512,1024]{1,0:T(8,128)(2,1)} %copy-done.5, ...), custom_call_target="tpu_custom_call" | custom-call | tf_op jit(solution)/shard_map/pallas_call | solution.py:674
  388.0 5.4 collective-permute-done.55
  397.8 10.5 %collective-permute-done.57 = bf16[128,1024]{1,0:T(8,128)(2,1)S(1)} collective-permute-done((bf16[128,1024]{1,0:T(8,128)(2,1)S(1)}, bf16[128,1024]{1,0:T(8,128)(2,1)S(1)}, u32[]{:S(2)}, u32[]{:S(2)}) %collective-permute-start.57) | collective-permute-done | bytes 262176 | tf_op jit(solution)/shard_map/ppermute | solution.py:105
  410.6 4.6 add_convert_fusion.1
  421.9 4.9 all-to-all-start.1
  431.1 11.9 %collective-permute-done.47.refs_2_ = bf16[512,1024]{1,0:T(8,128)(2,1)S(1)} collective-permute-done((bf16[512,1024]{1,0:T(8,128)(2,1)}, bf16[512,1024]{1,0:T(8,128)(2,1)S(1)}, u32[]{:S(2)}, u32[]{:S(2)}) %collective-permute-start.47) | collective-permute-done | bytes 1048608 | tf_op jit(solution)/shard_map/ppermute | solution.py:105
  444.9 21.7 %shard_map.331 = (bf16[512,1024]{1,0:T(8,128)(2,1)}, bf16[512,1024]{1,0:T(8,128)(2,1)}, bf16[256,2048]{1,0:T(8,128)(2,1)}, bf16[384,2048]{1,0:T(8,128)(2,1)}, bf...) custom-call(s32[2]{0:T(128)} %pad_add_fusion.at, ...), custom_call_target="tpu_custom_call" | custom-call | tf_op jit(solution)/shard_map/pallas_call | solution.py:626
  471.9 19.2 %collective-permute-done.48 = bf16[256,1024]{1,0:T(8,128)(2,1)S(1)} collective-permute-done((bf16[256,1024]{1,0:T(8,128)(2,1)S(1)}, bf16[256,1024]{1,0:T(8,128)(2,1)S(1)}, u32[]{:S(2)}, u32[]{:S(2)}) %collective-permute-start.48) | collective-permute-done | bytes 524320 | tf_op jit(solution)/shard_map/ppermute | solution.py:105
  501.3 4.8 all-to-all-start.2
  509.7 11.3 %collective-permute-done.61 = bf16[128,1024]{1,0:T(8,128)(2,1)} collective-permute-done((bf16[128,1024]{1,0:T(8,128)(2,1)}, bf16[128,1024]{1,0:T(8,128)(2,1)}, u32[]{:S(2)}, u32[]{:S(2)}) %collective-permute-start.61) | collective-permute-done | bytes 262176 | tf_op jit(solution)/shard_map/ppermute | solution.py:105
  543.3 4.3 collective-permute-done.64
  551.3 11.2 %collective-permute-done.66 = bf16[128,1024]{1,0:T(8,128)(2,1)} collective-permute-done((bf16[128,1024]{1,0:T(8,128)(2,1)}, bf16[128,1024]{1,0:T(8,128)(2,1)}, u32[]{:S(2)}, u32[]{:S(2)}) %collective-permute-start.66) | collective-permute-done | bytes 262176 | tf_op jit(solution)/shard_map/ppermute | solution.py:105
  564.5 8.0 %collective-permute-done.69.refs_2_.refs_3_ = bf16[1088,512]{1,0:T(8,128)(2,1)S(1)} collective-permute-done((bf16[1088,512]{1,0:T(8,128)(2,1)}, bf16[1088,512]{1,0:T(8,128)(2,1)S(1)}, u32[]{:S(2)}, u32[]{:S(2)}) %collective-permute-start.69) | collective-permute-done | bytes 1114144 | tf_op jit(solution)/shard_map/ppermute | solution.py:105
  580.7 5.2 convert_bitcast_fusion.1
  593.2 5.2 slice_convert_fusion
  605.0 12.6 %collective-permute-done.79 = bf16[4,288,128]{2,1,0:T(8,128)(2,1)} collective-permute-done((bf16[4,288,128]{2,1,0:T(8,128)(2,1)}, bf16[4,288,128]{2,1,0:T(8,128)(2,1)}, u32[]{:S(2)}, u32[]{:S(2)}) %collective-permute-start.79) | collective-permute-done | bytes 294944 | tf_op jit(solution)/shard_map/ppermute | solution.py:105
  640.5 5.2 convert_bitcast_fusion
  652.9 5.3 collective-permute-done.74
  658.6 12.6 %collective-permute-done.75 = bf16[1088,128]{1,0:T(8,128)(2,1)S(1)} collective-permute-done((bf16[1088,128]{1,0:T(8,128)(2,1)S(1)}, bf16[1088,128]{1,0:T(8,128)(2,1)S(1)}, u32[]{:S(2)}, u32[]{:S(2)}) %collective-permute-start.75) | collective-permute-done | bytes 278560 | tf_op jit(solution)/shard_map/ppermute | solution.py:105
  (639 shorter events, 311.8 us)
Async XLA Ops:
  5.5 39.2 %collective-permute-start = (bf16[128,2176]{1,0:T(8,128)(2,1)}, bf16[128,2176]{1,0:T(8,128)(2,1)}, u32[]{:S(2)}, u32[]{:S(2)}) collective-permute-start(bf16[128,2176]{1,0:T(8,128)(2,1)} %get-tuple-element.364.refs_3_), channel_id=1, source_target_pairs={{0,2},{2,0},{4,6},{6,4},{1,3},{3,1},{5,7},{7,5},{8,10},{10,8},{12,... | collective-permute-start | bytes 1671176 | tf_op jit(solution)/shard_map/ppermute | solution.py:105
  5.5 39.2 %collective-permute-start.1 = (bf16[128,2176]{1,0:T(8,128)(2,1)}, bf16[128,2176]{1,0:T(8,128)(2,1)}, u32[]{:S(2)}, u32[]{:S(2)}) collective-permute-start(bf16[128,2176]{1,0:T(8,128)(2,1)} %get-tuple-element.364.refs_3_), channel_id=1, source_target_pairs={{0,4},{2,6},{4,0},{6,2},{1,5},{3,7},{5,1},{7,3},{8,12},{10,14},{12... | collective-permute-start | bytes 1671176 | tf_op jit(solution)/shard_map/ppermute | solution.py:105
  8.0 48.1 %collective-permute-start.2 = (bf16[128,2176]{1,0:T(8,128)(2,1)}, bf16[128,2176]{1,0:T(8,128)(2,1)}, u32[]{:S(2)}, u32[]{:S(2)}) collective-permute-start(bf16[128,2176]{1,0:T(8,128)(2,1)} %get-tuple-element.364.refs_3_), channel_id=1, source_target_pairs={{0,6},{2,4},{4,2},{6,0},{1,7},{3,5},{5,3},{7,1},{8,14},{10,12},{12... | collective-permute-start | bytes 1671176 | tf_op jit(solution)/shard_map/ppermute | solution.py:105
  11.2 31.7 %collective-permute-start.6 = (bf16[1056,512]{1,0:T(8,128)(2,1)S(1)}, bf16[1056,512]{1,0:T(8,128)(2,1)S(1)}, u32[]{:S(2)}, u32[]{:S(2)}) collective-permute-start(bf16[1056,512]{1,0:T(8,128)(2,1)S(1)} %shard_map.297.refs_0_.refs_8_), channel_id=1, source_target_pairs={{0,8},{8,0},{16,24},{24,16},{1,9},{9,1},{17,25},{25,17},{2,10},{10... | collective-permute-start | bytes 3244040 | tf_op jit(solution)/shard_map/ppermute | solution.py:105
  12.5 31.3 %collective-permute-start.7 = (bf16[1056,512]{1,0:T(8,128)(2,1)S(1)}, bf16[1056,512]{1,0:T(8,128)(2,1)S(1)}, u32[]{:S(2)}, u32[]{:S(2)}) collective-permute-start(bf16[1056,512]{1,0:T(8,128)(2,1)S(1)} %shard_map.297.refs_0_.refs_8_), channel_id=1, source_target_pairs={{0,16},{8,24},{16,0},{24,8},{1,17},{9,25},{17,1},{25,9},{2,18},{10... | collective-permute-start | bytes 3244040 | tf_op jit(solution)/shard_map/ppermute | solution.py:105
  76.7 29.4 %all-to-all-start = ((bf16[4,264,512]{2,1,0:T(8,128)(2,1)}), bf16[4,264,512]{2,1,0:T(8,128)(2,1)S(1)}, u32[]{:S(2)}, u32[]{:S(2)}) async-start(bf16[4,264,512]{2,1,0:T(8,128)(2,1)} %bitcast.14), calls=%async_computation | async-start | bytes 2162688 | tf_op jit(solution)/shard_map/all_to_all | solution.py:803
  84.8 35.0 %collective-permute-start.15 = (bf16[512,1152]{1,0:T(8,128)(2,1)}, bf16[512,1152]{1,0:T(8,128)(2,1)S(1)}, u32[]{:S(2)}, u32[]{:S(2)}) collective-permute-start(bf16[512,1152]{1,0:T(8,128)(2,1)} %shard_map.303.g_own.refs_1_), channel_id=1, source_target_pairs={{0,8},{8,0},{16,24},{24,16},{1,9},{9,1},{17,25},{25,17},{2,10},{10... | collective-permute-start | bytes 3538952 | tf_op jit(solution)/shard_map/ppermute | solution.py:105
  86.5 35.4 %collective-permute-start.16 = (bf16[512,1152]{1,0:T(8,128)(2,1)}, bf16[512,1152]{1,0:T(8,128)(2,1)S(1)}, u32[]{:S(2)}, u32[]{:S(2)}) collective-permute-start(bf16[512,1152]{1,0:T(8,128)(2,1)} %shard_map.303.g_own.refs_1_), channel_id=1, source_target_pairs={{0,16},{8,24},{16,0},{24,8},{1,17},{9,25},{17,1},{25,9},{2,18},{10... | collective-permute-start | bytes 3538952 | tf_op jit(solution)/shard_map/ppermute | solution.py:105
  161.5 22.9 %collective-permute-start.20 = (bf16[128,1024]{1,0:T(8,128)(2,1)S(1)}, bf16[128,1024]{1,0:T(8,128)(2,1)S(1)}, u32[]{:S(2)}, u32[]{:S(2)}) collective-permute-start(bf16[128,1024]{1,0:T(8,128)(2,1)S(1)} %get-tuple-element.295.refs_1_), channel_id=1, source_target_pairs={{0,6},{2,4},{4,2},{6,0},{1,7},{3,5},{5,3},{7,1},{8,14},{10,12},{12... | collective-permute-start | bytes 786440 | tf_op jit(solution)/shard_map/ppermute | solution.py:105
  161.7 23.7 %collective-permute-start.23 = (bf16[128,1024]{1,0:T(8,128)(2,1)S(1)}, bf16[128,1024]{1,0:T(8,128)(2,1)S(1)}, u32[]{:S(2)}, u32[]{:S(2)}) collective-permute-start(bf16[128,1024]{1,0:T(8,128)(2,1)S(1)} %get-tuple-element.295.refs_1_), channel_id=1, source_target_pairs={{0,8},{8,0},{16,24},{24,16},{1,9},{9,1},{17,25},{25,17},{2,10},{10... | collective-permute-start | bytes 786440 | tf_op jit(solution)/shard_map/ppermute | solution.py:105
  162.9 22.5 %collective-permute-start.24 = (bf16[128,1024]{1,0:T(8,128)(2,1)S(1)}, bf16[128,1024]{1,0:T(8,128)(2,1)S(1)}, u32[]{:S(2)}, u32[]{:S(2)}) collective-permute-start(bf16[128,1024]{1,0:T(8,128)(2,1)S(1)} %get-tuple-element.295.refs_1_), channel_id=1, source_target_pairs={{0,16},{8,24},{16,0},{24,8},{1,17},{9,25},{17,1},{25,9},{2,18},{10... | collective-permute-start | bytes 786440 | tf_op jit(solution)/shard_map/ppermute | solution.py:105
  169.7 73.1 %collective-permute-start.35 = (bf16[1536,1152]{1,0:T(8,128)(2,1)}, bf16[1536,1152]{1,0:T(8,128)(2,1)}, u32[]{:S(2)}, u32[]{:S(2)}) collective-permute-start(bf16[1536,1152]{1,0:T(8,128)(2,1)} %shard_map.316.g_own.refs_2_), channel_id=1, source_target_pairs={{0,1},{1,0},{2,3},{3,2},{4,5},{5,4},{6,7},{7,6},{8,9},{9,8},{10,11... | collective-permute-start | bytes 10616840 | tf_op jit(solution)/shard_map/ppermute | solution.py:105
  189.5 23.6 %collective-permute-start.27 = (bf16[384,1024]{1,0:T(8,128)(2,1)S(1)}, bf16[384,1024]{1,0:T(8,128)(2,1)S(1)}, u32[]{:S(2)}, u32[]{:S(2)}) collective-permute-start(bf16[384,1024]{1,0:T(8,128)(2,1)S(1)} %copy-done.11), channel_id=1, source_target_pairs={{0,8},{8,0},{16,24},{24,16},{1,9},{9,1},{17,25},{25,17},{2,10},{10... | collective-permute-start | bytes 2359304 | tf_op jit(solution)/shard_map/ppermute | solution.py:105
  190.7 22.4 %collective-permute-start.28 = (bf16[384,1024]{1,0:T(8,128)(2,1)S(1)}, bf16[384,1024]{1,0:T(8,128)(2,1)S(1)}, u32[]{:S(2)}, u32[]{:S(2)}) collective-permute-start(bf16[384,1024]{1,0:T(8,128)(2,1)S(1)} %copy-done.11), channel_id=1, source_target_pairs={{0,16},{8,24},{16,0},{24,8},{1,17},{9,25},{17,1},{25,9},{2,18},{10... | collective-permute-start | bytes 2359304 | tf_op jit(solution)/shard_map/ppermute | solution.py:105
  213.3 26.1 %collective-permute-start.33 = (bf16[1024,1024]{1,0:T(8,128)(2,1)S(1)}, bf16[1024,1024]{1,0:T(8,128)(2,1)}, u32[]{:S(2)}, u32[]{:S(2)}) collective-permute-start(bf16[1024,1024]{1,0:T(8,128)(2,1)S(1)} %shard_map.311.refs_0_), channel_id=1, source_target_pairs={{0,1},{1,0},{2,3},{3,2},{4,5},{5,4},{6,7},{7,6},{8,9},{9,8},{10,11... | collective-permute-start | bytes 6291464 | tf_op jit(solution)/shard_map/ppermute | solution.py:105
  306.7 104.0 %collective-permute-start.38 = (bf16[1536,1024]{1,0:T(8,128)(2,1)}, bf16[1536,1024]{1,0:T(8,128)(2,1)}, u32[]{:S(2)}, u32[]{:S(2)}) collective-permute-start(bf16[1536,1024]{1,0:T(8,128)(2,1)} %shard_map.318), channel_id=1, source_target_pairs={{0,1},{1,0},{2,3},{3,2},{4,5},{5,4},{6,7},{7,6},{8,9},{9,8},{10,11... | collective-permute-start | bytes 9437192 | tf_op jit(solution)/shard_map/ppermute | solution.py:105
  385.5 22.7 %collective-permute-start.57 = (bf16[128,1024]{1,0:T(8,128)(2,1)S(1)}, bf16[128,1024]{1,0:T(8,128)(2,1)S(1)}, u32[]{:S(2)}, u32[]{:S(2)}) collective-permute-start(bf16[128,1024]{1,0:T(8,128)(2,1)S(1)} %constant_dynamic-slice_fusion.23), channel_id=1, source_target_pairs={{0,6},{2,4},{4,2},{6,0},{1,7},{3,5},{5,3},{7,1},{8,14},{10,12},{12... | collective-permute-start | bytes 786440 | tf_op jit(solution)/shard_map/ppermute | solution.py:105
  417.8 25.1 %collective-permute-start.47 = (bf16[512,1024]{1,0:T(8,128)(2,1)}, bf16[512,1024]{1,0:T(8,128)(2,1)S(1)}, u32[]{:S(2)}, u32[]{:S(2)}) collective-permute-start(bf16[512,1024]{1,0:T(8,128)(2,1)} %pad_maximum_fusion.7), channel_id=1, source_target_pairs={{0,16},{8,24},{16,0},{24,8},{1,17},{9,25},{17,1},{25,9},{2,18},{10... | collective-permute-start | bytes 3145736 | tf_op jit(solution)/shard_map/ppermute | solution.py:105
  420.1 24.8 %collective-permute-start.45 = (bf16[512,1024]{1,0:T(8,128)(2,1)}, bf16[512,1024]{1,0:T(8,128)(2,1)}, u32[]{:S(2)}, u32[]{:S(2)}) collective-permute-start(bf16[512,1024]{1,0:T(8,128)(2,1)} %pad_maximum_fusion.6), channel_id=1, source_target_pairs={{0,8},{8,0},{16,24},{24,16},{1,9},{9,1},{17,25},{25,17},{2,10},{10... | collective-permute-start | bytes 3145736 | tf_op jit(solution)/shard_map/ppermute | solution.py:105
  421.9 79.4 %all-to-all-start.1 = ((bf16[4,800,512]{2,1,0:T(8,128)(2,1)}), bf16[4,800,512]{2,1,0:T(8,128)(2,1)}, u32[]{:S(2)}, u32[]{:S(2)}) async-start(bf16[4,800,512]{2,1,0:T(8,128)(2,1)} %bitcast.134), calls=%async_computation.1 | async-start | bytes 6553600 | tf_op jit(solution)/shard_map/all_to_all | solution.py:1045
  466.6 58.1 %collective-permute-start.67 = (bf16[288,2048]{1,0:T(8,128)(2,1)}, bf16[288,2048]{1,0:T(8,128)(2,1)S(1)}, u32[]{:S(2)}, u32[]{:S(2)}) collective-permute-start(bf16[288,2048]{1,0:T(8,128)(2,1)} %get-tuple-element.108), channel_id=1, source_target_pairs={{0,1},{1,0},{2,3},{3,2},{4,5},{5,4},{6,7},{7,6},{8,9},{9,8},{10,11... | collective-permute-start | bytes 3538952 | tf_op jit(solution)/shard_map/ppermute | solution.py:105
  468.7 22.5 %collective-permute-start.48 = (bf16[256,1024]{1,0:T(8,128)(2,1)S(1)}, bf16[256,1024]{1,0:T(8,128)(2,1)S(1)}, u32[]{:S(2)}, u32[]{:S(2)}) collective-permute-start(bf16[256,1024]{1,0:T(8,128)(2,1)S(1)} %add_convert_fusion.15), channel_id=1, source_target_pairs={{0,8},{8,0},{16,24},{24,16},{1,9},{9,1},{17,25},{25,17},{2,10},{10... | collective-permute-start | bytes 1572872 | tf_op jit(solution)/shard_map/ppermute | solution.py:105
  498.6 22.4 %collective-permute-start.61 = (bf16[128,1024]{1,0:T(8,128)(2,1)}, bf16[128,1024]{1,0:T(8,128)(2,1)}, u32[]{:S(2)}, u32[]{:S(2)}) collective-permute-start(bf16[128,1024]{1,0:T(8,128)(2,1)} %get-tuple-element.254), channel_id=1, source_target_pairs={{0,6},{2,4},{4,2},{6,0},{1,7},{3,5},{5,3},{7,1},{8,14},{10,12},{12... | collective-permute-start | bytes 786440 | tf_op jit(solution)/shard_map/ppermute | solution.py:105
  498.9 35.6 %collective-permute-start.63 = (bf16[512,1024]{1,0:T(8,128)(2,1)}, bf16[512,1024]{1,0:T(8,128)(2,1)}, u32[]{:S(2)}, u32[]{:S(2)}) collective-permute-start(bf16[512,1024]{1,0:T(8,128)(2,1)} %get-tuple-element.104), channel_id=1, source_target_pairs={{0,1},{1,0},{2,3},{3,2},{4,5},{5,4},{6,7},{7,6},{8,9},{9,8},{10,11... | collective-permute-start | bytes 3145736 | tf_op jit(solution)/shard_map/ppermute | solution.py:105
  501.3 74.5 %all-to-all-start.2 = ((bf16[4,912,512]{2,1,0:T(8,128)(2,1)}), bf16[4,912,512]{2,1,0:T(8,128)(2,1)}, u32[]{:S(2)}, u32[]{:S(2)}) async-start(bf16[4,912,512]{2,1,0:T(8,128)(2,1)} %bitcast.133), calls=%async_computation.2 | async-start | bytes 7471104 | tf_op jit(solution)/shard_map/all_to_all | solution.py:1045
  530.5 42.0 %collective-permute-start.69 = (bf16[1088,512]{1,0:T(8,128)(2,1)}, bf16[1088,512]{1,0:T(8,128)(2,1)S(1)}, u32[]{:S(2)}, u32[]{:S(2)}) collective-permute-start(bf16[1088,512]{1,0:T(8,128)(2,1)} %pad_maximum_fusion.4), channel_id=1, source_target_pairs={{0,16},{8,24},{16,0},{24,8},{1,17},{9,25},{17,1},{25,9},{2,18},{10... | collective-permute-start | bytes 3342344 | tf_op jit(solution)/shard_map/ppermute | solution.py:105
  532.3 40.2 %collective-permute-start.68 = (bf16[1088,512]{1,0:T(8,128)(2,1)}, bf16[1088,512]{1,0:T(8,128)(2,1)S(1)}, u32[]{:S(2)}, u32[]{:S(2)}) collective-permute-start(bf16[1088,512]{1,0:T(8,128)(2,1)} %pad_maximum_fusion.3), channel_id=1, source_target_pairs={{0,8},{8,0},{16,24},{24,16},{1,9},{9,1},{17,25},{25,17},{2,10},{10... | collective-permute-start | bytes 3342344 | tf_op jit(solution)/shard_map/ppermute | solution.py:105
  575.8 63.1 %all-to-all-start.3 = ((bf16[4,704,512]{2,1,0:T(8,128)(2,1)}), bf16[4,704,512]{2,1,0:T(8,128)(2,1)S(1)}, u32[]{:S(2)}, u32[]{:S(2)}) async-start(bf16[4,704,512]{2,1,0:T(8,128)(2,1)} %bitcast.74), calls=%async_computation.3 | async-start | bytes 5767168 | tf_op jit(solution)/shard_map/all_to_all | solution.py:1045
  585.9 47.4 %collective-permute-start.71 = (bf16[544,512]{1,0:T(8,128)(2,1)}, bf16[544,512]{1,0:T(8,128)(2,1)}, u32[]{:S(2)}, u32[]{:S(2)}) collective-permute-start(bf16[544,512]{1,0:T(8,128)(2,1)} %get-tuple-element.112), channel_id=1, source_target_pairs={{0,16},{8,24},{16,0},{24,8},{1,17},{9,25},{17,1},{25,9},{2,18},{10... | collective-permute-start | bytes 1671176 | tf_op jit(solution)/shard_map/ppermute | solution.py:105
  587.3 46.0 %collective-permute-start.72 = (bf16[544,512]{1,0:T(8,128)(2,1)}, bf16[544,512]{1,0:T(8,128)(2,1)}, u32[]{:S(2)}, u32[]{:S(2)}) collective-permute-start(bf16[544,512]{1,0:T(8,128)(2,1)} %get-tuple-element.113), channel_id=1, source_target_pairs={{0,8},{8,0},{16,24},{24,16},{1,9},{9,1},{17,25},{25,17},{2,10},{10... | collective-permute-start | bytes 1671176 | tf_op jit(solution)/shard_map/ppermute | solution.py:105
  593.0 24.7 %collective-permute-start.79 = (bf16[4,288,128]{2,1,0:T(8,128)(2,1)}, bf16[4,288,128]{2,1,0:T(8,128)(2,1)}, u32[]{:S(2)}, u32[]{:S(2)}) collective-permute-start(bf16[4,288,128]{2,1,0:T(8,128)(2,1)} %get-tuple-element.239), channel_id=1, source_target_pairs={{0,6},{2,4},{4,2},{6,0},{1,7},{3,5},{5,3},{7,1},{8,14},{10,12},{12... | collective-permute-start | bytes 884744 | tf_op jit(solution)/shard_map/ppermute | solution.py:105
  601.1 27.1 %collective-permute-start.70 = (f32[128,1024]{1,0:T(8,128)}, f32[128,1024]{1,0:T(8,128)}, u32[]{:S(2)}, u32[]{:S(2)}) collective-permute-start(f32[128,1024]{1,0:T(8,128)} %shard_map.336), channel_id=1, source_target_pairs={{0,1},{1,0},{2,3},{3,2},{4,5},{5,4},{6,7},{7,6},{8,9},{9,8},{10,11... | collective-permute-start | bytes 1572872 | tf_op jit(solution)/shard_map/ppermute | solution.py:105
  (162 other events, 1413.5 us)

commit v3 on v2

--- a/solution.py
+++ b/solution.py
@@ -293,22 +293,29 @@
     return [made[c * rows : (c + 1) * rows] for c in range(columns // block)]
 
 
-def reduce_first(pieces):
+def reduce_first(pieces, others=None):
     cut = pieces[0].shape[0] // 2
     low, high = [p[:cut] for p in pieces], [p[cut:] for p in pieces]
-    low_got = swap(jnp.concatenate([low[1], low[3]], axis=0), "dp", 1)
-    high_got = swap(jnp.concatenate([high[2], high[3]], axis=0), "dp", 2)
-    return low, high, low_got, high_got
-
-
-def reduce_second(state, between=None):
+    low_sent = jnp.concatenate([low[1], low[3]], axis=0)
+    high_sent = jnp.concatenate([high[2], high[3]], axis=0)
+    if others is not None:
+        low_sent, high_sent = order([low_sent, high_sent], others)
+    return low, high, swap(low_sent, "dp", 1), swap(high_sent, "dp", 2)
+
+
+def reduce_step(state, between=None):
     low, high, low_got, high_got = state
     cut = low[0].shape[0]
     low_sum = (low[2].astype(f32) + low_got[cut:].astype(f32)).astype(bf16)
     high_sum = (high[1].astype(f32) + high_got[cut:].astype(f32)).astype(bf16)
     if between is not None:
         low_sum, high_sum = order([low_sum, high_sum], between)
-    low_next, high_next = swap(low_sum, "dp", 2), swap(high_sum, "dp", 1)
+    return swap(low_sum, "dp", 2), swap(high_sum, "dp", 1)
+
+
+def reduce_end(state, low_next, high_next):
+    low, high, low_got, high_got = state
+    cut = low[0].shape[0]
     return jnp.concatenate(
         [
             total([low[0], low_got[:cut], low_next]).astype(bf16),
@@ -316,6 +323,10 @@
         ],
         axis=0,
     )
+
+
+def reduce_second(state, between=None):
+    return reduce_end(state, *reduce_step(state, between))
 
 
 def gather_z(own_half):
@@ -1006,28 +1017,20 @@
         core, back_late, rows_own, rows_other,
         [routed_at, (0, sent_width), (hidden_width, sent_router)], n_dp,
     )
-    own_state = reduce_first(order(cut_of(grad_mine, theirs, many, tree_rows), others_first))
+    own_state = reduce_first(cut_of(grad_mine, theirs, many, tree_rows), others_first)
     gn2_others = reduce_second(others_state, [down_sent])
     gn2_own = order([reduce_second(own_state)], [gate_sent])[0]
 
     out_there.append(swap(order([out_parts[1][1]], [theirs[1]])[0], "tensor", 1))
     out_state = reduce_first(
-        order(
-            cut_of(
-                [p[0] for p in out_parts],
-                out_there,
-                0,
-                tree_rows,
-            ),
-            [gn2_own],
-        )
+        cut_of([p[0] for p in out_parts], out_there, 0, tree_rows), [gn2_own]
     )
     out_first = list(out_state[2:])
     z_sent = gn2_others
     z_got = exchange_rel(
         [gn2_own] + [z_sent[s * tok : (s + 1) * tok] for s in range(n_ex - 1)], "expert"
     )
-    back_last = order([back_late], [gn2_others])[0]
+    back_last = order([back_late], [z_got[1]])[0]
     up_sent = weight_call(core, back_last, rows_own, rows_other, [up_at], n_dp)
     gn2_half = order([total(z_got)], [up_sent])[0]
     gn2 = permute_blocks(halves(gn2_half, swap(gn2_half, "tensor", 1), core, 1), i, n_dp)
@@ -1038,7 +1041,11 @@
     )
     res_half = pick_half(grad_residual.astype(bf16), core, 1)
 
-    out_mine = reduce_second(out_state)
+    out_last = list(reduce_step(out_state))
+    out_mine = reduce_end(out_state, *out_last)
+    out_got = exchange_rel(
+        [out_mine[many:]] + [out_mine[s * tok : (s + 1) * tok] for s in range(n_ex - 1)], "expert"
+    )
 
     def to_owners(sent, others):
         sent = order([sent], others)[0]
@@ -1053,10 +1060,10 @@
         [lax.dynamic_index_in_dim(router_block, i ^ s, 0, False) for s in range(n_dp)], axis=1
     )
 
-    res_others = gather_z(res_half)
+    res_others = order([gather_z(res_half)], out_first)[0]
     res_others = halves(res_others, swap(res_others, "tensor", 1), core, 1)
     res_tree = jnp.concatenate([grad_residual.astype(bf16), res_others], axis=0)
-    res_tree = order([res_tree], out_first)[0]
+    res_tree = order([res_tree], out_last)[0]
     if by_kernel:
         (
             back_mine, back_other, grad_wo, wq_grad, wl_grad, wl_sent, by_r, grad_norm_gain,
@@ -1173,16 +1180,15 @@
         ],
         axis=1,
     )
-    by_d[0] = order([by_d[0]], [down_got])[0]
     tail_state = reduce_first(stack_rows(by_d + [by_r], block))
-    grad_normed = tree_scatter(back_mine, back_other, n_ex, 1, list(tail_state[2:]))
+    back_other = order([back_other], out_got[1:] + [down_got])[0]
+    grad_normed = tree_scatter(back_mine, back_other, n_ex, 1, list(tail_state[2:]) + [gate_got])
     grad_in = permute_blocks(
         grad_residual + rms_back(grad_normed * gain_one, unit_one, inverse_one), i, n_dp
     )
 
-    mine = reduce_second(tail_state, [gate_got])
-    out_mine = order([out_mine], [back_mine])[0]
-    ffn_half = along_z(out_mine[:many], out_mine[many:])
+    mine = reduce_second(tail_state)
+    ffn_half = total(out_got)
     out_half = (pick_half(permute_blocks(residual, i, n_dp), core, 1) + ffn_half).astype(bf16)
     layer_out = halves(out_half, swap(out_half, "tensor", 1), core, 1)
 
@@ -1231,13 +1237,12 @@
             for p in got
         ]
     ).T
-    rest = total([p[ends[1] : d_rows] for p in got])
+    rest = order([total([p[ends[1] : d_rows] for p in got])], [up_got])[0]
     rest_there = swap(rest, "tensor", 1)
     grad_latent_proj = rows_join(rest[:wl_rows], rest_there[:wl_rows], core).T
     small = rest[wl_rows:] + rest_there[wl_rows:]
 
-    down_got, gate_got = order([down_got, gate_got], list(tail_state[2:]))
-    up_got = order([up_got], [mine])[0]
+    down_got, gate_got = order([down_got, gate_got], [grad_normed])
     shared_all = jnp.concatenate(
         [gate_got[:, width : width + 2 * sent_width], down_got[:, width:]], axis=1
     )

time: 688 us -> 659 us (0.958)
  waiting for transfers between devices: 224 us -> 211 us
  local copies, waits for them, and re-layouts: 93 us -> 84 us
    ppermute x80, waiting for transfers between devices: 224 us -> 211 us  [swap(): lax.ppermute(values, axis, [(k, k ^ step) for k in range(lax.axis_size(ax...]
    convert_element_type x11 -> x12, other arithmetic: 11 us -> 15.4 us  [the longest x4 6.66 us: reduce_end(): total([low[0], low_got[:cut], low_next]).astype(bf16)]
    unnamed x259 -> x261, local copies, waits for them, and re-layouts: 56.6 us -> 59.6 us
  transfers between devices with their start and end apart: 84 -> 84, of which waited for: 36 -> 28; matrix products, arithmetic and copies ran while one was open for 21% -> 20% of each run, Pallas kernels for 17% -> 17%
where the time goes in v3:
time: 659 us; the launch traced here: 654 us
  waiting for transfers between devices  211 us (32%)
  Pallas kernels  164 us (25%)
  starting transfers between devices  100 us (15%)
  other arithmetic  91.1 us (14%)
  local copies, waits for them, and re-layouts  84 us (13%)
    ppermute x80, waiting for transfers between devices, swap(): lax.ppermute(values, axis, [(k, k ^ step) for k in range(lax.axis_size(ax...  211 us
    ppermute x80, starting transfers between devices, swap(): lax.ppermute(values, axis, [(k, k ^ step) for k in range(lax.axis_size(ax...  83.1 us
    pallas_call x2, Pallas kernels, feed_call(): pl.pallas_call(functools.partial(feed_kernel, sh_width, width, padded, su...  69.3 us
    unnamed x261, local copies, waits for them, and re-layouts  59.6 us
    pallas_call x3, Pallas kernels, weight_call(): pl.pallas_call(body, grid_spec=pltpu.PrefetchScalarGridSpec(num_scalar_pr...  42.3 us
    pallas_call x2, Pallas kernels, whole_call(): pl.pallas_call(kernel, in_specs=[pl.BlockSpec(memory_space=pltpu.SMEM)] +...  36.8 us
    convert_element_type x6, other arithmetic, joined(): (mine[low:high].astype(f32) + there[low:high].astype(f32)).astype(bf16)  15.2 us
    pallas_call x11, Pallas kernels, place_rows(): pl.pallas_call(body, in_specs=[anywhere] * (len(parts) + len(others)), ou...  13.7 us
  transfers between devices with their start and end apart: 84, of which 28 were waited for; matrix products, arithmetic and copies ran while one was open for 20% of the time, Pallas kernels for 17%

profile of v3, /device:TPU:9, one launch (start us, length us, event | category | flops | bytes accessed | tf_op | source)
XLA Modules:
  0.0 653.6 jit_solution(10154891501477245906)
XLA Ops:
  44.2 11.4 %collective-permute-done.2.refs_4_.refs_3_.refs_2_ = bf16[128,2176]{1,0:T(8,128)(2,1)} collective-permute-done((bf16[128,2176]{1,0:T(8,128)(2,1)}, bf16[128,2176]{1,0:T(8,128)(2,1)}, u32[]{:S(2)}, u32[]{:S(2)}) %collective-permute-start.2) | collective-permute-done | bytes 557088 | tf_op jit(solution)/shard_map/ppermute | solution.py:105
  60.5 7.3 %collective-permute-done.8.refs_3_.refs_11_.refs_1_ = bf16[528,512]{1,0:T(8,128)(2,1)S(1)} collective-permute-done((bf16[528,512]{1,0:T(8,128)(2,1)}, bf16[528,512]{1,0:T(8,128)(2,1)S(1)}, u32[]{:S(2)}, u32[]{:S(2)}) %collective-permute-start.8) | collective-permute-done | bytes 540704 | tf_op jit(solution)/shard_map/ppermute | solution.py:105
  76.2 3.7 all-to-all-start
  90.4 15.1 %shard_map.300 = (bf16[512,1024]{1,0:T(8,128)(2,1)}, bf16[512,1024]{1,0:T(8,128)(2,1)}, bf16[512,2048]{1,0:T(8,128)(2,1)}, bf16[512,640]{1,0:T(8,128)(2,1)}, bf1...) custom-call(s32[2]{0:T(128)} %pad_add_fusion.at, ...), custom_call_target="tpu_custom_call" | custom-call | tf_op jit(solution)/shard_map/pallas_call | solution.py:637
  107.3 12.0 %collective-permute-done.15.refs_1_.refs_0_ = bf16[512,1152]{1,0:T(8,128)(2,1)S(1)} collective-permute-done((bf16[512,1152]{1,0:T(8,128)(2,1)}, bf16[512,1152]{1,0:T(8,128)(2,1)S(1)}, u32[]{:S(2)}, u32[]{:S(2)}) %collective-permute-start.15) | collective-permute-done | bytes 1179680 | tf_op jit(solution)/shard_map/ppermute | solution.py:105
  136.4 3.5 shard_map.316.g_own.refs_2_
  140.0 10.7 %collective-permute-done.14 = bf16[128,1024]{1,0:T(8,128)(2,1)} collective-permute-done((bf16[128,1024]{1,0:T(8,128)(2,1)}, bf16[128,1024]{1,0:T(8,128)(2,1)}, u32[]{:S(2)}, u32[]{:S(2)}) %collective-permute-start.14) | collective-permute-done | bytes 262176 | tf_op jit(solution)/shard_map/ppermute | solution.py:105
  162.7 6.5 collective-permute-done.18.refs_0_
  172.7 11.2 %collective-permute-done.20.refs_2_ = bf16[128,1024]{1,0:T(8,128)(2,1)S(1)} collective-permute-done((bf16[128,1024]{1,0:T(8,128)(2,1)S(1)}, bf16[128,1024]{1,0:T(8,128)(2,1)S(1)}, u32[]{:S(2)}, u32[]{:S(2)}) %collective-permute-start.20) | collective-permute-done | bytes 262176 | tf_op jit(solution)/shard_map/ppermute | solution.py:105
  191.6 21.0 %shard_map.310 = (bf16[2048,896]{1,0:T(8,128)(2,1)}, bf16[2048,1792]{1,0:T(8,128)(2,1)}, bf16[512,1024]{1,0:T(8,128)(2,1)}, bf16[512,1024]{1,0:T(8,128)(2,1)}, b...) custom-call(s32[3]{0:T(128)} %pad_add_fusion.2.at, bf16[512,1024]{1,0:T(8,128)(2,1)} %copy-done.4, ...), custom_call_target="tpu_custom_call" | custom-call | flops 11274289152 | bytes 22151168 | tf_op jit(solution)/shard_map/pallas_call | solution.py:430
  217.9 12.0 %collective-permute-done.31.refs_2_ = bf16[64,1024]{1,0:T(8,128)(2,1)S(1)} collective-permute-done((bf16[64,1024]{1,0:T(8,128)(2,1)S(1)}, bf16[64,1024]{1,0:T(8,128)(2,1)S(1)}, u32[]{:S(2)}, u32[]{:S(2)}) %collective-permute-start.31) | collective-permute-done | bytes 131104 | tf_op jit(solution)/shard_map/ppermute | solution.py:105
  230.1 4.0 collective-permute-done.32.refs_3_
  243.8 48.3 %shard_map.317 = (bf16[2048,896]{1,0:T(8,128)(2,1)}, bf16[2048,1792]{1,0:T(8,128)(2,1)}, bf16[1536,1024]{1,0:T(8,128)(2,1)}, bf16[1536,1024]{1,0:T(8,128)(2,1)},...) custom-call(s32[3]{0:T(128)} %pad_add_fusion.2.at, ...), custom_call_target="tpu_custom_call", output_to_operand_aliasing={{0}: (9, {}), {1}: (10, {})} | custom-call | flops 33822867456 | bytes 44433408 | tf_op jit(solution)/shard_map/pallas_call | solution.py:430
  298.0 3.8 add_convert_fusion.7
  312.6 13.0 %shard_map.325.refs_2_.refs_0_ = bf16[3200,512]{1,0:T(8,128)(2,1)} custom-call(s32[1]{0:T(128)} %bitcast.at, bf16[2048,896]{1,0:T(8,128)(2,1)} %shard_map.324.refs_0_, bf16[512,1152]{1,0:T(8,128)(2,1)} %shard_map.303.g_own.refs_1_, bf16[1536,1152]{1,0:T(8,128)(2,1)} %shard_map.316.g_own.refs_2_, bf16[512,1152]{1,0:T(8,128)(2,1)} %copy-done.18, ...), custom_call_target="tpu_custom_call" | custom-call | tf_op jit(solution)/shard_map/pallas_call | solution.py:685
  332.3 15.7 %shard_map.321.refs_1_.refs_0_ = bf16[3648,512]{1,0:T(8,128)(2,1)} custom-call(s32[1]{0:T(128)} %bitcast.at, bf16[2048,1792]{1,0:T(8,128)(2,1)} %shard_map.320.refs_0_, bf16[512,1024]{1,0:T(8,128)(2,1)} %copy-done.4, bf16[1536,1024]{1,0:T(8,128)(2,1)} %shard_map.314.n_own.refs_2_, bf16[512,1024]{1,0:T(8,128)(2,1)} %copy-done.5, ...), custom_call_target="tpu_custom_call" | custom-call | tf_op jit(solution)/shard_map/pallas_call | solution.py:685
  358.3 13.6 %shard_map.328.refs_1_.refs_0_ = bf16[2816,512]{1,0:T(8,128)(2,1)} custom-call(s32[1]{0:T(128)} %bitcast.at, bf16[2048,1792]{1,0:T(8,128)(2,1)} %shard_map.327.refs_0_, bf16[512,1024]{1,0:T(8,128)(2,1)} %copy-done.4, bf16[1536,1024]{1,0:T(8,128)(2,1)} %shard_map.314.n_own.refs_2_, bf16[512,1024]{1,0:T(8,128)(2,1)} %copy-done.5, ...), custom_call_target="tpu_custom_call" | custom-call | tf_op jit(solution)/shard_map/pallas_call | solution.py:685
  383.0 3.7 all-to-all-start.1
  406.3 39.8 %collective-permute-done.45.refs_2_ = bf16[512,1024]{1,0:T(8,128)(2,1)S(1)} collective-permute-done((bf16[512,1024]{1,0:T(8,128)(2,1)}, bf16[512,1024]{1,0:T(8,128)(2,1)S(1)}, u32[]{:S(2)}, u32[]{:S(2)}) %collective-permute-start.45) | collective-permute-done | bytes 1048608 | tf_op jit(solution)/shard_map/ppermute | solution.py:105
  455.3 5.1 all-to-all-start.2
  469.5 21.6 %shard_map.332 = (bf16[512,1024]{1,0:T(8,128)(2,1)}, bf16[512,1024]{1,0:T(8,128)(2,1)}, bf16[256,2048]{1,0:T(8,128)(2,1)}, bf16[384,2048]{1,0:T(8,128)(2,1)}, bf...) custom-call(s32[2]{0:T(128)} %pad_add_fusion.at, ...), custom_call_target="tpu_custom_call" | custom-call | tf_op jit(solution)/shard_map/pallas_call | solution.py:637
  491.1 4.2 collective-permute-start.67
  503.5 4.7 all-to-all-start.3
  521.1 7.0 %collective-permute-done.64 = bf16[128,1024]{1,0:T(8,128)(2,1)S(1)} collective-permute-done((bf16[128,1024]{1,0:T(8,128)(2,1)S(1)}, bf16[128,1024]{1,0:T(8,128)(2,1)S(1)}, u32[]{:S(2)}, u32[]{:S(2)}) %collective-permute-start.64) | collective-permute-done | bytes 262176 | tf_op jit(solution)/shard_map/ppermute | solution.py:105
  531.3 11.3 %collective-permute-done.66 = bf16[128,1024]{1,0:T(8,128)(2,1)S(1)} collective-permute-done((bf16[128,1024]{1,0:T(8,128)(2,1)S(1)}, bf16[128,1024]{1,0:T(8,128)(2,1)S(1)}, u32[]{:S(2)}, u32[]{:S(2)}) %collective-permute-start.66) | collective-permute-done | bytes 262176 | tf_op jit(solution)/shard_map/ppermute | solution.py:105
  543.6 21.6 %collective-permute-done.69.refs_2_ = bf16[1088,512]{1,0:T(8,128)(2,1)S(1)} collective-permute-done((bf16[1088,512]{1,0:T(8,128)(2,1)S(1)}, bf16[1088,512]{1,0:T(8,128)(2,1)S(1)}, u32[]{:S(2)}, u32[]{:S(2)}) %collective-permute-start.69) | collective-permute-done | bytes 1114144 | tf_op jit(solution)/shard_map/ppermute | solution.py:105
  568.2 5.2 convert_bitcast_fusion
  578.4 5.3 convert_bitcast_fusion.1
  599.6 12.6 %collective-permute-done.79 = bf16[4,288,128]{2,1,0:T(8,128)(2,1)S(1)} collective-permute-done((bf16[4,288,128]{2,1,0:T(8,128)(2,1)S(1)}, bf16[4,288,128]{2,1,0:T(8,128)(2,1)S(1)}, u32[]{:S(2)}, u32[]{:S(2)}) %collective-permute-start.79) | collective-permute-done | bytes 294944 | tf_op jit(solution)/shard_map/ppermute | solution.py:105
  621.2 5.6 collective-permute-done.73
  627.2 4.5 collective-permute-done.74
  632.1 11.7 %collective-permute-done.75 = bf16[1088,128]{1,0:T(8,128)(2,1)S(1)} collective-permute-done((bf16[1088,128]{1,0:T(8,128)(2,1)S(1)}, bf16[1088,128]{1,0:T(8,128)(2,1)S(1)}, u32[]{:S(2)}, u32[]{:S(2)}) %collective-permute-start.75) | collective-permute-done | bytes 278560 | tf_op jit(solution)/shard_map/ppermute | solution.py:105
  (638 shorter events, 274.2 us)
Async XLA Ops:
  5.0 39.2 %collective-permute-start = (bf16[128,2176]{1,0:T(8,128)(2,1)}, bf16[128,2176]{1,0:T(8,128)(2,1)}, u32[]{:S(2)}, u32[]{:S(2)}) collective-permute-start(bf16[128,2176]{1,0:T(8,128)(2,1)} %get-tuple-element.352.refs_3_), channel_id=1, source_target_pairs={{0,2},{2,0},{4,6},{6,4},{1,3},{3,1},{5,7},{7,5},{8,10},{10,8},{12,... | collective-permute-start | bytes 1671176 | tf_op jit(solution)/shard_map/ppermute | solution.py:105
  5.0 39.2 %collective-permute-start.1 = (bf16[128,2176]{1,0:T(8,128)(2,1)}, bf16[128,2176]{1,0:T(8,128)(2,1)}, u32[]{:S(2)}, u32[]{:S(2)}) collective-permute-start(bf16[128,2176]{1,0:T(8,128)(2,1)} %get-tuple-element.352.refs_3_), channel_id=1, source_target_pairs={{0,4},{2,6},{4,0},{6,2},{1,5},{3,7},{5,1},{7,3},{8,12},{10,14},{12... | collective-permute-start | bytes 1671176 | tf_op jit(solution)/shard_map/ppermute | solution.py:105
  7.5 48.1 %collective-permute-start.2 = (bf16[128,2176]{1,0:T(8,128)(2,1)}, bf16[128,2176]{1,0:T(8,128)(2,1)}, u32[]{:S(2)}, u32[]{:S(2)}) collective-permute-start(bf16[128,2176]{1,0:T(8,128)(2,1)} %get-tuple-element.352.refs_3_), channel_id=1, source_target_pairs={{0,6},{2,4},{4,2},{6,0},{1,7},{3,5},{5,3},{7,1},{8,14},{10,12},{12... | collective-permute-start | bytes 1671176 | tf_op jit(solution)/shard_map/ppermute | solution.py:105
  10.7 31.7 %collective-permute-start.6 = (bf16[1056,512]{1,0:T(8,128)(2,1)S(1)}, bf16[1056,512]{1,0:T(8,128)(2,1)S(1)}, u32[]{:S(2)}, u32[]{:S(2)}) collective-permute-start(bf16[1056,512]{1,0:T(8,128)(2,1)S(1)} %shard_map.297.refs_0_.refs_8_), channel_id=1, source_target_pairs={{0,8},{8,0},{16,24},{24,16},{1,9},{9,1},{17,25},{25,17},{2,10},{10... | collective-permute-start | bytes 3244040 | tf_op jit(solution)/shard_map/ppermute | solution.py:105
  12.0 31.3 %collective-permute-start.7 = (bf16[1056,512]{1,0:T(8,128)(2,1)S(1)}, bf16[1056,512]{1,0:T(8,128)(2,1)S(1)}, u32[]{:S(2)}, u32[]{:S(2)}) collective-permute-start(bf16[1056,512]{1,0:T(8,128)(2,1)S(1)} %shard_map.297.refs_0_.refs_8_), channel_id=1, source_target_pairs={{0,16},{8,24},{16,0},{24,8},{1,17},{9,25},{17,1},{25,9},{2,18},{10... | collective-permute-start | bytes 3244040 | tf_op jit(solution)/shard_map/ppermute | solution.py:105
  76.2 29.3 %all-to-all-start = ((bf16[4,264,512]{2,1,0:T(8,128)(2,1)}), bf16[4,264,512]{2,1,0:T(8,128)(2,1)S(1)}, u32[]{:S(2)}, u32[]{:S(2)}) async-start(bf16[4,264,512]{2,1,0:T(8,128)(2,1)} %bitcast.14), calls=%async_computation | async-start | bytes 2162688 | tf_op jit(solution)/shard_map/all_to_all | solution.py:814
  84.3 35.0 %collective-permute-start.15 = (bf16[512,1152]{1,0:T(8,128)(2,1)}, bf16[512,1152]{1,0:T(8,128)(2,1)S(1)}, u32[]{:S(2)}, u32[]{:S(2)}) collective-permute-start(bf16[512,1152]{1,0:T(8,128)(2,1)} %shard_map.303.g_own.refs_1_), channel_id=1, source_target_pairs={{0,8},{8,0},{16,24},{24,16},{1,9},{9,1},{17,25},{25,17},{2,10},{10... | collective-permute-start | bytes 3538952 | tf_op jit(solution)/shard_map/ppermute | solution.py:105
  86.0 35.4 %collective-permute-start.16 = (bf16[512,1152]{1,0:T(8,128)(2,1)}, bf16[512,1152]{1,0:T(8,128)(2,1)S(1)}, u32[]{:S(2)}, u32[]{:S(2)}) collective-permute-start(bf16[512,1152]{1,0:T(8,128)(2,1)} %shard_map.303.g_own.refs_1_), channel_id=1, source_target_pairs={{0,16},{8,24},{16,0},{24,8},{1,17},{9,25},{17,1},{25,9},{2,18},{10... | collective-permute-start | bytes 3538952 | tf_op jit(solution)/shard_map/ppermute | solution.py:105
  160.9 22.9 %collective-permute-start.20 = (bf16[128,1024]{1,0:T(8,128)(2,1)S(1)}, bf16[128,1024]{1,0:T(8,128)(2,1)S(1)}, u32[]{:S(2)}, u32[]{:S(2)}) collective-permute-start(bf16[128,1024]{1,0:T(8,128)(2,1)S(1)} %get-tuple-element.279.refs_1_), channel_id=1, source_target_pairs={{0,6},{2,4},{4,2},{6,0},{1,7},{3,5},{5,3},{7,1},{8,14},{10,12},{12... | collective-permute-start | bytes 786440 | tf_op jit(solution)/shard_map/ppermute | solution.py:105
  161.2 23.7 %collective-permute-start.23 = (bf16[128,1024]{1,0:T(8,128)(2,1)S(1)}, bf16[128,1024]{1,0:T(8,128)(2,1)S(1)}, u32[]{:S(2)}, u32[]{:S(2)}) collective-permute-start(bf16[128,1024]{1,0:T(8,128)(2,1)S(1)} %get-tuple-element.279.refs_1_), channel_id=1, source_target_pairs={{0,8},{8,0},{16,24},{24,16},{1,9},{9,1},{17,25},{25,17},{2,10},{10... | collective-permute-start | bytes 786440 | tf_op jit(solution)/shard_map/ppermute | solution.py:105
  169.2 73.3 %collective-permute-start.35 = (bf16[1536,1152]{1,0:T(8,128)(2,1)}, bf16[1536,1152]{1,0:T(8,128)(2,1)}, u32[]{:S(2)}, u32[]{:S(2)}) collective-permute-start(bf16[1536,1152]{1,0:T(8,128)(2,1)} %shard_map.316.g_own.refs_2_), channel_id=1, source_target_pairs={{0,1},{1,0},{2,3},{3,2},{4,5},{5,4},{6,7},{7,6},{8,9},{9,8},{10,11... | collective-permute-start | bytes 10616840 | tf_op jit(solution)/shard_map/ppermute | solution.py:105
  189.0 23.6 %collective-permute-start.27 = (bf16[384,1024]{1,0:T(8,128)(2,1)S(1)}, bf16[384,1024]{1,0:T(8,128)(2,1)S(1)}, u32[]{:S(2)}, u32[]{:S(2)}) collective-permute-start(bf16[384,1024]{1,0:T(8,128)(2,1)S(1)} %copy-done.11), channel_id=1, source_target_pairs={{0,8},{8,0},{16,24},{24,16},{1,9},{9,1},{17,25},{25,17},{2,10},{10... | collective-permute-start | bytes 2359304 | tf_op jit(solution)/shard_map/ppermute | solution.py:105
  212.9 26.1 %collective-permute-start.33 = (bf16[1024,1024]{1,0:T(8,128)(2,1)S(1)}, bf16[1024,1024]{1,0:T(8,128)(2,1)}, u32[]{:S(2)}, u32[]{:S(2)}) collective-permute-start(bf16[1024,1024]{1,0:T(8,128)(2,1)S(1)} %shard_map.311.refs_0_), channel_id=1, source_target_pairs={{0,1},{1,0},{2,3},{3,2},{4,5},{5,4},{6,7},{7,6},{8,9},{9,8},{10,11... | collective-permute-start | bytes 6291464 | tf_op jit(solution)/shard_map/ppermute | solution.py:105
  310.2 79.3 %collective-permute-start.38 = (bf16[1536,1024]{1,0:T(8,128)(2,1)}, bf16[1536,1024]{1,0:T(8,128)(2,1)}, u32[]{:S(2)}, u32[]{:S(2)}) collective-permute-start(bf16[1536,1024]{1,0:T(8,128)(2,1)} %shard_map.318), channel_id=1, source_target_pairs={{0,1},{1,0},{2,3},{3,2},{4,5},{5,4},{6,7},{7,6},{8,9},{9,8},{10,11... | collective-permute-start | bytes 9437192 | tf_op jit(solution)/shard_map/ppermute | solution.py:105
  325.6 22.5 %collective-permute-start.43 = (bf16[128,1024]{1,0:T(8,128)(2,1)}, bf16[128,1024]{1,0:T(8,128)(2,1)S(1)}, u32[]{:S(2)}, u32[]{:S(2)}) collective-permute-start(bf16[128,1024]{1,0:T(8,128)(2,1)} %get-tuple-element.77), channel_id=1, source_target_pairs={{0,16},{8,24},{16,0},{24,8},{1,17},{9,25},{17,1},{25,9},{2,18},{10... | collective-permute-start | bytes 786440 | tf_op jit(solution)/shard_map/ppermute | solution.py:105
  325.9 23.5 %collective-permute-start.41 = (bf16[128,1024]{1,0:T(8,128)(2,1)}, bf16[128,1024]{1,0:T(8,128)(2,1)S(1)}, u32[]{:S(2)}, u32[]{:S(2)}) collective-permute-start(bf16[128,1024]{1,0:T(8,128)(2,1)} %get-tuple-element.76), channel_id=1, source_target_pairs={{0,8},{8,0},{16,24},{24,16},{1,9},{9,1},{17,25},{25,17},{2,10},{10... | collective-permute-start | bytes 786440 | tf_op jit(solution)/shard_map/ppermute | solution.py:105
  383.0 70.6 %all-to-all-start.1 = ((bf16[4,800,512]{2,1,0:T(8,128)(2,1)}), bf16[4,800,512]{2,1,0:T(8,128)(2,1)S(1)}, u32[]{:S(2)}, u32[]{:S(2)}) async-start(bf16[4,800,512]{2,1,0:T(8,128)(2,1)} %bitcast.134), calls=%async_computation.1 | async-start | bytes 6553600 | tf_op jit(solution)/shard_map/all_to_all | solution.py:1052
  396.4 49.6 %collective-permute-start.45 = (bf16[512,1024]{1,0:T(8,128)(2,1)}, bf16[512,1024]{1,0:T(8,128)(2,1)S(1)}, u32[]{:S(2)}, u32[]{:S(2)}) collective-permute-start(bf16[512,1024]{1,0:T(8,128)(2,1)} %get-tuple-element.79), channel_id=1, source_target_pairs={{0,16},{8,24},{16,0},{24,8},{1,17},{9,25},{17,1},{25,9},{2,18},{10... | collective-permute-start | bytes 3145736 | tf_op jit(solution)/shard_map/ppermute | solution.py:105
  399.6 48.3 %collective-permute-start.47 = (bf16[512,1024]{1,0:T(8,128)(2,1)S(1)}, bf16[512,1024]{1,0:T(8,128)(2,1)S(1)}, u32[]{:S(2)}, u32[]{:S(2)}) collective-permute-start(bf16[512,1024]{1,0:T(8,128)(2,1)S(1)} %copy-done.58), channel_id=1, source_target_pairs={{0,8},{8,0},{16,24},{24,16},{1,9},{9,1},{17,25},{25,17},{2,10},{10... | collective-permute-start | bytes 3145736 | tf_op jit(solution)/shard_map/ppermute | solution.py:105
  403.6 45.8 %collective-permute-start.59 = (bf16[128,1024]{1,0:T(8,128)(2,1)S(1)}, bf16[128,1024]{1,0:T(8,128)(2,1)S(1)}, u32[]{:S(2)}, u32[]{:S(2)}) collective-permute-start(bf16[128,1024]{1,0:T(8,128)(2,1)S(1)} %constant_dynamic-slice_fusion.20), channel_id=1, source_target_pairs={{0,2},{2,0},{4,6},{6,4},{1,3},{3,1},{5,7},{7,5},{8,10},{10,8},{12,... | collective-permute-start | bytes 786440 | tf_op jit(solution)/shard_map/ppermute | solution.py:105
  403.7 45.7 %collective-permute-start.60 = (bf16[128,1024]{1,0:T(8,128)(2,1)S(1)}, bf16[128,1024]{1,0:T(8,128)(2,1)S(1)}, u32[]{:S(2)}, u32[]{:S(2)}) collective-permute-start(bf16[128,1024]{1,0:T(8,128)(2,1)S(1)} %constant_dynamic-slice_fusion.20), channel_id=1, source_target_pairs={{0,4},{2,6},{4,0},{6,2},{1,5},{3,7},{5,1},{7,3},{8,12},{10,14},{12... | collective-permute-start | bytes 786440 | tf_op jit(solution)/shard_map/ppermute | solution.py:105
  406.1 43.3 %collective-permute-start.61 = (bf16[128,1024]{1,0:T(8,128)(2,1)S(1)}, bf16[128,1024]{1,0:T(8,128)(2,1)S(1)}, u32[]{:S(2)}, u32[]{:S(2)}) collective-permute-start(bf16[128,1024]{1,0:T(8,128)(2,1)S(1)} %constant_dynamic-slice_fusion.20), channel_id=1, source_target_pairs={{0,6},{2,4},{4,2},{6,0},{1,7},{3,5},{5,3},{7,1},{8,14},{10,12},{12... | collective-permute-start | bytes 786440 | tf_op jit(solution)/shard_map/ppermute | solution.py:105
  455.3 48.1 %all-to-all-start.2 = ((bf16[4,912,512]{2,1,0:T(8,128)(2,1)}), bf16[4,912,512]{2,1,0:T(8,128)(2,1)}, u32[]{:S(2)}, u32[]{:S(2)}) async-start(bf16[4,912,512]{2,1,0:T(8,128)(2,1)} %bitcast.133), calls=%async_computation.2 | async-start | bytes 7471104 | tf_op jit(solution)/shard_map/all_to_all | solution.py:1052
  463.1 37.9 %collective-permute-start.49 = (bf16[128,1024]{1,0:T(8,128)(2,1)S(1)}, bf16[128,1024]{1,0:T(8,128)(2,1)S(1)}, u32[]{:S(2)}, u32[]{:S(2)}) collective-permute-start(bf16[128,1024]{1,0:T(8,128)(2,1)S(1)} %get-tuple-element.272), channel_id=1, source_target_pairs={{0,2},{2,0},{4,6},{6,4},{1,3},{3,1},{5,7},{7,5},{8,10},{10,8},{12,... | collective-permute-start | bytes 786440 | tf_op jit(solution)/shard_map/ppermute | solution.py:105
  463.2 37.8 %collective-permute-start.50 = (bf16[128,1024]{1,0:T(8,128)(2,1)S(1)}, bf16[128,1024]{1,0:T(8,128)(2,1)S(1)}, u32[]{:S(2)}, u32[]{:S(2)}) collective-permute-start(bf16[128,1024]{1,0:T(8,128)(2,1)S(1)} %get-tuple-element.273), channel_id=1, source_target_pairs={{0,4},{2,6},{4,0},{6,2},{1,5},{3,7},{5,1},{7,3},{8,12},{10,14},{12... | collective-permute-start | bytes 786440 | tf_op jit(solution)/shard_map/ppermute | solution.py:105
  465.6 35.4 %collective-permute-start.51 = (bf16[128,1024]{1,0:T(8,128)(2,1)S(1)}, bf16[128,1024]{1,0:T(8,128)(2,1)S(1)}, u32[]{:S(2)}, u32[]{:S(2)}) collective-permute-start(bf16[128,1024]{1,0:T(8,128)(2,1)S(1)} %slice.857), channel_id=1, source_target_pairs={{0,6},{2,4},{4,2},{6,0},{1,7},{3,5},{5,3},{7,1},{8,14},{10,12},{12... | collective-permute-start | bytes 786440 | tf_op jit(solution)/shard_map/ppermute | solution.py:105
  503.5 64.8 %all-to-all-start.3 = ((bf16[4,704,512]{2,1,0:T(8,128)(2,1)}), bf16[4,704,512]{2,1,0:T(8,128)(2,1)}, u32[]{:S(2)}, u32[]{:S(2)}) async-start(bf16[4,704,512]{2,1,0:T(8,128)(2,1)} %bitcast.135), calls=%async_computation.3 | async-start | bytes 5767168 | tf_op jit(solution)/shard_map/all_to_all | solution.py:1052
  513.4 51.8 %collective-permute-start.69 = (bf16[1088,512]{1,0:T(8,128)(2,1)S(1)}, bf16[1088,512]{1,0:T(8,128)(2,1)S(1)}, u32[]{:S(2)}, u32[]{:S(2)}) collective-permute-start(bf16[1088,512]{1,0:T(8,128)(2,1)S(1)} %pad_maximum_fusion.3), channel_id=1, source_target_pairs={{0,16},{8,24},{16,0},{24,8},{1,17},{9,25},{17,1},{25,9},{2,18},{10... | collective-permute-start | bytes 3342344 | tf_op jit(solution)/shard_map/ppermute | solution.py:105
  514.9 50.3 %collective-permute-start.68 = (bf16[1088,512]{1,0:T(8,128)(2,1)S(1)}, bf16[1088,512]{1,0:T(8,128)(2,1)S(1)}, u32[]{:S(2)}, u32[]{:S(2)}) collective-permute-start(bf16[1088,512]{1,0:T(8,128)(2,1)S(1)} %pad_maximum_fusion.2), channel_id=1, source_target_pairs={{0,8},{8,0},{16,24},{24,16},{1,9},{9,1},{17,25},{25,17},{2,10},{10... | collective-permute-start | bytes 3342344 | tf_op jit(solution)/shard_map/ppermute | solution.py:105
  528.1 45.4 %collective-permute-start.52 = (bf16[128,1024]{1,0:T(8,128)(2,1)S(1)}, bf16[128,1024]{1,0:T(8,128)(2,1)S(1)}, u32[]{:S(2)}, u32[]{:S(2)}) collective-permute-start(bf16[128,1024]{1,0:T(8,128)(2,1)S(1)} %fusion.11), channel_id=1, source_target_pairs={{0,1},{1,0},{2,3},{3,2},{4,5},{5,4},{6,7},{7,6},{8,9},{9,8},{10,11... | collective-permute-start | bytes 786440 | tf_op jit(solution)/shard_map/ppermute | solution.py:105
  586.4 25.7 %collective-permute-start.79 = (bf16[4,288,128]{2,1,0:T(8,128)(2,1)S(1)}, bf16[4,288,128]{2,1,0:T(8,128)(2,1)S(1)}, u32[]{:S(2)}, u32[]{:S(2)}) collective-permute-start(bf16[4,288,128]{2,1,0:T(8,128)(2,1)S(1)} %get-tuple-element.227), channel_id=1, source_target_pairs={{0,6},{2,4},{4,2},{6,0},{1,7},{3,5},{5,3},{7,1},{8,14},{10,12},{12... | collective-permute-start | bytes 884744 | tf_op jit(solution)/shard_map/ppermute | solution.py:105
  620.7 23.1 %collective-permute-start.75 = (bf16[1088,128]{1,0:T(8,128)(2,1)S(1)}, bf16[1088,128]{1,0:T(8,128)(2,1)S(1)}, u32[]{:S(2)}, u32[]{:S(2)}) collective-permute-start(bf16[1088,128]{1,0:T(8,128)(2,1)S(1)} %maximum_maximum_fusion.2), channel_id=1, source_target_pairs={{0,6},{2,4},{4,2},{6,0},{1,7},{3,5},{5,3},{7,1},{8,14},{10,12},{12... | collective-permute-start | bytes 835592 | tf_op jit(solution)/shard_map/ppermute | solution.py:105
  (164 other events, 1401.7 us)
